TPU v7x, 32 devices: a whole 2x2x4 slice. The times are simulated.
32 devices in a mesh: depth: 4 (over x, core), rows: 8 (over z, y).
Axes of the slice: x: 2, y: 2, z: 4, core: 2. Of those that a mesh axis runs over, the one named last changes fastest.
Arguments:
- source_top: bfloat16 [2, 2, 512, 512], P(None, None, 'rows'), may hold values from -8 to 8
- adjoint_bottom: bfloat16 [2, 2, 512, 512], P(None, None, 'rows'), may hold values from -8 to 8
- slowness: float32 [4, 512, 512], P('depth', 'rows'), may hold values from 0.7 to 1.3
- correction: float32 [4, 512, 512], P('depth', 'rows'), may hold values from -0.16 to 0.16
- slowness_ref: float32 [4], P('depth'), may hold values from 0.9 to 1.1
- omega: float32 [2], replicated, may hold values from 0.8 to 1.6
Outputs:
- gradient: float32 [4, 512, 512], P('depth', 'rows')
All inputs are finite; a program needn't handle non-finite values.
Results may differ from a plain program's by a relative error of at most 0.025.
Values may be sent and summed in bfloat16 or wider, within the bound.
No kernel may reach another device: no remote copies, remote signals or barrier semaphores. Data moves between devices by JAX's collectives and lax.ppermute only.
A program may use at most 64 MiB of HBM per device.

v0:
```python
from functools import partial
import math

import jax
import jax.numpy as jnp
from jax import lax
from jax.sharding import PartitionSpec as P

depth_step = 1.0
y_radix = 16


def extended_2(shard, sides, width):
    for axis, dim in sides:
        size, length = (lax.axis_size(axis), shard.shape[dim])
        up = [(i, (i + 1) % size) for i in range(size)]
        down = [(j, i) for i, j in up]
        last = lax.slice_in_dim(shard, length - width, length, axis=dim)
        initial = lax.slice_in_dim(shard, 0, width, axis=dim)
        before = lax.ppermute(last, axis, up)
        after = lax.ppermute(initial, axis, down)
        shard = jnp.concatenate([before, shard, after], axis=dim)
    return shard


def passed_along(shard, axis, by):
    length = lax.axis_size(axis)
    pairs = [(i, i + by) for i in range(length) if 0 <= i + by < length]
    return lax.ppermute(shard, axis, pairs)


def from_behind(block, axis, distance):
    devices = range(lax.axis_size(axis))
    route = [((i - distance) % len(devices), i) for i in devices]
    return lax.ppermute(block, axis, route)


def dft_table(length, direction):
    row_index = lax.broadcasted_iota(jnp.int32, (length, length), 0)
    col_index = lax.broadcasted_iota(jnp.int32, (length, length), 1)
    angles = (row_index * col_index % length).astype(jnp.float32) * (2.0 * math.pi / length)
    norm_scale = 1.0 / math.sqrt(length)
    return (jnp.cos(angles) * norm_scale, direction * jnp.sin(angles) * norm_scale)


def twiddle_table(first_len, second_len, length, direction):
    row_index = lax.broadcasted_iota(jnp.int32, (first_len, second_len), 0)
    col_index = lax.broadcasted_iota(jnp.int32, (first_len, second_len), 1)
    angles = (row_index * col_index % length).astype(jnp.float32) * (2.0 * math.pi / length)
    return (jnp.cos(angles), direction * jnp.sin(angles))


def contract(pattern, values, matrix):
    product = partial(
        jnp.einsum, pattern, precision=lax.Precision.HIGHEST, preferred_element_type=jnp.float32
    )
    return (
        product(values[0], matrix[0]) - product(values[1], matrix[1]),
        product(values[0], matrix[1]) + product(values[1], matrix[0]),
    )


def rotate(values, factor):
    return (
        values[0] * factor[0] - values[1] * factor[1],
        values[0] * factor[1] + values[1] * factor[0],
    )


def conjugate(values):
    return (values[0], -values[1])


def split_parts(stacked):
    return (stacked[:, 0].astype(jnp.float32), stacked[:, 1].astype(jnp.float32))


def joined_bf16(values):
    return jnp.stack(values, 1).astype(jnp.bfloat16)


def wavenumbers(positions, length):
    signed = jnp.where(positions >= length // 2, positions - length, positions)
    return signed.astype(jnp.float32) * (2.0 * math.pi / length)


def forward_rows(values):
    slot_count, rows_here, width_y = values[0].shape
    inner_len = width_y // y_radix
    shaped = tuple((member.reshape(slot_count, rows_here, y_radix, inner_len) for member in values))
    section_one = contract("kxab,ac->kxcb", shaped, dft_table(y_radix, -1.0))
    section_one = rotate(section_one, twiddle_table(y_radix, inner_len, width_y, -1.0))
    section_two = contract("kxcb,bd->kxcd", section_one, dft_table(inner_len, -1.0))
    return tuple((member.reshape(slot_count, rows_here, width_y) for member in section_two))


def inverse_rows(values):
    slot_count, rows_here, width_y = values[0].shape
    inner_len = width_y // y_radix
    shaped = tuple((member.reshape(slot_count, rows_here, y_radix, inner_len) for member in values))
    section_one = contract("kxcd,bd->kxcb", shaped, dft_table(inner_len, 1.0))
    section_one = rotate(section_one, twiddle_table(y_radix, inner_len, width_y, 1.0))
    section_two = contract("kxcb,ac->kxab", section_one, dft_table(y_radix, 1.0))
    return tuple((member.reshape(slot_count, rows_here, width_y) for member in section_two))


def forward_cols(values, row_parts):
    slot_count, rows_here, width_y = values[0].shape
    local_cols = width_y // row_parts
    width_x = rows_here * row_parts
    shaped = tuple(
        (member.reshape(slot_count, rows_here, row_parts, local_cols) for member in values)
    )
    section_one = contract("kbay,ac->kbcy", shaped, dft_table(row_parts, -1.0))
    factor = twiddle_table(rows_here, row_parts, width_x, -1.0)
    section_one = rotate(section_one, (factor[0][:, :, None], factor[1][:, :, None]))
    section_two = contract("kbcy,bd->kycd", section_one, dft_table(rows_here, -1.0))
    return tuple((member.reshape(slot_count, local_cols, width_x) for member in section_two))


def inverse_cols(values, row_parts):
    slot_count, local_cols, width_x = values[0].shape
    rows_here = width_x // row_parts
    shaped = tuple(
        (member.reshape(slot_count, local_cols, row_parts, rows_here) for member in values)
    )
    section_one = contract("kycd,bd->kbcy", shaped, dft_table(rows_here, 1.0))
    factor = twiddle_table(rows_here, row_parts, width_x, 1.0)
    section_one = rotate(section_one, (factor[0][:, :, None], factor[1][:, :, None]))
    section_two = contract("kbcy,ac->kbay", section_one, dft_table(row_parts, 1.0))
    return tuple(
        (member.reshape(slot_count, rows_here, row_parts * local_cols) for member in section_two)
    )


def rim_laplace(rimmed):
    widened_values = rimmed.astype(jnp.float32)
    center = widened_values[:, :, 1:-1]
    return (
        widened_values[:, :, 2:]
        + widened_values[:, :, :-2]
        + jnp.roll(center, 1, 3)
        + jnp.roll(center, -1, 3)
        - 4.0 * center
    )


def per_device(source_top, adjoint_bottom, slowness, correction, slowness_ref, omega):
    row_parts = lax.axis_size("rows")
    section_count = lax.axis_size("depth")
    section_id = lax.axis_index("depth")
    part_id = lax.axis_index("rows")
    freq_count = omega.shape[0]
    rows_here = slowness.shape[1]
    width_y = slowness.shape[2]
    width_x = rows_here * row_parts
    local_cols = width_y // row_parts
    slot_count = 1
    group_count = freq_count // slot_count
    tick_count = group_count + section_count
    slow_here = slowness[0]
    coef_here = correction[0]
    ref_here = slowness_ref[0]
    inner_y = width_y // y_radix
    spectral_y = part_id * local_cols + lax.iota(jnp.int32, local_cols)
    index_y = spectral_y // inner_y + y_radix * (spectral_y % inner_y)
    first_x = lax.broadcasted_iota(jnp.int32, (row_parts, rows_here), 0)
    second_x = lax.broadcasted_iota(jnp.int32, (row_parts, rows_here), 1)
    index_x = (first_x + row_parts * second_x).reshape(width_x)
    wave_y = wavenumbers(index_y, width_y)
    wave_x = wavenumbers(index_x, width_x)

    def phase_for(omega_slot):
        squared = (
            (omega_slot[:, None, None] * ref_here) ** 2
            - wave_x[None, None, :] ** 2
            - wave_y[None, :, None] ** 2
        )
        damping = jnp.exp(-jnp.sqrt(jnp.maximum(-squared, 0.0)) * depth_step)
        angles = jnp.sqrt(jnp.maximum(squared, 0.0)) * depth_step
        return (damping * jnp.cos(angles), damping * jnp.sin(angles))

    def lens_for(omega_slot, slow_rows):
        angles = omega_slot[:, None, None] * (slow_rows - ref_here) * depth_step
        return (jnp.cos(angles), jnp.sin(angles))

    def slot_of(source_array, group_id):
        start_row = jnp.clip(group_id, 0, group_count - 1) * slot_count
        return lax.dynamic_slice_in_dim(source_array, start_row, slot_count, 0)

    def store_slot(buffer, values, group_id):
        start_row = jnp.clip(group_id, 0, group_count - 1) * slot_count
        active = jnp.logical_and(group_id >= 0, group_id < group_count)
        old_slot = lax.dynamic_slice_in_dim(buffer, start_row, slot_count, 0)
        return lax.dynamic_update_slice_in_dim(
            buffer, jnp.where(active, values, old_slot), start_row, 0
        )

    def one_tick(tick_index, loop_state):
        fwd_in, adj_in, fwd_store, adj_store = loop_state
        group_f = tick_index - section_id
        group_a = tick_index - section_count + section_id
        omega_f = slot_of(omega, group_f)
        omega_a = slot_of(omega, group_a)
        adj_center = adj_in[:, :, 1:-1].astype(jnp.float32)
        adj_laplace = rim_laplace(adj_in)
        pulled = (
            adj_center[:, 0] + coef_here * adj_laplace[:, 1],
            adj_center[:, 1] - coef_here * adj_laplace[:, 0],
        )
        pulled = rotate(pulled, conjugate(lens_for(omega_a, slow_here)))
        spec_f = forward_rows(split_parts(fwd_in))
        spec_a = forward_rows(pulled)
        cross_f, cross_a = (
            lax.all_to_all(joined_bf16(spec_f), "rows", split_axis=3, concat_axis=3, tiled=True),
            lax.all_to_all(joined_bf16(spec_a), "rows", split_axis=3, concat_axis=3, tiled=True),
        )
        wave_f = rotate(forward_cols(split_parts(cross_f), row_parts), phase_for(omega_f))
        wave_a = rotate(
            forward_cols(split_parts(cross_a), row_parts), conjugate(phase_for(omega_a))
        )
        outgoing = (
            joined_bf16(inverse_cols(wave_f, row_parts)),
            joined_bf16(inverse_cols(wave_a, row_parts)),
        )
        back_f, back_a = (
            lax.all_to_all(outgoing[0], "rows", split_axis=3, concat_axis=3, tiled=True),
            lax.all_to_all(outgoing[1], "rows", split_axis=3, concat_axis=3, tiled=True),
        )
        field_f = inverse_rows(split_parts(back_f))
        field_a = joined_bf16(inverse_rows(split_parts(back_a)))
        lensed = rotate(field_f, lens_for(omega_f, slow_here))
        scaled = joined_bf16((coef_here * lensed[0], coef_here * lensed[1]))
        upward = jnp.where(section_id == 0, slot_of(adjoint_bottom, tick_index), field_a)
        scaled_rims, upward_rims = (
            extended_2(scaled, (("rows", 2),), 1),
            extended_2(upward, (("rows", 2),), 1),
        )
        fwd_laplace = rim_laplace(scaled_rims)
        fwd_out = joined_bf16((lensed[0] - fwd_laplace[:, 1], lensed[1] + fwd_laplace[:, 0]))
        passed = passed_along(fwd_out, "depth", 1)
        next_up = from_behind(upward_rims, "depth", -1)
        next_fwd = jnp.where(section_id == 0, slot_of(source_top, tick_index + 1), passed)
        fwd_store = store_slot(fwd_store, fwd_out, group_f)
        adj_store = store_slot(adj_store, adj_in[:, :, 1:-1], group_a)
        return (next_fwd, next_up, fwd_store, adj_store)

    initial = (
        slot_of(source_top, 0),
        jnp.zeros((slot_count, 2, rows_here + 2, width_y), jnp.bfloat16),
        jnp.zeros((freq_count, 2, rows_here, width_y), jnp.bfloat16),
        jnp.zeros((freq_count, 2, rows_here, width_y), jnp.bfloat16),
    )
    final_state = lax.fori_loop(0, tick_count, one_tick, initial)
    forward_part = split_parts(final_state[2])
    adjoint_part = split_parts(final_state[3])
    product = forward_part[0] * adjoint_part[1] - forward_part[1] * adjoint_part[0]
    gradient = jnp.sum(omega[:, None, None] * product, axis=0)
    return gradient[None]


def solution(mesh):
    in_specs = (
        P(None, None, "rows", None),
        P(None, None, "rows", None),
        P("depth", "rows", None),
        P("depth", "rows", None),
        P("depth"),
        P(),
    )
    out_specs = P("depth", "rows", None)
    return jax.shard_map(
        per_device, mesh=mesh, in_specs=in_specs, out_specs=out_specs, check_vma=False
    )
```

profile of v0, /device:TPU:0, one launch (start us, length us, event | category | flops | bytes accessed | tf_op | source)
XLA Modules:
  0.0 790.1 jit_solution(15758955502320841641)
XLA Ops:
  4.1 784.7 %while.24 = (s32[]{:T(128)}, bf16[1,2,64,512]{2,3,1,0:T(8,128)(2,1)}, bf16[1,2,66,512]{2,3,1,0:T(8,128)(2,1)S(1)}, bf16[2,2,64,512]{2,3,1,0:T(8,128)(2,1)S(1)}, ...) while((s32[]{:T(128)}, ...), condition=%wide.region_1.2_spmd.clone.clone, body=%wide.region_0.1_spmd.clone.clone.sunk | while | flops 766117632 | bytes 53786332 | solution.py:254
  17.6 7.3 all-to-all-start.1
  32.2 6.3 all-to-all-start
  118.9 11.5 %collective-permute-done.3 = bf16[1,2,1,512]{2,3,1,0:T(8,128)(2,1)S(1)} collective-permute-done((bf16[1,2,1,512]{2,3,1,0:T(8,128)(2,1)S(1)}, bf16[1,2,1,512]{2,3,1,0:T(8,128)(2,1)S(1)}, u32[]{:S(2)}, u32[]{:S(2)}) %collective-permute-start.3) | collective-permute-done | bytes 2080 | tf_op jit(solution)/shard_map/while/body/eval_jaxpr/ppermute | solution.py:21
  159.5 6.1 all-to-all-start
  214.1 6.0 all-to-all-done.2
  232.0 10.3 %collective-permute-done = bf16[1,2,1,512]{2,3,1,0:T(8,128)(2,1)S(1)} collective-permute-done((bf16[1,2,1,512]{2,3,1,0:T(8,128)(2,1)S(1)}, bf16[1,2,1,512]{2,3,1,0:T(8,128)(2,1)S(1)}, u32[]{:S(2)}, u32[]{:S(2)}) %collective-permute-start) | collective-permute-done | bytes 2080 | tf_op jit(solution)/shard_map/while/body/eval_jaxpr/ppermute | solution.py:21
  249.7 11.6 %collective-permute-done.3 = bf16[1,2,1,512]{2,3,1,0:T(8,128)(2,1)S(1)} collective-permute-done((bf16[1,2,1,512]{2,3,1,0:T(8,128)(2,1)S(1)}, bf16[1,2,1,512]{2,3,1,0:T(8,128)(2,1)S(1)}, u32[]{:S(2)}, u32[]{:S(2)}) %collective-permute-start.3) | collective-permute-done | bytes 2080 | tf_op jit(solution)/shard_map/while/body/eval_jaxpr/ppermute | solution.py:21
  298.1 6.3 all-to-all-done
  362.6 9.8 %collective-permute-done = bf16[1,2,1,512]{2,3,1,0:T(8,128)(2,1)S(1)} collective-permute-done((bf16[1,2,1,512]{2,3,1,0:T(8,128)(2,1)S(1)}, bf16[1,2,1,512]{2,3,1,0:T(8,128)(2,1)S(1)}, u32[]{:S(2)}, u32[]{:S(2)}) %collective-permute-start) | collective-permute-done | bytes 2080 | tf_op jit(solution)/shard_map/while/body/eval_jaxpr/ppermute | solution.py:21
  379.5 12.4 %collective-permute-done.3 = bf16[1,2,1,512]{2,3,1,0:T(8,128)(2,1)S(1)} collective-permute-done((bf16[1,2,1,512]{2,3,1,0:T(8,128)(2,1)S(1)}, bf16[1,2,1,512]{2,3,1,0:T(8,128)(2,1)S(1)}, u32[]{:S(2)}, u32[]{:S(2)}) %collective-permute-start.3) | collective-permute-done | bytes 2080 | tf_op jit(solution)/shard_map/while/body/eval_jaxpr/ppermute | solution.py:21
  428.3 6.3 all-to-all-done
  475.2 6.0 all-to-all-done.2
  493.1 9.8 %collective-permute-done = bf16[1,2,1,512]{2,3,1,0:T(8,128)(2,1)S(1)} collective-permute-done((bf16[1,2,1,512]{2,3,1,0:T(8,128)(2,1)S(1)}, bf16[1,2,1,512]{2,3,1,0:T(8,128)(2,1)S(1)}, u32[]{:S(2)}, u32[]{:S(2)}) %collective-permute-start) | collective-permute-done | bytes 2080 | tf_op jit(solution)/shard_map/while/body/eval_jaxpr/ppermute | solution.py:21
  509.9 12.6 %collective-permute-done.3 = bf16[1,2,1,512]{2,3,1,0:T(8,128)(2,1)S(1)} collective-permute-done((bf16[1,2,1,512]{2,3,1,0:T(8,128)(2,1)S(1)}, bf16[1,2,1,512]{2,3,1,0:T(8,128)(2,1)S(1)}, u32[]{:S(2)}, u32[]{:S(2)}) %collective-permute-start.3) | collective-permute-done | bytes 2080 | tf_op jit(solution)/shard_map/while/body/eval_jaxpr/ppermute | solution.py:21
  551.1 6.1 all-to-all-start
  558.8 6.1 all-to-all-done
  605.6 6.0 all-to-all-done.2
  623.5 9.8 %collective-permute-done = bf16[1,2,1,512]{2,3,1,0:T(8,128)(2,1)S(1)} collective-permute-done((bf16[1,2,1,512]{2,3,1,0:T(8,128)(2,1)S(1)}, bf16[1,2,1,512]{2,3,1,0:T(8,128)(2,1)S(1)}, u32[]{:S(2)}, u32[]{:S(2)}) %collective-permute-start) | collective-permute-done | bytes 2080 | tf_op jit(solution)/shard_map/while/body/eval_jaxpr/ppermute | solution.py:21
  640.4 12.4 %collective-permute-done.3 = bf16[1,2,1,512]{2,3,1,0:T(8,128)(2,1)S(1)} collective-permute-done((bf16[1,2,1,512]{2,3,1,0:T(8,128)(2,1)S(1)}, bf16[1,2,1,512]{2,3,1,0:T(8,128)(2,1)S(1)}, u32[]{:S(2)}, u32[]{:S(2)}) %collective-permute-start.3) | collective-permute-done | bytes 2080 | tf_op jit(solution)/shard_map/while/body/eval_jaxpr/ppermute | solution.py:21
  689.3 6.3 all-to-all-done
  736.2 6.0 all-to-all-done.2
  754.0 9.8 %collective-permute-done = bf16[1,2,1,512]{2,3,1,0:T(8,128)(2,1)S(1)} collective-permute-done((bf16[1,2,1,512]{2,3,1,0:T(8,128)(2,1)S(1)}, bf16[1,2,1,512]{2,3,1,0:T(8,128)(2,1)S(1)}, u32[]{:S(2)}, u32[]{:S(2)}) %collective-permute-start) | collective-permute-done | bytes 2080 | tf_op jit(solution)/shard_map/while/body/eval_jaxpr/ppermute | solution.py:21
  770.9 12.6 %collective-permute-done.3 = bf16[1,2,1,512]{2,3,1,0:T(8,128)(2,1)S(1)} collective-permute-done((bf16[1,2,1,512]{2,3,1,0:T(8,128)(2,1)S(1)}, bf16[1,2,1,512]{2,3,1,0:T(8,128)(2,1)S(1)}, u32[]{:S(2)}, u32[]{:S(2)}) %collective-permute-start.3) | collective-permute-done | bytes 2080 | tf_op jit(solution)/shard_map/while/body/eval_jaxpr/ppermute | solution.py:21
  (1063 shorter events, 568.4 us)
Async XLA Ops:
  17.6 14.6 %all-to-all-start.1 = ((bf16[8,2,4096]{2,1,0:T(2,128)(2,1)}), bf16[8,2,4096]{2,1,0:T(2,128)(2,1)S(1)}, u32[]{:S(2)}, u32[]{:S(2)}) async-start(bf16[8,2,4096]{2,1,0:T(2,128)(2,1)} %reshape.2402), calls=%async_computation.1 | async-start | bytes 262144 | tf_op jit(solution)/shard_map/while/body/eval_jaxpr/all_to_all | solution.py:215
  32.2 13.3 %all-to-all-start = ((bf16[8,2,4096]{2,1,0:T(2,128)(2,1)}), bf16[8,2,4096]{2,1,0:T(2,128)(2,1)S(1)}, u32[]{:S(2)}, u32[]{:S(2)}) async-start(bf16[8,2,4096]{2,1,0:T(2,128)(2,1)} %reshape.2398), calls=%async_computation | async-start | bytes 262144 | tf_op jit(solution)/shard_map/while/body/eval_jaxpr/all_to_all | solution.py:216
  115.3 15.4 %collective-permute-start.2 = (bf16[1,2,64,512]{2,3,1,0:T(8,128)(2,1)S(1)}, bf16[1,2,64,512]{2,3,1,0:T(8,128)(2,1)S(1)}, u32[]{:S(2)}, u32[]{:S(2)}) collective-permute-start(bf16[1,2,64,512]{2,3,1,0:T(8,128)(2,1)S(1)} %get-tuple-element.913), channel_id=1, source_target_pairs={{0,8},{8,16},{16,24},{1,9},{9,17},{17,25},{2,10},{10,18},{18,26},{... | collective-permute-start | bytes 393224 | tf_op jit(solution)/shard_map/while/body/eval_jaxpr/ppermute | solution.py:29
  116.8 13.6 %collective-permute-start.3 = (bf16[1,2,1,512]{2,3,1,0:T(8,128)(2,1)S(1)}, bf16[1,2,1,512]{2,3,1,0:T(8,128)(2,1)S(1)}, u32[]{:S(2)}, u32[]{:S(2)}) collective-permute-start(bf16[1,2,1,512]{2,3,1,0:T(8,128)(2,1)S(1)} %get-tuple-element.916), channel_id=1, source_target_pairs={{1,0},{2,1},{3,2},{4,3},{5,4},{6,5},{7,6},{0,7},{9,8},{10,9},{11,1... | collective-permute-start | bytes 6152 | tf_op jit(solution)/shard_map/while/body/eval_jaxpr/ppermute | solution.py:21
  159.5 13.3 %all-to-all-start = ((bf16[8,2,4096]{2,1,0:T(2,128)(2,1)}), bf16[8,2,4096]{2,1,0:T(2,128)(2,1)S(1)}, u32[]{:S(2)}, u32[]{:S(2)}) async-start(bf16[8,2,4096]{2,1,0:T(2,128)(2,1)} %reshape.2398), calls=%async_computation | async-start | bytes 262144 | tf_op jit(solution)/shard_map/while/body/eval_jaxpr/all_to_all | solution.py:216
  229.8 12.5 %collective-permute-start = (bf16[1,2,1,512]{2,3,1,0:T(8,128)(2,1)S(1)}, bf16[1,2,1,512]{2,3,1,0:T(8,128)(2,1)S(1)}, u32[]{:S(2)}, u32[]{:S(2)}) collective-permute-start(bf16[1,2,1,512]{2,3,1,0:T(8,128)(2,1)S(1)} %get-tuple-element.905), channel_id=1, source_target_pairs={{1,0},{2,1},{3,2},{4,3},{5,4},{6,5},{7,6},{0,7},{9,8},{10,9},{11,1... | collective-permute-start | bytes 6152 | tf_op jit(solution)/shard_map/while/body/eval_jaxpr/ppermute | solution.py:21
  245.8 15.8 %collective-permute-start.2 = (bf16[1,2,64,512]{2,3,1,0:T(8,128)(2,1)S(1)}, bf16[1,2,64,512]{2,3,1,0:T(8,128)(2,1)S(1)}, u32[]{:S(2)}, u32[]{:S(2)}) collective-permute-start(bf16[1,2,64,512]{2,3,1,0:T(8,128)(2,1)S(1)} %get-tuple-element.913), channel_id=1, source_target_pairs={{0,8},{8,16},{16,24},{1,9},{9,17},{17,25},{2,10},{10,18},{18,26},{... | collective-permute-start | bytes 393224 | tf_op jit(solution)/shard_map/while/body/eval_jaxpr/ppermute | solution.py:29
  247.2 14.0 %collective-permute-start.3 = (bf16[1,2,1,512]{2,3,1,0:T(8,128)(2,1)S(1)}, bf16[1,2,1,512]{2,3,1,0:T(8,128)(2,1)S(1)}, u32[]{:S(2)}, u32[]{:S(2)}) collective-permute-start(bf16[1,2,1,512]{2,3,1,0:T(8,128)(2,1)S(1)} %get-tuple-element.916), channel_id=1, source_target_pairs={{1,0},{2,1},{3,2},{4,3},{5,4},{6,5},{7,6},{0,7},{9,8},{10,9},{11,1... | collective-permute-start | bytes 6152 | tf_op jit(solution)/shard_map/while/body/eval_jaxpr/ppermute | solution.py:21
  290.9 13.6 %all-to-all-start = ((bf16[8,2,4096]{2,1,0:T(2,128)(2,1)}), bf16[8,2,4096]{2,1,0:T(2,128)(2,1)S(1)}, u32[]{:S(2)}, u32[]{:S(2)}) async-start(bf16[8,2,4096]{2,1,0:T(2,128)(2,1)} %reshape.2398), calls=%async_computation | async-start | bytes 262144 | tf_op jit(solution)/shard_map/while/body/eval_jaxpr/all_to_all | solution.py:216
  375.9 16.3 %collective-permute-start.2 = (bf16[1,2,64,512]{2,3,1,0:T(8,128)(2,1)S(1)}, bf16[1,2,64,512]{2,3,1,0:T(8,128)(2,1)S(1)}, u32[]{:S(2)}, u32[]{:S(2)}) collective-permute-start(bf16[1,2,64,512]{2,3,1,0:T(8,128)(2,1)S(1)} %get-tuple-element.913), channel_id=1, source_target_pairs={{0,8},{8,16},{16,24},{1,9},{9,17},{17,25},{2,10},{10,18},{18,26},{... | collective-permute-start | bytes 393224 | tf_op jit(solution)/shard_map/while/body/eval_jaxpr/ppermute | solution.py:29
  377.4 14.5 %collective-permute-start.3 = (bf16[1,2,1,512]{2,3,1,0:T(8,128)(2,1)S(1)}, bf16[1,2,1,512]{2,3,1,0:T(8,128)(2,1)S(1)}, u32[]{:S(2)}, u32[]{:S(2)}) collective-permute-start(bf16[1,2,1,512]{2,3,1,0:T(8,128)(2,1)S(1)} %get-tuple-element.916), channel_id=1, source_target_pairs={{1,0},{2,1},{3,2},{4,3},{5,4},{6,5},{7,6},{0,7},{9,8},{10,9},{11,1... | collective-permute-start | bytes 6152 | tf_op jit(solution)/shard_map/while/body/eval_jaxpr/ppermute | solution.py:21
  378.2 13.6 %collective-permute-start.4 = (bf16[1,2,1,512]{2,3,1,0:T(8,128)(2,1)S(1)}, bf16[1,2,1,512]{2,3,1,0:T(8,128)(2,1)S(1)}, u32[]{:S(2)}, u32[]{:S(2)}) collective-permute-start(bf16[1,2,1,512]{2,3,1,0:T(8,128)(2,1)S(1)} %get-tuple-element.917), channel_id=1, source_target_pairs={{0,1},{1,2},{2,3},{3,4},{4,5},{5,6},{6,7},{7,0},{8,9},{9,10},{10,1... | collective-permute-start | bytes 6152 | tf_op jit(solution)/shard_map/while/body/eval_jaxpr/ppermute | solution.py:20
  420.7 13.8 %all-to-all-start = ((bf16[8,2,4096]{2,1,0:T(2,128)(2,1)}), bf16[8,2,4096]{2,1,0:T(2,128)(2,1)S(1)}, u32[]{:S(2)}, u32[]{:S(2)}) async-start(bf16[8,2,4096]{2,1,0:T(2,128)(2,1)} %reshape.2398), calls=%async_computation | async-start | bytes 262144 | tf_op jit(solution)/shard_map/while/body/eval_jaxpr/all_to_all | solution.py:216
  506.4 16.5 %collective-permute-start.2 = (bf16[1,2,64,512]{2,3,1,0:T(8,128)(2,1)S(1)}, bf16[1,2,64,512]{2,3,1,0:T(8,128)(2,1)S(1)}, u32[]{:S(2)}, u32[]{:S(2)}) collective-permute-start(bf16[1,2,64,512]{2,3,1,0:T(8,128)(2,1)S(1)} %get-tuple-element.913), channel_id=1, source_target_pairs={{0,8},{8,16},{16,24},{1,9},{9,17},{17,25},{2,10},{10,18},{18,26},{... | collective-permute-start | bytes 393224 | tf_op jit(solution)/shard_map/while/body/eval_jaxpr/ppermute | solution.py:29
  507.9 14.7 %collective-permute-start.3 = (bf16[1,2,1,512]{2,3,1,0:T(8,128)(2,1)S(1)}, bf16[1,2,1,512]{2,3,1,0:T(8,128)(2,1)S(1)}, u32[]{:S(2)}, u32[]{:S(2)}) collective-permute-start(bf16[1,2,1,512]{2,3,1,0:T(8,128)(2,1)S(1)} %get-tuple-element.916), channel_id=1, source_target_pairs={{1,0},{2,1},{3,2},{4,3},{5,4},{6,5},{7,6},{0,7},{9,8},{10,9},{11,1... | collective-permute-start | bytes 6152 | tf_op jit(solution)/shard_map/while/body/eval_jaxpr/ppermute | solution.py:21
  509.5 13.0 %collective-permute-start.4 = (bf16[1,2,1,512]{2,3,1,0:T(8,128)(2,1)S(1)}, bf16[1,2,1,512]{2,3,1,0:T(8,128)(2,1)S(1)}, u32[]{:S(2)}, u32[]{:S(2)}) collective-permute-start(bf16[1,2,1,512]{2,3,1,0:T(8,128)(2,1)S(1)} %get-tuple-element.917), channel_id=1, source_target_pairs={{0,1},{1,2},{2,3},{3,4},{4,5},{5,6},{6,7},{7,0},{8,9},{9,10},{10,1... | collective-permute-start | bytes 6152 | tf_op jit(solution)/shard_map/while/body/eval_jaxpr/ppermute | solution.py:20
  551.1 13.8 %all-to-all-start = ((bf16[8,2,4096]{2,1,0:T(2,128)(2,1)}), bf16[8,2,4096]{2,1,0:T(2,128)(2,1)S(1)}, u32[]{:S(2)}, u32[]{:S(2)}) async-start(bf16[8,2,4096]{2,1,0:T(2,128)(2,1)} %reshape.2398), calls=%async_computation | async-start | bytes 262144 | tf_op jit(solution)/shard_map/while/body/eval_jaxpr/all_to_all | solution.py:216
  636.8 16.3 %collective-permute-start.2 = (bf16[1,2,64,512]{2,3,1,0:T(8,128)(2,1)S(1)}, bf16[1,2,64,512]{2,3,1,0:T(8,128)(2,1)S(1)}, u32[]{:S(2)}, u32[]{:S(2)}) collective-permute-start(bf16[1,2,64,512]{2,3,1,0:T(8,128)(2,1)S(1)} %get-tuple-element.913), channel_id=1, source_target_pairs={{0,8},{8,16},{16,24},{1,9},{9,17},{17,25},{2,10},{10,18},{18,26},{... | collective-permute-start | bytes 393224 | tf_op jit(solution)/shard_map/while/body/eval_jaxpr/ppermute | solution.py:29
  638.3 14.5 %collective-permute-start.3 = (bf16[1,2,1,512]{2,3,1,0:T(8,128)(2,1)S(1)}, bf16[1,2,1,512]{2,3,1,0:T(8,128)(2,1)S(1)}, u32[]{:S(2)}, u32[]{:S(2)}) collective-permute-start(bf16[1,2,1,512]{2,3,1,0:T(8,128)(2,1)S(1)} %get-tuple-element.916), channel_id=1, source_target_pairs={{1,0},{2,1},{3,2},{4,3},{5,4},{6,5},{7,6},{0,7},{9,8},{10,9},{11,1... | collective-permute-start | bytes 6152 | tf_op jit(solution)/shard_map/while/body/eval_jaxpr/ppermute | solution.py:21
  640.1 12.8 %collective-permute-start.4 = (bf16[1,2,1,512]{2,3,1,0:T(8,128)(2,1)S(1)}, bf16[1,2,1,512]{2,3,1,0:T(8,128)(2,1)S(1)}, u32[]{:S(2)}, u32[]{:S(2)}) collective-permute-start(bf16[1,2,1,512]{2,3,1,0:T(8,128)(2,1)S(1)} %get-tuple-element.917), channel_id=1, source_target_pairs={{0,1},{1,2},{2,3},{3,4},{4,5},{5,6},{6,7},{7,0},{8,9},{9,10},{10,1... | collective-permute-start | bytes 6152 | tf_op jit(solution)/shard_map/while/body/eval_jaxpr/ppermute | solution.py:20
  681.7 13.9 %all-to-all-start = ((bf16[8,2,4096]{2,1,0:T(2,128)(2,1)}), bf16[8,2,4096]{2,1,0:T(2,128)(2,1)S(1)}, u32[]{:S(2)}, u32[]{:S(2)}) async-start(bf16[8,2,4096]{2,1,0:T(2,128)(2,1)} %reshape.2398), calls=%async_computation | async-start | bytes 262144 | tf_op jit(solution)/shard_map/while/body/eval_jaxpr/all_to_all | solution.py:216
  767.4 16.5 %collective-permute-start.2 = (bf16[1,2,64,512]{2,3,1,0:T(8,128)(2,1)S(1)}, bf16[1,2,64,512]{2,3,1,0:T(8,128)(2,1)S(1)}, u32[]{:S(2)}, u32[]{:S(2)}) collective-permute-start(bf16[1,2,64,512]{2,3,1,0:T(8,128)(2,1)S(1)} %get-tuple-element.913), channel_id=1, source_target_pairs={{0,8},{8,16},{16,24},{1,9},{9,17},{17,25},{2,10},{10,18},{18,26},{... | collective-permute-start | bytes 393224 | tf_op jit(solution)/shard_map/while/body/eval_jaxpr/ppermute | solution.py:29
  768.8 14.7 %collective-permute-start.3 = (bf16[1,2,1,512]{2,3,1,0:T(8,128)(2,1)S(1)}, bf16[1,2,1,512]{2,3,1,0:T(8,128)(2,1)S(1)}, u32[]{:S(2)}, u32[]{:S(2)}) collective-permute-start(bf16[1,2,1,512]{2,3,1,0:T(8,128)(2,1)S(1)} %get-tuple-element.916), channel_id=1, source_target_pairs={{1,0},{2,1},{3,2},{4,3},{5,4},{6,5},{7,6},{0,7},{9,8},{10,9},{11,1... | collective-permute-start | bytes 6152 | tf_op jit(solution)/shard_map/while/body/eval_jaxpr/ppermute | solution.py:21
  770.5 13.0 %collective-permute-start.4 = (bf16[1,2,1,512]{2,3,1,0:T(8,128)(2,1)S(1)}, bf16[1,2,1,512]{2,3,1,0:T(8,128)(2,1)S(1)}, u32[]{:S(2)}, u32[]{:S(2)}) collective-permute-start(bf16[1,2,1,512]{2,3,1,0:T(8,128)(2,1)S(1)} %get-tuple-element.917), channel_id=1, source_target_pairs={{0,1},{1,2},{2,3},{3,4},{4,5},{5,6},{6,7},{7,0},{8,9},{9,10},{10,1... | collective-permute-start | bytes 6152 | tf_op jit(solution)/shard_map/while/body/eval_jaxpr/ppermute | solution.py:20
  (70 other events, 475.0 us)
where the time goes:
time: 796 us; the launch traced here: 790 us
  waiting for transfers between devices  248 us (31%)
  matrix products  223 us (28%)
  starting transfers between devices  137 us (17%)
  local copies, waits for them, and re-layouts  80.6 us (10%)
  other arithmetic  77.5 us (10%)
  loops' own time  23.9 us (3%)
    ppermute x12, waiting for transfers between devices, extended_2(): after = lax.ppermute(initial, axis, down)  128 us
    dot_general x96, matrix products, contract(): product(values[1], matrix[0])  73.9 us
    dot_general x96, matrix products, contract(): product(values[1], matrix[1])  60.1 us
    dot_general x96, matrix products, contract(): product(values[0], matrix[0]) - product(values[1], matrix[1])  44.4 us
    dot_general x96, matrix products, contract(): product(values[0], matrix[1]) + product(values[1], matrix[0])  44.2 us
    all_to_all x6, starting transfers between devices, one_tick(): lax.all_to_all(joined_bf16(spec_a), 'rows', split_axis=3, concat_axis=3,...  36.1 us
    all_to_all x6, waiting for transfers between devices, one_tick(): lax.all_to_all(outgoing[1], 'rows', split_axis=3, concat_axis=3, tiled=True)  36 us
    all_to_all x6, waiting for transfers between devices, one_tick(): lax.all_to_all(joined_bf16(spec_a), 'rows', split_axis=3, concat_axis=3,...  36 us
  transfers between devices with their start and end apart: 60, of which 40 were waited for; matrix products, arithmetic and copies ran while one was open for 9% of the time, Pallas kernels for 0%

commit v1 on v0

v1 whole, which is shorter than its diff:
```python
from functools import partial
import math

import jax
import jax.numpy as jnp
import numpy as np
from jax import lax
from jax.experimental import pallas as pl
from jax.experimental.pallas import tpu as pltpu
from jax.sharding import PartitionSpec as P

bf16 = jnp.bfloat16
f32 = jnp.float32
vmem_bytes = 48 * 1024 * 1024


def basis(length):
    half, quarter = length // 2, length // 4
    n = np.arange(half)[:, None]
    j = np.arange(quarter)[None, :]
    scale = math.sqrt(2.0 / length)
    even_cos = scale * np.cos(2 * np.pi * ((2 * j * n) % length) / length)
    even_sin = scale * np.sin(2 * np.pi * ((2 * j * n) % length) / length)
    even_cos[:, 0] = 1.0 / math.sqrt(length)
    even_sin[:, 0] = (1.0 - 2.0 * (np.arange(half) % 2)) / math.sqrt(length)
    odd_cos = scale * np.cos(2 * np.pi * (((2 * j + 1) * n) % length) / length)
    odd_sin = scale * np.sin(2 * np.pi * (((2 * j + 1) * n) % length) / length)
    even = np.concatenate([even_cos, even_sin], 1).astype(np.float32)
    odd = np.concatenate([odd_cos, odd_sin], 1).astype(np.float32)
    return even, odd


def basis_tables(length):
    even, odd = basis(length)
    return jnp.asarray(np.stack([even, odd, even.T, odd.T]), bf16)


def dot(a, b):
    return jnp.dot(a, b, preferred_element_type=f32)


def small_cos_sin(a):
    s = a * a
    cos = 1.0 + s * (-0.5 + s * (1.0 / 24 + s * (-1.0 / 720 + s * (1.0 / 40320))))
    sin = a * (1.0 + s * (-1.0 / 6 + s * (1.0 / 120 + s * (-1.0 / 5040 + s * (1.0 / 362880)))))
    return cos, sin


def phase_kernel(nx, ny, ks_ref, sign_ref, out_ref):
    qx, qy = nx // 4, ny // 4
    slot = pl.program_id(0)
    level = ks_ref[slot]
    sign = sign_ref[0]

    def waves(rows, cols, axis, parity, length):
        j = lax.broadcasted_iota(jnp.int32, (rows, cols), axis)
        return (2 * j + parity).astype(f32) * (2.0 * math.pi / length)

    def values(kx, ky):
        squared = level * level - kx * kx - ky * ky
        damping = jnp.exp(-jnp.sqrt(jnp.maximum(-squared, 0.0)))
        angle = jnp.sqrt(jnp.maximum(squared, 0.0))
        return damping * jnp.cos(angle), sign * damping * jnp.sin(angle)

    edge = math.pi
    for px in range(2):
        for py in range(2):
            kx = waves(qx, qy, 0, px, nx)
            ky = waves(qx, qy, 1, py, ny)
            first_row = lax.broadcasted_iota(jnp.int32, (qx, qy), 0) == 0
            first_col = lax.broadcasted_iota(jnp.int32, (qx, qy), 1) == 0
            for sx in range(2):
                for sy in range(2):
                    if (sx and not px) or (sy and not py):
                        kxs = jnp.where(first_row, edge, kx) if (sx and not px) else kx
                        kys = jnp.where(first_col, edge, ky) if (sy and not py) else ky
                    else:
                        kxs, kys = kx, ky
                    re, im = values(kxs, kys)
                    rows = pl.ds((2 * px + sx) * qx, qx)
                    cols = pl.ds((2 * py + sy) * qy, qy)
                    out_ref[0, 0, rows, cols] = re.astype(bf16)
                    out_ref[0, 1, rows, cols] = im.astype(bf16)


def phase_table(nx, ny, levels, sign):
    slots = levels.shape[0]
    return pl.pallas_call(
        partial(phase_kernel, nx, ny),
        out_shape=jax.ShapeDtypeStruct((slots, 2, nx, ny), bf16),
        grid=(slots,),
        in_specs=[pl.BlockSpec(memory_space=pltpu.SMEM)] * 2,
        out_specs=pl.BlockSpec((1, 2, nx, ny), lambda i: (i, 0, 0, 0)),
        compiler_params=pltpu.CompilerParams(vmem_limit_bytes=vmem_bytes),
        name="phase_table",
    )(levels, sign)


def fold_cols(values):
    half = values.shape[1] // 2
    a, b = values[:, :half], values[:, half:]
    return (a + b).astype(bf16), (a - b).astype(bf16)


def transform(nx, ny, folded, phase, qx_ref, qy_ref, mid, spec, out):
    hx, hy = nx // 2, ny // 2
    step = min(128, hx)
    for part in range(2):
        for start in range(0, hx, step):
            top, low = pl.ds(start, step), pl.ds(hx + start, step)
            for par in range(2):
                cols = pl.ds(par * hy, hy)
                a = dot(folded[part, top, cols], qy_ref[par])
                b = dot(folded[part, low, cols], qy_ref[par])
                mid[part, top, cols] = (a + b).astype(bf16)
                mid[part, low, cols] = (a - b).astype(bf16)
    for start in range(0, ny, hy):
        cols = pl.ds(start, hy)
        back = []
        for par in range(2):
            rows = pl.ds(par * hx, hx)
            zr = dot(qx_ref[2 + par], mid[0, rows, cols])
            zi = dot(qx_ref[2 + par], mid[1, rows, cols])
            pr = phase[0, 0, rows, cols].astype(f32)
            pi = phase[0, 1, rows, cols].astype(f32)
            yr = (zr * pr - zi * pi).astype(bf16)
            yi = (zr * pi + zi * pr).astype(bf16)
            back.append((dot(qx_ref[par], yr), dot(qx_ref[par], yi)))
        for part in range(2):
            a, b = back[0][part], back[1][part]
            spec[part, pl.ds(0, hx), cols] = (a + b).astype(bf16)
            spec[part, pl.ds(hx, hx), cols] = (a - b).astype(bf16)
    for part in range(2):
        for start in range(0, nx, 2 * step):
            rows = pl.ds(start, 2 * step)
            a = dot(spec[part, rows, pl.ds(0, hy)], qy_ref[2])
            b = dot(spec[part, rows, pl.ds(hy, hy)], qy_ref[3])
            out[part, rows, pl.ds(0, hy)] = (a + b).astype(bf16)
            out[part, rows, pl.ds(hy, hy)] = (a - b).astype(bf16)


def first_kernel(dims, orders, ints_ref, phase, qx_ref, qy_ref, *rest):
    nx, ny, rows_here = dims
    counts = [len(o) for o in orders]
    pieces, (out, folded, mid, spec) = rest[: sum(counts)], rest[sum(counts) :]
    part_id, forward = ints_ref[0], ints_ref[1]
    at = 0
    for part, order in enumerate(orders):
        for piece_order in order:
            piece = pieces[at]
            at += 1
            for i, offset in enumerate(piece_order):
                block = part_id ^ offset
                rows = pl.ds(pl.multiple_of(block * rows_here, rows_here), rows_here)
                values = piece[i]

                @pl.when(forward == 1)
                def _():
                    a, b = fold_cols(values.astype(f32))
                    folded[part, rows, pl.ds(0, ny // 2)] = a
                    folded[part, rows, pl.ds(ny // 2, ny // 2)] = b

                @pl.when(forward == 0)
                def _():
                    out[part, rows, :] = values

    @pl.when(forward == 1)
    def _():
        transform(nx, ny, folded, phase, qx_ref, qy_ref, mid, spec, out)


def laplace_rows(ref, part, start, count):
    center = ref[part, pl.ds(start + 8, count), :]
    width = center.shape[1]
    return (
        ref[part, pl.ds(start + 7, count), :]
        + ref[part, pl.ds(start + 9, count), :]
        + pltpu.roll(center, 1, 1)
        + pltpu.roll(center, width - 1, 1)
        - 4.0 * center
    )


def wrap_rows(ref, nx):
    for part in range(2):
        ref[part, pl.ds(7, 1), :] = ref[part, pl.ds(nx + 7, 1), :]
        ref[part, pl.ds(nx + 8, 1), :] = ref[part, pl.ds(8, 1), :]


def step_kernel(
    dims, pos, last, ints_ref, omega_ref, w_ref, own_ref, other_ref, phase, qx_ref, qy_ref, *rest
):
    nx, ny, rows_here = dims
    if last:
        (coef_rows, edges, out_rows, end_rows, out, coef, lens, plane, halo, folded, mid, spec, tall) = rest
    else:
        out, out_rows, coef, lens, plane, halo, folded, mid, spec = rest
    part_id, forward, side = ints_ref[0], ints_ref[1], ints_ref[2]
    omega = omega_ref[0]
    hy = ny // 2
    blocks = nx // rows_here
    for q, src in enumerate((own_ref, other_ref)):
        cols = pl.ds(pl.multiple_of((side ^ q) * hy, hy), hy)
        for offset in range(blocks):
            block = part_id ^ offset
            rows = pl.ds(pl.multiple_of(block * rows_here, rows_here), rows_here)
            coef[rows, cols] = src[pos[0][offset]].astype(f32)
            cos, sin = small_cos_sin(omega * src[blocks + pos[1][offset]].astype(f32))
            lens[0, rows, cols] = cos
            lens[1, rows, cols] = sin
    chunk = 32

    @pl.when(forward == 1)
    def _():
        for start in range(0, nx, chunk):
            rows = pl.ds(start, chunk)
            lr, li = lens[0, rows, :], lens[1, rows, :]
            wr, wi = w_ref[0, rows, :].astype(f32), w_ref[1, rows, :].astype(f32)
            c = coef[rows, :]
            ur, ui = wr * lr - wi * li, wr * li + wi * lr
            plane[0, rows, :] = ur
            plane[1, rows, :] = ui
            halo[0, pl.ds(start + 8, chunk), :] = c * ur
            halo[1, pl.ds(start + 8, chunk), :] = c * ui
        wrap_rows(halo, nx)
        for start in range(0, nx, chunk):
            rows = pl.ds(start, chunk)
            ur = plane[0, rows, :] - laplace_rows(halo, 1, start, chunk)
            ui = plane[1, rows, :] + laplace_rows(halo, 0, start, chunk)
            plane[0, rows, :] = ur
            plane[1, rows, :] = ui
            for part, u in enumerate((ur, ui)):
                a, b = fold_cols(u)
                folded[part, rows, pl.ds(0, hy)] = a
                folded[part, rows, pl.ds(hy, hy)] = b
        mine = pl.ds(pl.multiple_of(part_id * rows_here, rows_here), rows_here)
        for part in range(2):
            out_rows[part] = plane[part, mine, :].astype(bf16)

    @pl.when(forward == 0)
    def _():
        for part in range(2):
            halo[part, pl.ds(8, nx), :] = w_ref[part].astype(f32)
        wrap_rows(halo, nx)
        for start in range(0, nx, chunk):
            rows = pl.ds(start, chunk)
            lr, li = lens[0, rows, :], lens[1, rows, :]
            c = coef[rows, :]
            tr = halo[0, pl.ds(start + 8, chunk), :] + c * laplace_rows(halo, 1, start, chunk)
            ti = halo[1, pl.ds(start + 8, chunk), :] - c * laplace_rows(halo, 0, start, chunk)
            for part, u in enumerate((tr * lr + ti * li, ti * lr - tr * li)):
                a, b = fold_cols(u)
                folded[part, rows, pl.ds(0, hy)] = a
                folded[part, rows, pl.ds(hy, hy)] = b

    transform(nx, ny, folded, phase, qx_ref, qy_ref, mid, spec, out)
    first = pl.multiple_of(part_id * rows_here, rows_here)
    mine = pl.ds(first, rows_here)

    @pl.when(forward == 0)
    def _():
        for part in range(2):
            out_rows[part] = out[part, mine, :]

    if not last:
        return

    @pl.when(forward == 0)
    def _():
        end_rows[...] = jnp.zeros_like(end_rows)

    @pl.when(forward == 1)
    def _():
        before = pl.ds(pl.multiple_of(lax.rem(first + nx - 16, nx), 16), 16)
        after = pl.ds(pl.multiple_of(lax.rem(first + rows_here, nx), 16), 16)

        def scaled(values, c, d):
            lr, li = small_cos_sin(omega * d.astype(f32))
            wr, wi = values[0].astype(f32), values[1].astype(f32)
            ur, ui = wr * lr - wi * li, wr * li + wi * lr
            cf = c.astype(f32)
            return ur, ui, cf * ur, cf * ui

        ur, ui, gr, gi = scaled(
            (out[0, mine, :], out[1, mine, :]), coef_rows[0], coef_rows[1]
        )
        tall[0, pl.ds(8, rows_here), :] = gr
        tall[1, pl.ds(8, rows_here), :] = gi
        _, _, gr, gi = scaled(
            (out[0, before, :][15:16], out[1, before, :][15:16]), edges[0, 0], edges[0, 1]
        )
        tall[0, pl.ds(7, 1), :] = gr
        tall[1, pl.ds(7, 1), :] = gi
        _, _, gr, gi = scaled(
            (out[0, after, :][0:1], out[1, after, :][0:1]), edges[1, 0], edges[1, 1]
        )
        tall[0, pl.ds(rows_here + 8, 1), :] = gr
        tall[1, pl.ds(rows_here + 8, 1), :] = gi
        end_rows[0] = (ur - laplace_rows(tall, 1, 0, rows_here)).astype(bf16)
        end_rows[1] = (ui + laplace_rows(tall, 0, 0, rows_here)).astype(bf16)


vm = pl.BlockSpec(memory_space=pltpu.VMEM)
sm = pl.BlockSpec(memory_space=pltpu.SMEM)


def phase_spec(slot, nx, ny):
    return pl.BlockSpec((1, 2, nx, ny), lambda i: (slot, 0, 0, 0))


def run_first(dims, orders, ints, phases, qx, qy, pieces):
    nx, ny, _ = dims
    return pl.pallas_call(
        partial(first_kernel, dims, orders),
        out_shape=jax.ShapeDtypeStruct((2, nx, ny), bf16),
        grid=(1,),
        in_specs=[sm, phase_spec(0, nx, ny), vm, vm] + [vm] * len(pieces),
        out_specs=vm,
        scratch_shapes=[pltpu.VMEM((2, nx, ny), bf16)] * 3,
        compiler_params=pltpu.CompilerParams(vmem_limit_bytes=vmem_bytes),
        cost_estimate=pl.CostEstimate(flops=2**30, bytes_accessed=2**22, transcendentals=0),
        name="first_step",
    )(ints, phases, qx, qy, *pieces)


def run_step(dims, pos, slot, ints, omega, w, own, other, phases, qx, qy, ends=None):
    nx, ny, rows_here = dims
    last = ends is not None
    rows_shape = jax.ShapeDtypeStruct((2, rows_here, ny), bf16)
    full = pltpu.VMEM((2, nx, ny), bf16)
    scratch = [
        pltpu.VMEM((nx, ny), f32),
        pltpu.VMEM((2, nx, ny), f32),
        pltpu.VMEM((2, nx, ny), f32),
        pltpu.VMEM((2, nx + 16, ny), f32),
        full,
        full,
        full,
    ]
    if last:
        outs = (rows_shape, rows_shape)
        scratch = [full] + scratch + [pltpu.VMEM((2, rows_here + 16, ny), f32)]
    else:
        outs = (jax.ShapeDtypeStruct((2, nx, ny), bf16), rows_shape)
    return pl.pallas_call(
        partial(step_kernel, dims, pos, last),
        out_shape=outs,
        grid=(1,),
        in_specs=[sm, sm, vm, vm, vm, phase_spec(slot, nx, ny), vm, vm] + [vm] * (2 if last else 0),
        out_specs=(vm, vm),
        scratch_shapes=scratch,
        compiler_params=pltpu.CompilerParams(vmem_limit_bytes=vmem_bytes),
        cost_estimate=pl.CostEstimate(flops=2**31, bytes_accessed=2**23, transcendentals=0),
        name="end_step" if last else "depth_step",
    )(ints, omega, w, own, other, phases, qx, qy, *(ends or ()))


def swap(values, axis, mask):
    size = lax.axis_size(axis)
    return lax.ppermute(values, axis, [(i, i ^ mask) for i in range(size)])


def doubling_masks(size):
    masks = []
    mask = size // 2
    while mask:
        masks.append(mask)
        mask //= 2
    descending = masks
    ascending = masks[:1] + masks[1:][::-1]
    return descending, ascending


def doubling_orders(masks):
    orders = [[0]]
    seen = [0]
    for mask in masks:
        new = [mask ^ o for o in seen]
        orders.append(new)
        seen = seen + new
    return orders


def gathered_pair(pair, axis):
    size = lax.axis_size(axis)
    order_pair = doubling_masks(size)
    pieces = [[pair[0:1]], [pair[1:2]]]
    got = swap(pair, axis, order_pair[0][0])
    pieces[0].append(got[0:1])
    pieces[1].append(got[1:2])
    for level in range(1, len(order_pair[0])):
        for which in range(2):
            have = jnp.concatenate(pieces[which], 0)
            pieces[which].append(swap(have, axis, order_pair[which][level]))
    return pieces


def per_device(source_top, adjoint_bottom, slowness, correction, slowness_ref, omega):
    row_parts = lax.axis_size("rows")
    sections = lax.axis_size("depth")
    group = lax.axis_index("depth")
    part_id = lax.axis_index("rows")
    freq_count = omega.shape[0]
    chains = 2 * freq_count
    rep = sections // chains
    rows_here, ny = slowness.shape[1:]
    nx = rows_here * row_parts
    dims = (nx, ny, rows_here)
    hy = ny // 2
    chain = group // rep
    forward = chain // freq_count
    freq = chain % freq_count
    side = group % 2
    omega_here = lax.dynamic_slice_in_dim(omega, freq, 1, 0)
    masks = doubling_masks(row_parts)
    orders = [doubling_orders(m) for m in masks]
    flat = [sum(o, []) for o in orders]
    pos = [[f.index(o) for o in range(row_parts)] for f in flat]

    def pick(values, index):
        return lax.dynamic_index_in_dim(values, index, 0, keepdims=False)

    plane = jnp.where(forward == 1, pick(source_top, freq), pick(adjoint_bottom, freq))
    plane_pieces = gathered_pair(plane, "rows")

    own = jnp.concatenate([correction, slowness - slowness_ref[:, None, None]], 0).astype(bf16)
    by_mask = jnp.stack([own] + [swap(own, "depth", k) for k in range(1, sections)])
    refs = jnp.stack([slowness_ref] + [swap(slowness_ref, "depth", k) for k in range(1, sections)])

    def depth_at(slot):
        return jnp.where(forward == 1, slot, sections - 1 - slot)

    def slot_coefs(slot):
        mine = pick(by_mask, group ^ depth_at(slot))
        half = lax.dynamic_slice_in_dim(mine, side * hy, hy, 2)
        pieces = gathered_pair(half, "rows")
        every = jnp.concatenate(pieces[0] + pieces[1], 0)
        return every, swap(every, "depth", 1)

    levels = jnp.concatenate(
        [pick(refs, group ^ jnp.where(forward == 1, t, (sections - t) % sections)) for t in range(sections)]
    )
    sign = jnp.where(forward == 1, 1.0, -1.0).astype(f32)[None]
    phases = phase_table(nx, ny, levels * omega_here, sign)

    coef_rows = pick(by_mask, group ^ (sections - 1))
    rows_up = [(i, (i + 1) % row_parts) for i in range(row_parts)]
    rows_down = [(j, i) for i, j in rows_up]
    edges = jnp.stack(
        [
            lax.ppermute(coef_rows[:, rows_here - 1 :], "rows", rows_up),
            lax.ppermute(coef_rows[:, :1], "rows", rows_down),
        ]
    )

    ints = jnp.stack([part_id, forward, side]).astype(jnp.int32)
    qx, qy = basis_tables(nx), basis_tables(ny)
    w = run_first(dims, orders, ints, phases, qx, qy, plane_pieces[0] + plane_pieces[1])
    row_outs = []
    for slot in range(sections - 1):
        every, other = slot_coefs(slot)
        ends = (coef_rows, edges) if slot == sections - 2 else None
        first, second = run_step(
            dims, pos, slot + 1, ints, omega_here, w, every, other, phases, qx, qy, ends
        )
        if ends is None:
            w = first
            row_outs.append(second)
        else:
            row_outs += [first, second]

    half_sections = sections // 2

    def index_for(g, target):
        return target if g >= half_sections else sections - 2 - target

    def to_target(mask):
        used = sorted(
            {index_for(g, g ^ mask) for g in range(sections) if index_for(g, g ^ mask) >= 0}
        )
        low = used[0]
        stack = jnp.stack(row_outs[low : used[-1] + 1])
        target = group ^ mask
        index = jnp.where(forward == 1, target, sections - 2 - target)
        payload = pick(stack, jnp.clip(index - low, 0, len(stack) - 1))
        return payload if mask == 0 else swap(payload, "depth", mask)

    fields = [to_target(i * rep) for i in range(chains)]
    gradient = jnp.zeros((rows_here, ny), f32)
    for i in range(freq_count):
        freq_i = freq ^ i
        a = fields[i].astype(f32)
        adjoint = jnp.where(
            group == sections - 1, pick(adjoint_bottom, freq_i), fields[i + freq_count]
        )
        b = adjoint.astype(f32)
        weight = pick(omega, freq_i) * sign[0]
        gradient = gradient + weight * (a[0] * b[1] - a[1] * b[0])
    return gradient[None]


def solution(mesh):
    in_specs = (
        P(None, None, "rows", None),
        P(None, None, "rows", None),
        P("depth", "rows", None),
        P("depth", "rows", None),
        P("depth"),
        P(),
    )
    out_specs = P("depth", "rows", None)
    return jax.shard_map(
        per_device, mesh=mesh, in_specs=in_specs, out_specs=out_specs, check_vma=False
    )
```

time: 796 us -> 115 us (0.14)
  matrix products: 223 us -> 0 us
  waiting for transfers between devices: 248 us -> 35.7 us
  starting transfers between devices: 137 us -> 32.6 us
  local copies, waits for them, and re-layouts: 80.6 us -> 2.56 us
  other arithmetic: 77.5 us -> 11.4 us
  Pallas kernels: 0 us -> 29.9 us
  loops' own time: 23.9 us -> 0 us
    dot_general x384 -> x0, matrix products: 223 us -> none  [the longest x96 73.9 us: contract(): product(values[1], matrix[0])]
    ppermute x36 -> x34, waiting for transfers between devices: 149 us -> 35.7 us  [the longest x32 30 us: swap(): return lax.ppermute(values, axis, [(i, i ^ mask) for i in range(size)])]
    all_to_all x24 -> x0, starting transfers between devices: 103 us -> none  [the longest x6 36.1 us: one_tick(): lax.all_to_all(joined_bf16(spec_a), 'rows', split_axis=3, concat_axis=3,...]
    all_to_all x24 -> x0, waiting for transfers between devices: 98.9 us -> none  [the longest x6 36 us: one_tick(): lax.all_to_all(outgoing[1], 'rows', split_axis=3, concat_axis=3, tiled=True)]
    while x132 -> x0, local copies, waits for them, and re-layouts: 34.4 us -> none
    pallas_call x0 -> x5, Pallas kernels: none -> 29.9 us  [the longest x3 20.6 us: run_step(): pl.pallas_call(partial(step_kernel, dims, pos, last), out_shape=outs, gri...]
    another operation x18 -> x7, other arithmetic: 28.8 us -> 4.07 us  [the longest x1 2.02 us: per_device(): jnp.stack([slowness_ref] + [swap(slowness_ref, 'depth', k) for k in range...]
    another operation x1 -> x0, loops' own time: 23.9 us -> none  [per_device(): final_state = lax.fori_loop(0, tick_count, one_tick, initial)]
  transfers between devices with their start and end apart: 60 -> 34, of which waited for: 40 -> 17; matrix products, arithmetic and copies ran while one was open for 9% -> 11% of each run, Pallas kernels for 0% -> 20%
where the time goes in v1:
time: 115 us
  waiting for transfers between devices  35.7 us (31%)
  starting transfers between devices  32.6 us (28%)
  Pallas kernels  29.9 us (26%)
  other arithmetic  11.4 us (10%)
  local copies, waits for them, and re-layouts  2.56 us (2%)
  between operations  2.45 us (2%)
    ppermute x32, starting transfers between devices, swap(): return lax.ppermute(values, axis, [(i, i ^ mask) for i in range(size)])  31.8 us
    ppermute x32, waiting for transfers between devices, swap(): return lax.ppermute(values, axis, [(i, i ^ mask) for i in range(size)])  30 us
    pallas_call x3, Pallas kernels, run_step(): pl.pallas_call(partial(step_kernel, dims, pos, last), out_shape=outs, gri...  20.6 us
    pallas_call x1, Pallas kernels, phase_table(): pl.pallas_call(partial(phase_kernel, nx, ny), out_shape=jax.ShapeDtypeStr...  7.88 us
    ppermute x1, waiting for transfers between devices, per_device(): lax.ppermute(coef_rows[:, rows_here - 1:], 'rows', rows_up)  5.7 us
    mul x1, other arithmetic, per_device(): phases = phase_table(nx, ny, levels * omega_here, sign)  3.3 us
  transfers between devices with their start and end apart: 34, of which 17 were waited for; matrix products, arithmetic and copies ran while one was open for 11% of the time, Pallas kernels for 20%

profile of v1, /device:TPU:0, one launch (start us, length us, event | category | flops | bytes accessed | tf_op | source)
XLA Modules:
  0.0 114.5 jit_solution(18073356227432946600)
XLA Ops:
  0.0 2.4 %collective-permute-start.2 = (f32[1]{0:T(128)}, f32[1]{0:T(128)}, u32[]{:S(2)}, u32[]{:S(2)}) collective-permute-start(f32[1]{0:T(128)} %param.12), channel_id=1, source_target_pairs={{0,24},{8,16},{16,8},{24,0},{1,25},{9,17},{17,9},{25,1},{2,26},{10... | collective-permute-start | bytes 20 | tf_op jit(solution)/shard_map/ppermute | solution.py:360
  4.0 2.9 %collective-permute-start.3 = (bf16[2,64,512]{2,1,0:T(8,128)(2,1)S(1)}, bf16[2,64,512]{2,1,0:T(8,128)(2,1)S(1)}, u32[]{:S(2)}, u32[]{:S(2)}) collective-permute-start(bf16[2,64,512]{2,1,0:T(8,128)(2,1)S(1)} %bitcast_select_fusion.2), channel_id=1, source_target_pairs={{0,4},{1,5},{2,6},{3,7},{4,0},{5,1},{6,2},{7,3},{8,12},{9,13},{10,... | collective-permute-start | bytes 393224 | tf_op jit(solution)/shard_map/ppermute | solution.py:360
  14.8 2.0 %pad_maximum_fusion.20 = f32[4,1]{0,1:T(1,128)S(1)} fusion(f32[1,1]{0,1:T(1,128)} %bitcast.7, f32[1,1]{0,1:T(1,128)} %bitcast.6, f32[1,1]{0,1:T(1,128)} %bitcast.5, f32[1,1]{0,1:T(1,128)} %bitcast.79), kind=kLoop, calls=%fused_computation.86 | loop fusion | flops 12 | bytes 32 | tf_op jit(solution)/shard_map/stack | solution.py:428
  17.5 3.3 %maximum_multiply_fusion.ks_ref = f32[4]{0:T(128)S(1)} fusion(f32[1]{0:T(128)} %bitcast.11, f32[1]{0:T(128)} %bitcast.10, f32[1]{0:T(128)} %bitcast.9, f32[1]{0:T(128)} %bitcast.8, f32[]{:T(128)} %bitcast), kind=kLoop, calls=%fused_computation.87 | loop fusion | flops 16 | bytes 36 | tf_op jit(solution)/shard_map/mul | solution.py:444
  20.8 7.9 %phase_table.1.phase = bf16[4,2,512,512]{3,2,1,0:T(8,128)(2,1)S(1)} custom-call(f32[4]{0:T(128)S(1)} %maximum_multiply_fusion.ks_ref, f32[1]{0:T(128)} %bitcast.12.sign_ref), custom_call_target="tpu_custom_call" | custom-call | tf_op jit(solution)/shard_map/phase_table/pallas_call | solution.py:88
  28.7 1.6 %collective-permute-start.4 = (bf16[2,64,512]{2,1,0:T(8,128)(2,1)S(1)}, bf16[2,64,512]{2,1,0:T(8,128)(2,1)S(1)}, u32[]{:S(2)}, u32[]{:S(2)}) collective-permute-start(bf16[2,64,512]{2,1,0:T(8,128)(2,1)S(1)} %pad_maximum_fusion.4), channel_id=1, source_target_pairs={{0,2},{1,3},{2,0},{3,1},{4,6},{5,7},{6,4},{7,5},{8,10},{9,11},{10,... | collective-permute-start | bytes 393224 | tf_op jit(solution)/shard_map/ppermute | solution.py:360
  30.4 1.6 %collective-permute-start.6 = (bf16[2,64,512]{2,1,0:T(8,128)(2,1)S(1)}, bf16[2,64,512]{2,1,0:T(8,128)(2,1)S(1)}, u32[]{:S(2)}, u32[]{:S(2)}) collective-permute-start(bf16[2,64,512]{2,1,0:T(8,128)(2,1)S(1)} %pad_maximum_fusion.5), channel_id=1, source_target_pairs={{0,1},{1,0},{2,3},{3,2},{4,5},{5,4},{6,7},{7,6},{8,9},{9,8},{10,11... | collective-permute-start | bytes 393224 | tf_op jit(solution)/shard_map/ppermute | solution.py:360
  32.6 2.6 %collective-permute-start.17 = (bf16[2,64,256]{2,1,0:T(8,128)(2,1)S(1)}, bf16[2,64,256]{2,1,0:T(8,128)(2,1)S(1)}, u32[]{:S(2)}, u32[]{:S(2)}) collective-permute-start(bf16[2,64,256]{2,1,0:T(8,128)(2,1)S(1)} %get-tuple-element.34), channel_id=1, source_target_pairs={{0,4},{1,5},{2,6},{3,7},{4,0},{5,1},{6,2},{7,3},{8,12},{9,13},{10,... | collective-permute-start | bytes 196616 | tf_op jit(solution)/shard_map/ppermute | solution.py:360
  35.7 5.3 %collective-permute-done.23 = bf16[2,64,256]{2,1,0:T(8,128)(2,1)S(1)} collective-permute-done((bf16[2,64,256]{2,1,0:T(8,128)(2,1)S(1)}, bf16[2,64,256]{2,1,0:T(8,128)(2,1)S(1)}, u32[]{:S(2)}, u32[]{:S(2)}) %collective-permute-start.23) | collective-permute-done | bytes 65568 | tf_op jit(solution)/shard_map/ppermute | solution.py:360
  51.7 7.5 %collective-permute-done.25 = bf16[4,64,256]{2,1,0:T(8,128)(2,1)S(1)} collective-permute-done((bf16[4,64,256]{2,1,0:T(8,128)(2,1)S(1)}, bf16[4,64,256]{2,1,0:T(8,128)(2,1)S(1)}, u32[]{:S(2)}, u32[]{:S(2)}) %collective-permute-start.25) | collective-permute-done | bytes 131104 | tf_op jit(solution)/shard_map/ppermute | solution.py:360
  59.2 1.5 %collective-permute-done.19 = bf16[4,64,256]{2,1,0:T(8,128)(2,1)S(1)} collective-permute-done((bf16[4,64,256]{2,1,0:T(8,128)(2,1)S(1)}, bf16[4,64,256]{2,1,0:T(8,128)(2,1)S(1)}, u32[]{:S(2)}, u32[]{:S(2)}) %collective-permute-start.19) | collective-permute-done | bytes 131104 | tf_op jit(solution)/shard_map/ppermute | solution.py:360
  60.7 1.4 %collective-permute-done.13 = bf16[4,64,256]{2,1,0:T(8,128)(2,1)S(1)} collective-permute-done((bf16[4,64,256]{2,1,0:T(8,128)(2,1)S(1)}, bf16[4,64,256]{2,1,0:T(8,128)(2,1)S(1)}, u32[]{:S(2)}, u32[]{:S(2)}) %collective-permute-start.13) | collective-permute-done | bytes 131104 | tf_op jit(solution)/shard_map/ppermute | solution.py:360
  63.0 1.4 %collective-permute-start.20 = (bf16[2,64,256]{2,1,0:T(8,128)(2,1)S(1)}, bf16[2,64,256]{2,1,0:T(8,128)(2,1)S(1)}, u32[]{:S(2)}, u32[]{:S(2)}) collective-permute-start(bf16[2,64,256]{2,1,0:T(8,128)(2,1)S(1)} %pad_maximum_fusion.16), channel_id=1, source_target_pairs={{0,1},{1,0},{2,3},{3,2},{4,5},{5,4},{6,7},{7,6},{8,9},{9,8},{10,11... | collective-permute-start | bytes 196616 | tf_op jit(solution)/shard_map/ppermute | solution.py:360
  65.2 1.4 %collective-permute-done.14 = bf16[2,64,256]{2,1,0:T(8,128)(2,1)S(1)} collective-permute-done((bf16[2,64,256]{2,1,0:T(8,128)(2,1)S(1)}, bf16[2,64,256]{2,1,0:T(8,128)(2,1)S(1)}, u32[]{:S(2)}, u32[]{:S(2)}) %collective-permute-start.14) | collective-permute-done | bytes 65568 | tf_op jit(solution)/shard_map/ppermute | solution.py:360
  67.3 1.4 %collective-permute-start.21 = (bf16[4,64,256]{2,1,0:T(8,128)(2,1)S(1)}, bf16[4,64,256]{2,1,0:T(8,128)(2,1)S(1)}, u32[]{:S(2)}, u32[]{:S(2)}) collective-permute-start(bf16[4,64,256]{2,1,0:T(8,128)(2,1)S(1)} %pad_maximum_fusion.10), channel_id=1, source_target_pairs={{0,2},{1,3},{2,0},{3,1},{4,6},{5,7},{6,4},{7,5},{8,10},{9,11},{10,... | collective-permute-start | bytes 393224 | tf_op jit(solution)/shard_map/ppermute | solution.py:360
  69.5 2.1 %collective-permute-done.15 = bf16[4,64,256]{2,1,0:T(8,128)(2,1)S(1)} collective-permute-done((bf16[4,64,256]{2,1,0:T(8,128)(2,1)S(1)}, bf16[4,64,256]{2,1,0:T(8,128)(2,1)S(1)}, u32[]{:S(2)}, u32[]{:S(2)}) %collective-permute-start.15) | collective-permute-done | bytes 131104 | tf_op jit(solution)/shard_map/ppermute | solution.py:360
  74.5 5.7 %collective-permute-done.29 = bf16[2,1,512]{2,1,0:T(2,128)(2,1)S(1)} collective-permute-done((bf16[2,1,512]{2,1,0:T(2,128)(2,1)S(1)}, bf16[2,1,512]{2,1,0:T(2,128)(2,1)S(1)}, u32[]{:S(2)}, u32[]{:S(2)}) %collective-permute-start.29) | collective-permute-done | bytes 2080 | tf_op jit(solution)/shard_map/ppermute | solution.py:451
  80.5 1.4 %first_step.1.w_ref = bf16[2,512,512]{2,1,0:T(8,128)(2,1)S(1)} custom-call(s32[3]{0:T(128)S(1)} %pad_add_fusion.ints_ref, bf16[4,2,512,512]{3,2,1,0:T(8,128)(2,1)} %copy-done, bf16[4,256,256]{2,1,0:T(8,128)(2,1)S(1)} %copy-done.1, bf16[4,256,256]{2,1,0:T(8,128)(2,1)S(1)} %copy-done.1, bf16[1,64,512]{2,1,0:T(8,128)(2,1)S(1)} %get-tuple-element.51.rest_0_, ...), custom_call_target="tpu_custom_call" | custom-call | flops 1073741824 | bytes 4194304 | tf_op jit(solution)/shard_map/first_step/pallas_call | solution.py:313
  81.9 6.9 %depth_step.2 = (bf16[2,512,512]{2,1,0:T(8,128)(2,1)S(1)}, bf16[2,64,512]{2,1,0:T(8,128)(2,1)S(1)}) custom-call(s32[3]{0:T(128)S(1)} %pad_add_fusion.ints_ref, f32[1]{0:T(128)} %get-tuple-element.62.omega_ref, bf16[2,512,512]{2,1,0:T(8,128)(2,1)S(1)} %first_step.1.w_ref, bf16[16,64,256]{2,1,0:T(8,128)(2,1)S(1)} %constant_dynamic-update-slice_fusion.own_ref, ...), custom_call_target="tpu_custom_call" | custom-call | flops 2147483648 | bytes 8388608 | tf_op jit(solution)/shard_map/depth_step/pallas_call | solution.py:345
  88.8 6.7 %depth_step.3 = (bf16[2,512,512]{2,1,0:T(8,128)(2,1)S(1)}, bf16[2,64,512]{2,1,0:T(8,128)(2,1)S(1)}) custom-call(s32[3]{0:T(128)S(1)} %pad_add_fusion.ints_ref, f32[1]{0:T(128)} %get-tuple-element.62.omega_ref, bf16[2,512,512]{2,1,0:T(8,128)(2,1)S(1)} %get-tuple-element.11.w_ref, bf16[16,64,256]{2,1,0:T(8,128)(2,1)S(1)} %constant_dynamic-update-slice_fusion.8.own_ref, ...), custom_call_target="tpu_custom_call" | custom-call | flops 2147483648 | bytes 8388608 | tf_op jit(solution)/shard_map/depth_step/pallas_call | solution.py:345
  95.6 7.0 %end_step.1 = (bf16[2,64,512]{2,1,0:T(8,128)(2,1)S(1)}, bf16[2,64,512]{2,1,0:T(8,128)(2,1)S(1)}) custom-call(s32[3]{0:T(128)S(1)} %pad_add_fusion.ints_ref, f32[1]{0:T(128)} %get-tuple-element.62.omega_ref, bf16[2,512,512]{2,1,0:T(8,128)(2,1)S(1)} %get-tuple-element.13.w_ref, bf16[16,64,256]{2,1,0:T(8,128)(2,1)S(1)} %constant_dynamic-update-slice_fusion.16.own_ref, ...), custom_call_target="tpu_custom_call" | custom-call | flops 2147483648 | bytes 8388608 | tf_op jit(solution)/shard_map/end_step/pallas_call | solution.py:345
  103.1 4.3 %collective-permute-start.31 = (bf16[2,64,512]{2,1,0:T(8,128)(2,1)S(1)}, bf16[2,64,512]{2,1,0:T(8,128)(2,1)S(1)}, u32[]{:S(2)}, u32[]{:S(2)}) collective-permute-start(bf16[2,64,512]{2,1,0:T(8,128)(2,1)S(1)} %get-tuple-element.44), channel_id=1, source_target_pairs={{0,16},{8,24},{16,0},{24,8},{1,17},{9,25},{17,1},{25,9},{2,18},{10... | collective-permute-start | bytes 393224 | tf_op jit(solution)/shard_map/ppermute | solution.py:360
  108.7 3.0 %collective-permute-done.31 = bf16[2,64,512]{2,1,0:T(8,128)(2,1)S(1)} collective-permute-done((bf16[2,64,512]{2,1,0:T(8,128)(2,1)S(1)}, bf16[2,64,512]{2,1,0:T(8,128)(2,1)S(1)}, u32[]{:S(2)}, u32[]{:S(2)}) %collective-permute-start.31) | collective-permute-done | bytes 131104 | tf_op jit(solution)/shard_map/ppermute | solution.py:360
  111.7 2.0 %collective-permute-done.33 = bf16[2,64,512]{2,1,0:T(8,128)(2,1)S(1)} collective-permute-done((bf16[2,64,512]{2,1,0:T(8,128)(2,1)S(1)}, bf16[2,64,512]{2,1,0:T(8,128)(2,1)S(1)}, u32[]{:S(2)}, u32[]{:S(2)}) %collective-permute-start.33) | collective-permute-done | bytes 131104 | tf_op jit(solution)/shard_map/ppermute | solution.py:360
  (114 shorter events, 28.8 us)
Async XLA Ops:
  0.0 13.8 %collective-permute-start.2 = (f32[1]{0:T(128)}, f32[1]{0:T(128)}, u32[]{:S(2)}, u32[]{:S(2)}) collective-permute-start(f32[1]{0:T(128)} %param.12), channel_id=1, source_target_pairs={{0,24},{8,16},{16,8},{24,0},{1,25},{9,17},{17,9},{25,1},{2,26},{10... | collective-permute-start | bytes 20 | tf_op jit(solution)/shard_map/ppermute | solution.py:360
  2.4 12.1 %collective-permute-start.1 = (f32[1]{0:T(128)}, f32[1]{0:T(128)}, u32[]{:S(2)}, u32[]{:S(2)}) collective-permute-start(f32[1]{0:T(128)} %param.12), channel_id=1, source_target_pairs={{0,16},{8,24},{16,0},{24,8},{1,17},{9,25},{17,1},{25,9},{2,18},{10... | collective-permute-start | bytes 20 | tf_op jit(solution)/shard_map/ppermute | solution.py:360
  3.0 11.8 %collective-permute-start = (f32[1]{0:T(128)}, f32[1]{0:T(128)}, u32[]{:S(2)}, u32[]{:S(2)}) collective-permute-start(f32[1]{0:T(128)} %param.12), channel_id=1, source_target_pairs={{0,8},{8,0},{16,24},{24,16},{1,9},{9,1},{17,25},{25,17},{2,10},{10... | collective-permute-start | bytes 20 | tf_op jit(solution)/shard_map/ppermute | solution.py:360
  4.0 24.6 %collective-permute-start.3 = (bf16[2,64,512]{2,1,0:T(8,128)(2,1)S(1)}, bf16[2,64,512]{2,1,0:T(8,128)(2,1)S(1)}, u32[]{:S(2)}, u32[]{:S(2)}) collective-permute-start(bf16[2,64,512]{2,1,0:T(8,128)(2,1)S(1)} %bitcast_select_fusion.2), channel_id=1, source_target_pairs={{0,4},{1,5},{2,6},{3,7},{4,0},{5,1},{6,2},{7,3},{8,12},{9,13},{10,... | collective-permute-start | bytes 393224 | tf_op jit(solution)/shard_map/ppermute | solution.py:360
  9.5 22.5 %collective-permute-start.10 = (bf16[2,64,512]{2,1,0:T(8,128)(2,1)S(1)}, bf16[2,64,512]{2,1,0:T(8,128)(2,1)S(1)}, u32[]{:S(2)}, u32[]{:S(2)}) collective-permute-start(bf16[2,64,512]{2,1,0:T(8,128)(2,1)S(1)} %pad_maximum_fusion.6), channel_id=1, source_target_pairs={{0,24},{8,16},{16,8},{24,0},{1,25},{9,17},{17,9},{25,1},{2,26},{10... | collective-permute-start | bytes 393224 | tf_op jit(solution)/shard_map/ppermute | solution.py:360
  13.8 18.1 %collective-permute-start.9 = (bf16[2,64,512]{2,1,0:T(8,128)(2,1)S(1)}, bf16[2,64,512]{2,1,0:T(8,128)(2,1)S(1)}, u32[]{:S(2)}, u32[]{:S(2)}) collective-permute-start(bf16[2,64,512]{2,1,0:T(8,128)(2,1)S(1)} %pad_maximum_fusion.6), channel_id=1, source_target_pairs={{0,16},{8,24},{16,0},{24,8},{1,17},{9,25},{17,1},{25,9},{2,18},{10... | collective-permute-start | bytes 393224 | tf_op jit(solution)/shard_map/ppermute | solution.py:360
  14.5 17.5 %collective-permute-start.8 = (bf16[2,64,512]{2,1,0:T(8,128)(2,1)S(1)}, bf16[2,64,512]{2,1,0:T(8,128)(2,1)S(1)}, u32[]{:S(2)}, u32[]{:S(2)}) collective-permute-start(bf16[2,64,512]{2,1,0:T(8,128)(2,1)S(1)} %pad_maximum_fusion.6), channel_id=1, source_target_pairs={{0,8},{8,0},{16,24},{24,16},{1,9},{9,1},{17,25},{25,17},{2,10},{10... | collective-permute-start | bytes 393224 | tf_op jit(solution)/shard_map/ppermute | solution.py:360
  28.7 15.8 %collective-permute-start.4 = (bf16[2,64,512]{2,1,0:T(8,128)(2,1)S(1)}, bf16[2,64,512]{2,1,0:T(8,128)(2,1)S(1)}, u32[]{:S(2)}, u32[]{:S(2)}) collective-permute-start(bf16[2,64,512]{2,1,0:T(8,128)(2,1)S(1)} %pad_maximum_fusion.4), channel_id=1, source_target_pairs={{0,2},{1,3},{2,0},{3,1},{4,6},{5,7},{6,4},{7,5},{8,10},{9,11},{10,... | collective-permute-start | bytes 393224 | tf_op jit(solution)/shard_map/ppermute | solution.py:360
  30.4 20.5 %collective-permute-start.6 = (bf16[2,64,512]{2,1,0:T(8,128)(2,1)S(1)}, bf16[2,64,512]{2,1,0:T(8,128)(2,1)S(1)}, u32[]{:S(2)}, u32[]{:S(2)}) collective-permute-start(bf16[2,64,512]{2,1,0:T(8,128)(2,1)S(1)} %pad_maximum_fusion.5), channel_id=1, source_target_pairs={{0,1},{1,0},{2,3},{3,2},{4,5},{5,4},{6,7},{7,6},{8,9},{9,8},{10,11... | collective-permute-start | bytes 393224 | tf_op jit(solution)/shard_map/ppermute | solution.py:360
  32.2 8.8 %collective-permute-start.23 = (bf16[2,64,256]{2,1,0:T(8,128)(2,1)S(1)}, bf16[2,64,256]{2,1,0:T(8,128)(2,1)S(1)}, u32[]{:S(2)}, u32[]{:S(2)}) collective-permute-start(bf16[2,64,256]{2,1,0:T(8,128)(2,1)S(1)} %get-tuple-element.33), channel_id=1, source_target_pairs={{0,4},{1,5},{2,6},{3,7},{4,0},{5,1},{6,2},{7,3},{8,12},{9,13},{10,... | collective-permute-start | bytes 196616 | tf_op jit(solution)/shard_map/ppermute | solution.py:360
  32.6 9.8 %collective-permute-start.17 = (bf16[2,64,256]{2,1,0:T(8,128)(2,1)S(1)}, bf16[2,64,256]{2,1,0:T(8,128)(2,1)S(1)}, u32[]{:S(2)}, u32[]{:S(2)}) collective-permute-start(bf16[2,64,256]{2,1,0:T(8,128)(2,1)S(1)} %get-tuple-element.34), channel_id=1, source_target_pairs={{0,4},{1,5},{2,6},{3,7},{4,0},{5,1},{6,2},{7,3},{8,12},{9,13},{10,... | collective-permute-start | bytes 196616 | tf_op jit(solution)/shard_map/ppermute | solution.py:360
  35.2 8.6 %collective-permute-start.11 = (bf16[2,64,256]{2,1,0:T(8,128)(2,1)S(1)}, bf16[2,64,256]{2,1,0:T(8,128)(2,1)S(1)}, u32[]{:S(2)}, u32[]{:S(2)}) collective-permute-start(bf16[2,64,256]{2,1,0:T(8,128)(2,1)S(1)} %get-tuple-element.35), channel_id=1, source_target_pairs={{0,4},{1,5},{2,6},{3,7},{4,0},{5,1},{6,2},{7,3},{8,12},{9,13},{10,... | collective-permute-start | bytes 196616 | tf_op jit(solution)/shard_map/ppermute | solution.py:360
  41.0 32.7 %collective-permute-start.30 = (bf16[2,1,512]{2,1,0:T(2,128)(2,1)S(1)}, bf16[2,1,512]{2,1,0:T(2,128)(2,1)S(1)}, u32[]{:S(2)}, u32[]{:S(2)}) collective-permute-start(bf16[2,1,512]{2,1,0:T(2,128)(2,1)S(1)} %get-tuple-element.47), channel_id=1, source_target_pairs={{1,0},{2,1},{3,2},{4,3},{5,4},{6,5},{7,6},{0,7},{9,8},{10,9},{11,1... | collective-permute-start | bytes 6152 | tf_op jit(solution)/shard_map/ppermute | solution.py:452
  47.1 33.1 %collective-permute-start.5 = (bf16[4,64,512]{2,1,0:T(8,128)(2,1)S(1)}, bf16[4,64,512]{2,1,0:T(8,128)(2,1)S(1)}, u32[]{:S(2)}, u32[]{:S(2)}) collective-permute-start(bf16[4,64,512]{2,1,0:T(8,128)(2,1)S(1)} %pad_maximum_fusion.2), channel_id=1, source_target_pairs={{0,1},{1,0},{2,3},{3,2},{4,5},{5,4},{6,7},{7,6},{8,9},{9,8},{10,11... | collective-permute-start | bytes 786440 | tf_op jit(solution)/shard_map/ppermute | solution.py:360
  48.7 10.4 %collective-permute-start.25 = (bf16[4,64,256]{2,1,0:T(8,128)(2,1)S(1)}, bf16[4,64,256]{2,1,0:T(8,128)(2,1)S(1)}, u32[]{:S(2)}, u32[]{:S(2)}) collective-permute-start(bf16[4,64,256]{2,1,0:T(8,128)(2,1)S(1)} %pad_maximum_fusion.11), channel_id=1, source_target_pairs={{0,1},{1,0},{2,3},{3,2},{4,5},{5,4},{6,7},{7,6},{8,9},{9,8},{10,11... | collective-permute-start | bytes 393224 | tf_op jit(solution)/shard_map/ppermute | solution.py:360
  49.5 11.2 %collective-permute-start.19 = (bf16[4,64,256]{2,1,0:T(8,128)(2,1)S(1)}, bf16[4,64,256]{2,1,0:T(8,128)(2,1)S(1)}, u32[]{:S(2)}, u32[]{:S(2)}) collective-permute-start(bf16[4,64,256]{2,1,0:T(8,128)(2,1)S(1)} %pad_maximum_fusion.9), channel_id=1, source_target_pairs={{0,1},{1,0},{2,3},{3,2},{4,5},{5,4},{6,7},{7,6},{8,9},{9,8},{10,11... | collective-permute-start | bytes 393224 | tf_op jit(solution)/shard_map/ppermute | solution.py:360
  50.9 11.2 %collective-permute-start.13 = (bf16[4,64,256]{2,1,0:T(8,128)(2,1)S(1)}, bf16[4,64,256]{2,1,0:T(8,128)(2,1)S(1)}, u32[]{:S(2)}, u32[]{:S(2)}) collective-permute-start(bf16[4,64,256]{2,1,0:T(8,128)(2,1)S(1)} %pad_maximum_fusion.7), channel_id=1, source_target_pairs={{0,1},{1,0},{2,3},{3,2},{4,5},{5,4},{6,7},{7,6},{8,9},{9,8},{10,11... | collective-permute-start | bytes 393224 | tf_op jit(solution)/shard_map/ppermute | solution.py:360
  71.6 10.3 %collective-permute-start.16 = (bf16[16,64,256]{2,1,0:T(8,128)(2,1)S(1)}, bf16[16,64,256]{2,1,0:T(8,128)(2,1)S(1)}, u32[]{:S(2)}, u32[]{:S(2)}) collective-permute-start(bf16[16,64,256]{2,1,0:T(8,128)(2,1)S(1)} %constant_dynamic-update-slice_fusion.own_ref), channel_id=1, source_target_pairs={{0,8},{8,0},{16,24},{24,16},{1,9},{9,1},{17,25},{25,17},{2,10},{10... | collective-permute-start | bytes 1572872 | tf_op jit(solution)/shard_map/ppermute | solution.py:360
  73.0 7.5 %collective-permute-start.7 = (bf16[4,64,512]{2,1,0:T(8,128)(2,1)S(1)}, bf16[4,64,512]{2,1,0:T(8,128)(2,1)S(1)}, u32[]{:S(2)}, u32[]{:S(2)}) collective-permute-start(bf16[4,64,512]{2,1,0:T(8,128)(2,1)S(1)} %pad_maximum_fusion.3), channel_id=1, source_target_pairs={{0,2},{1,3},{2,0},{3,1},{4,6},{5,7},{6,4},{7,5},{8,10},{9,11},{10,... | collective-permute-start | bytes 786440 | tf_op jit(solution)/shard_map/ppermute | solution.py:360
  73.8 6.5 %collective-permute-start.29 = (bf16[2,1,512]{2,1,0:T(2,128)(2,1)S(1)}, bf16[2,1,512]{2,1,0:T(2,128)(2,1)S(1)}, u32[]{:S(2)}, u32[]{:S(2)}) collective-permute-start(bf16[2,1,512]{2,1,0:T(2,128)(2,1)S(1)} %get-tuple-element.46), channel_id=1, source_target_pairs={{0,1},{1,2},{2,3},{3,4},{4,5},{5,6},{6,7},{7,0},{8,9},{9,10},{10,1... | collective-permute-start | bytes 6152 | tf_op jit(solution)/shard_map/ppermute | solution.py:451
  74.5 14.3 %collective-permute-start.22 = (bf16[16,64,256]{2,1,0:T(8,128)(2,1)S(1)}, bf16[16,64,256]{2,1,0:T(8,128)(2,1)S(1)}, u32[]{:S(2)}, u32[]{:S(2)}) collective-permute-start(bf16[16,64,256]{2,1,0:T(8,128)(2,1)S(1)} %constant_dynamic-update-slice_fusion.8.own_ref), channel_id=1, source_target_pairs={{0,8},{8,0},{16,24},{24,16},{1,9},{9,1},{17,25},{25,17},{2,10},{10... | collective-permute-start | bytes 1572872 | tf_op jit(solution)/shard_map/ppermute | solution.py:360
  80.2 15.3 %collective-permute-start.28 = (bf16[16,64,256]{2,1,0:T(8,128)(2,1)S(1)}, bf16[16,64,256]{2,1,0:T(8,128)(2,1)S(1)}, u32[]{:S(2)}, u32[]{:S(2)}) collective-permute-start(bf16[16,64,256]{2,1,0:T(8,128)(2,1)S(1)} %constant_dynamic-update-slice_fusion.16.own_ref), channel_id=1, source_target_pairs={{0,8},{8,0},{16,24},{24,16},{1,9},{9,1},{17,25},{25,17},{2,10},{10... | collective-permute-start | bytes 1572872 | tf_op jit(solution)/shard_map/ppermute | solution.py:360
  103.1 8.6 %collective-permute-start.31 = (bf16[2,64,512]{2,1,0:T(8,128)(2,1)S(1)}, bf16[2,64,512]{2,1,0:T(8,128)(2,1)S(1)}, u32[]{:S(2)}, u32[]{:S(2)}) collective-permute-start(bf16[2,64,512]{2,1,0:T(8,128)(2,1)S(1)} %get-tuple-element.44), channel_id=1, source_target_pairs={{0,16},{8,24},{16,0},{24,8},{1,17},{9,25},{17,1},{25,9},{2,18},{10... | collective-permute-start | bytes 393224 | tf_op jit(solution)/shard_map/ppermute | solution.py:360
  107.4 6.3 %collective-permute-start.33 = (bf16[2,64,512]{2,1,0:T(8,128)(2,1)S(1)}, bf16[2,64,512]{2,1,0:T(8,128)(2,1)S(1)}, u32[]{:S(2)}, u32[]{:S(2)}) collective-permute-start(bf16[2,64,512]{2,1,0:T(8,128)(2,1)S(1)} %get-tuple-element.45), channel_id=1, source_target_pairs={{0,24},{8,16},{16,8},{24,0},{1,25},{9,17},{17,9},{25,1},{2,26},{10... | collective-permute-start | bytes 393224 | tf_op jit(solution)/shard_map/ppermute | solution.py:360
  (13 other events, 156.9 us)

commit v2 on v1

v2 whole, which is shorter than its diff:
```python
from functools import partial
import math

import jax
import jax.numpy as jnp
import numpy as np
from jax import lax
from jax.experimental import pallas as pl
from jax.experimental.pallas import tpu as pltpu
from jax.sharding import PartitionSpec as P

bf16 = jnp.bfloat16
f32 = jnp.float32
vmem_bytes = 20 * 1024 * 1024


def basis(length):
    half, quarter = length // 2, length // 4
    n = np.arange(half)[:, None]
    j = np.arange(quarter)[None, :]
    scale = math.sqrt(2.0 / length)
    even_cos = scale * np.cos(2 * np.pi * ((2 * j * n) % length) / length)
    even_sin = scale * np.sin(2 * np.pi * ((2 * j * n) % length) / length)
    even_cos[:, 0] = 1.0 / math.sqrt(length)
    even_sin[:, 0] = (1.0 - 2.0 * (np.arange(half) % 2)) / math.sqrt(length)
    odd_cos = scale * np.cos(2 * np.pi * (((2 * j + 1) * n) % length) / length)
    odd_sin = scale * np.sin(2 * np.pi * (((2 * j + 1) * n) % length) / length)
    even = np.concatenate([even_cos, even_sin], 1).astype(np.float32)
    odd = np.concatenate([odd_cos, odd_sin], 1).astype(np.float32)
    return even, odd


def basis_tables(length):
    even, odd = basis(length)
    return jnp.asarray(np.stack([even, odd, even.T, odd.T]), bf16)


def dot(a, b):
    return jnp.dot(a, b, preferred_element_type=f32)


def fitted(function, top, degree):
    fit = np.polynomial.Chebyshev.interpolate(function, degree, [0.0, top])
    return [float(c) for c in fit.convert(kind=np.polynomial.Polynomial).coef]


def horner(coefs, x):
    total = coefs[-1] * x + coefs[-2]
    for c in coefs[-3::-1]:
        total = total * x + c
    return total


def sinc_root(x):
    return np.sinc(np.sqrt(x) / np.pi)


def cos_root(x):
    return np.cos(np.sqrt(x))


lens_top = 0.45
lens_cos, lens_sin = fitted(cos_root, lens_top, 3), fitted(sinc_root, lens_top, 3)
phase_top = 3.2
phase_cos, phase_sin = fitted(cos_root, phase_top, 7), fitted(sinc_root, phase_top, 7)


def small_cos_sin(a):
    s = a * a
    return horner(lens_cos, s), a * horner(lens_sin, s)


def phase_kernel(nx, ny, ints_ref, omega_ref, refs_ref, out_ref):
    qx, qy = nx // 4, ny // 4
    sign = (2 * ints_ref[1] - 1).astype(f32)
    level = omega_ref[ints_ref[3]] * refs_ref[0, 0:1, 0:1]

    def waves(rows, cols, axis, parity, length):
        j = lax.broadcasted_iota(jnp.int32, (rows, cols), axis)
        return (2 * j + parity).astype(f32) * (2.0 * math.pi / length)

    def values(kx, ky):
        squared = level * level - kx * kx - ky * ky
        inside = jnp.maximum(squared, 0.0)
        damping = jnp.exp(-jnp.sqrt(jnp.maximum(-squared, 0.0)))
        sine = jnp.sqrt(inside) * horner(phase_sin, inside)
        return damping * horner(phase_cos, inside), sign * damping * sine

    edge = math.pi
    row_zero = lax.broadcasted_iota(jnp.int32, (qx, qy), 0) == 0
    col_zero = lax.broadcasted_iota(jnp.int32, (qx, qy), 1) == 0
    for px in range(2):
        for py in range(2):
            kx = waves(qx, qy, 0, px, nx)
            ky = waves(qx, qy, 1, py, ny)
            base = values(kx, ky)
            across = values(jnp.full((8, qy), edge), waves(8, qy, 1, py, ny))
            along = values(waves(qx, 1, 0, px, nx), jnp.full((qx, 1), edge))
            corner = values(jnp.full((8, 1), edge), jnp.full((8, 1), edge))
            for sx in range(2):
                for sy in range(2):
                    new_row, new_col = sx and not px, sy and not py
                    for part in range(2):
                        v = base[part]
                        if new_col:
                            v = jnp.where(col_zero, along[part], v)
                        if new_row:
                            v = jnp.where(row_zero, across[part][0:1], v)
                        if new_row and new_col:
                            v = jnp.where(row_zero & col_zero, corner[part][0:1], v)
                        rows = pl.ds((2 * px + sx) * qx, qx)
                        cols = pl.ds((2 * py + sy) * qy, qy)
                        out_ref[0, part, rows, cols] = v.astype(bf16)


def phase_table(nx, ny, ints, omega, refs):
    slots = refs.shape[0]
    return pl.pallas_call(
        partial(phase_kernel, nx, ny),
        out_shape=jax.ShapeDtypeStruct((slots, 2, nx, ny), bf16),
        grid=(slots,),
        in_specs=[
            pl.BlockSpec(memory_space=pltpu.SMEM),
            pl.BlockSpec(memory_space=pltpu.SMEM),
            pl.BlockSpec((1, 8, 128), lambda i: (i, 0, 0)),
        ],
        out_specs=pl.BlockSpec((1, 2, nx, ny), lambda i: (i, 0, 0, 0)),
        compiler_params=pltpu.CompilerParams(vmem_limit_bytes=vmem_bytes),
        name="phase_table",
    )(ints, omega, refs)


def pack_kernel(
    rows_here, hy, ints_ref, ref_ref, source, adjoint, slow_ref, coef_ref, plane, packed, same, other, slow, coef, sems
):
    forward, side, freq = ints_ref[1], ints_ref[2], ints_ref[3]
    slow_copy = pltpu.make_async_copy(slow_ref, slow, sems.at[0])
    coef_copy = pltpu.make_async_copy(coef_ref, coef, sems.at[1])

    @pl.when(forward == 1)
    def _():
        pltpu.make_async_copy(source.at[freq], plane, sems.at[2]).start()

    @pl.when(forward == 0)
    def _():
        pltpu.make_async_copy(adjoint.at[freq], plane, sems.at[2]).start()

    slow_copy.start()
    coef_copy.start()
    slow_copy.wait()
    coef_copy.wait()
    level = jnp.full((16, hy), ref_ref[0], f32)
    high = level.astype(bf16)
    rest = level - high.astype(f32)
    middle = rest.astype(bf16)
    low = (rest - middle.astype(f32)).astype(bf16)
    row = lax.broadcasted_iota(jnp.int32, (16, hy), 0)
    parts = jnp.where(row == 0, high.astype(f32), jnp.where(row == 1, middle.astype(f32), low.astype(f32)))
    parts = parts.astype(bf16)
    for i, alone in enumerate((same, other)):
        cols = pl.ds(pl.multiple_of((side ^ i) * hy, hy), hy)
        c = coef[0, :, cols].astype(bf16)
        d = (slow[0, :, cols] - ref_ref[0]).astype(bf16)
        for out in (packed.at[i], alone):
            out[pl.ds(0, rows_here), :] = c
            out[pl.ds(rows_here, rows_here), :] = d
            out[pl.ds(2 * rows_here, 16), :] = parts
    pltpu.make_async_copy(source.at[freq], plane, sems.at[2]).wait()


def run_pack(ints, slowness_ref, source_top, adjoint_bottom, slowness, correction):
    rows_here, ny = slowness.shape[1:]
    hy = ny // 2
    half = jax.ShapeDtypeStruct((2 * rows_here + 16, hy), bf16)
    return pl.pallas_call(
        partial(pack_kernel, rows_here, hy),
        out_shape=(
            jax.ShapeDtypeStruct((2, rows_here, ny), bf16),
            jax.ShapeDtypeStruct((2,) + half.shape, bf16),
            half,
            half,
        ),
        in_specs=[sm, sm] + [pl.BlockSpec(memory_space=pl.ANY)] * 4,
        out_specs=(vm, vm, vm, vm),
        scratch_shapes=[
            pltpu.VMEM((1, rows_here, ny), f32),
            pltpu.VMEM((1, rows_here, ny), f32),
            pltpu.SemaphoreType.DMA((3,)),
        ],
        compiler_params=pltpu.CompilerParams(vmem_limit_bytes=60 * 1024 * 1024),
        name="pack_rows",
    )(ints, slowness_ref, source_top, adjoint_bottom, slowness, correction)


def sort_kernel(rows_here, hy, sections, ints_ref, *refs):
    blocks, (early, late, refs_out, coef_rows, ends) = refs[:sections], refs[sections:]
    forward, side, group = ints_ref[1], ints_ref[2], ints_ref[4]
    half_sections = sections // 2

    def block_of(k):
        return blocks[k].at[k % 2] if k < half_sections else blocks[k]

    def chosen(index, body):
        for k in range(sections):
            pl.when(index == k)(partial(body, k))

    for slot in range(sections - 1):
        depth = jnp.where(forward == 1, slot, sections - 1 - slot)

        def place(k, slot=slot):
            block = block_of(k)
            for j in range(2):
                out = early.at[j, 0] if slot == 0 else late.at[j, slot - 1]
                out[...] = block[pl.ds(j * rows_here, rows_here), :]

        chosen(group ^ depth, place)
    for slot in range(sections):
        depth = jnp.where(forward == 1, slot, (sections - slot) % sections)

        def level(k, slot=slot):
            parts = block_of(k)[pl.ds(2 * rows_here, 16), pl.ds(0, 128)].astype(f32)
            refs_out[slot] = jnp.broadcast_to(parts[0:1] + parts[1:2] + parts[2:3], (8, 128))

        chosen(group ^ depth, level)

    for k in range(half_sections):

        @pl.when(jnp.clip(group ^ (sections - 1), 0, half_sections - 1) == k)
        def _(k=k):
            for i in range(2):
                cols = pl.ds(pl.multiple_of((side ^ (k % 2) ^ i) * hy, hy), hy)
                block = blocks[k].at[i]
                for j in range(2):
                    part = block[pl.ds(j * rows_here, rows_here), :]
                    coef_rows[j, :, cols] = part
                    ends[0, j, :, cols] = part[rows_here - 1 :]
                    ends[1, j, :, cols] = part[:1]


def run_sort(ints, blocks, rows_here, hy):
    sections = len(blocks)
    return pl.pallas_call(
        partial(sort_kernel, rows_here, hy, sections),
        out_shape=(
            jax.ShapeDtypeStruct((2, 1, rows_here, hy), bf16),
            jax.ShapeDtypeStruct((2, sections - 2, rows_here, hy), bf16),
            jax.ShapeDtypeStruct((sections, 8, 128), f32),
            jax.ShapeDtypeStruct((2, rows_here, 2 * hy), bf16),
            jax.ShapeDtypeStruct((2, 2, 1, 2 * hy), bf16),
        ),
        in_specs=[sm] + [vm] * sections,
        out_specs=(vm, vm, vm, vm, vm),
        compiler_params=pltpu.CompilerParams(vmem_limit_bytes=vmem_bytes),
        name="sort_depths",
    )(ints, *blocks)


vm = pl.BlockSpec(memory_space=pltpu.VMEM)
sm = pl.BlockSpec(memory_space=pltpu.SMEM)


def fold_cols(values):
    half = values.shape[1] // 2
    a, b = values[:, :half], values[:, half:]
    return (a + b).astype(bf16), (a - b).astype(bf16)


def transform(nx, ny, folded, phase, qx_ref, qy_ref, mid, spec, out):
    hx, hy = nx // 2, ny // 2
    step = min(128, hx)
    for part in range(2):
        for start in range(0, hx, step):
            top, low = pl.ds(start, step), pl.ds(hx + start, step)
            for par in range(2):
                cols = pl.ds(par * hy, hy)
                a = dot(folded[part, top, cols], qy_ref[par])
                b = dot(folded[part, low, cols], qy_ref[par])
                mid[part, top, cols] = (a + b).astype(bf16)
                mid[part, low, cols] = (a - b).astype(bf16)
    for start in range(0, ny, hy):
        cols = pl.ds(start, hy)
        back = []
        for par in range(2):
            rows = pl.ds(par * hx, hx)
            zr = dot(qx_ref[2 + par], mid[0, rows, cols])
            zi = dot(qx_ref[2 + par], mid[1, rows, cols])
            pr = phase[0, 0, rows, cols].astype(f32)
            pi = phase[0, 1, rows, cols].astype(f32)
            yr = (zr * pr - zi * pi).astype(bf16)
            yi = (zr * pi + zi * pr).astype(bf16)
            back.append((dot(qx_ref[par], yr), dot(qx_ref[par], yi)))
        for part in range(2):
            a, b = back[0][part], back[1][part]
            spec[part, pl.ds(0, hx), cols] = (a + b).astype(bf16)
            spec[part, pl.ds(hx, hx), cols] = (a - b).astype(bf16)
    for part in range(2):
        for start in range(0, nx, 2 * step):
            rows = pl.ds(start, 2 * step)
            a = dot(spec[part, rows, pl.ds(0, hy)], qy_ref[2])
            b = dot(spec[part, rows, pl.ds(hy, hy)], qy_ref[3])
            out[part, rows, pl.ds(0, hy)] = (a + b).astype(bf16)
            out[part, rows, pl.ds(hy, hy)] = (a - b).astype(bf16)


def first_kernel(dims, orders, ints_ref, phase, qx_ref, qy_ref, *rest):
    nx, ny, rows_here = dims
    counts = [len(o) for o in orders]
    pieces, (out, folded, mid, spec) = rest[: sum(counts)], rest[sum(counts) :]
    part_id, forward = ints_ref[0], ints_ref[1]
    at = 0
    for part, order in enumerate(orders):
        for piece_order in order:
            piece = pieces[at]
            at += 1
            for i, offset in enumerate(piece_order):
                block = part_id ^ offset
                rows = pl.ds(pl.multiple_of(block * rows_here, rows_here), rows_here)
                values = piece[i]

                @pl.when(forward == 1)
                def _():
                    a, b = fold_cols(values.astype(f32))
                    folded[part, rows, pl.ds(0, ny // 2)] = a
                    folded[part, rows, pl.ds(ny // 2, ny // 2)] = b

                @pl.when(forward == 0)
                def _():
                    out[part, rows, :] = values

    @pl.when(forward == 1)
    def _():
        transform(nx, ny, folded, phase, qx_ref, qy_ref, mid, spec, out)


def laplace_rows(ref, part, start, count):
    center = ref[part, pl.ds(start + 8, count), :]
    width = center.shape[1]
    return (
        ref[part, pl.ds(start + 7, count), :]
        + ref[part, pl.ds(start + 9, count), :]
        + pltpu.roll(center, 1, 1)
        + pltpu.roll(center, width - 1, 1)
        - 4.0 * center
    )


def wrap_rows(ref, nx):
    for part in range(2):
        ref[part, pl.ds(7, 1), :] = ref[part, pl.ds(nx + 7, 1), :]
        ref[part, pl.ds(nx + 8, 1), :] = ref[part, pl.ds(8, 1), :]


def step_kernel(dims, orders, slot, last, ints_ref, omega_ref, w_ref, phase, qx_ref, qy_ref, *rest):
    nx, ny, rows_here = dims
    count = sum(len(o) for o in orders)
    coefs, rest = (rest[:count], rest[count : 2 * count]), rest[2 * count :]
    if last:
        coef_rows, before_row, after_row, out_rows, end_rows, out, plane, halo, folded, mid, spec, tall = rest
    else:
        out, out_rows, plane, halo, folded, mid, spec = rest
    part_id, forward, side = ints_ref[0], ints_ref[1], ints_ref[2]
    omega = omega_ref[ints_ref[3]]
    hy = ny // 2
    blocks = nx // rows_here
    place = []
    at = 0
    for order in orders:
        where = {}
        for piece_order in order:
            for i, offset in enumerate(piece_order):
                where[offset] = (at, i)
            at += 1
        place.append(where)
    step = min(32, rows_here)

    def portions():
        for offset in range(blocks):
            for sub in range(0, rows_here, step):
                start = pl.multiple_of((part_id ^ offset) * rows_here + sub, step)
                yield offset, sub, start

    def lens_at(q, offset, sub):
        cols = pl.ds(pl.multiple_of((side ^ q) * hy, hy), hy)
        (ca, ci), (da, di) = place[0][offset], place[1][offset]
        rows = pl.ds(sub, step)
        c = coefs[q][ca][ci, slot, rows, :].astype(f32)
        cos, sin = small_cos_sin(omega * coefs[q][da][di, slot, rows, :].astype(f32))
        return cols, c, cos, sin

    chunk = 32

    @pl.when(forward == 1)
    def _():
        for offset, sub, start in portions():
            rows, shifted = pl.ds(start, step), pl.ds(start + 8, step)
            for q in range(2):
                cols, c, lr, li = lens_at(q, offset, sub)
                wr, wi = w_ref[0, rows, cols].astype(f32), w_ref[1, rows, cols].astype(f32)
                ur, ui = wr * lr - wi * li, wr * li + wi * lr
                plane[0, rows, cols] = ur
                plane[1, rows, cols] = ui
                halo[0, shifted, cols] = c * ur
                halo[1, shifted, cols] = c * ui
        wrap_rows(halo, nx)
        for start in range(0, nx, chunk):
            rows = pl.ds(start, chunk)
            ur = plane[0, rows, :] - laplace_rows(halo, 1, start, chunk)
            ui = plane[1, rows, :] + laplace_rows(halo, 0, start, chunk)
            for part, u in enumerate((ur, ui)):
                mid[part, rows, :] = u.astype(bf16)
                a, b = fold_cols(u)
                folded[part, rows, pl.ds(0, hy)] = a
                folded[part, rows, pl.ds(hy, hy)] = b
        mine = pl.ds(pl.multiple_of(part_id * rows_here, rows_here), rows_here)
        for part in range(2):
            out_rows[part] = mid[part, mine, :]

    @pl.when(forward == 0)
    def _():
        for part in range(2):
            halo[part, pl.ds(8, nx), :] = w_ref[part].astype(f32)
        wrap_rows(halo, nx)
        for start in range(0, nx, chunk):
            for part in range(2):
                plane[part, pl.ds(start, chunk), :] = laplace_rows(halo, part, start, chunk)
        flip = (1 - 2 * side).astype(f32)
        for offset, sub, start in portions():
            rows = pl.ds(start, step)
            shifted = pl.ds(start + 8, step)
            halves = []
            for q in range(2):
                cols, c, lr, li = lens_at(q, offset, sub)
                tr = halo[0, shifted, cols] + c * plane[1, rows, cols]
                ti = halo[1, shifted, cols] - c * plane[0, rows, cols]
                halves.append((tr * lr + ti * li, ti * lr - tr * li))
            for part in range(2):
                a, b = halves[0][part], halves[1][part]
                folded[part, rows, pl.ds(0, hy)] = (a + b).astype(bf16)
                folded[part, rows, pl.ds(hy, hy)] = (flip * (a - b)).astype(bf16)

    transform(nx, ny, folded, phase, qx_ref, qy_ref, mid, spec, out)
    first = pl.multiple_of(part_id * rows_here, rows_here)
    mine = pl.ds(first, rows_here)

    @pl.when(forward == 0)
    def _():
        for part in range(2):
            out_rows[part] = out[part, mine, :]

    if not last:
        return

    @pl.when(forward == 0)
    def _():
        end_rows[...] = jnp.zeros_like(end_rows)

    @pl.when(forward == 1)
    def _():
        before = pl.ds(pl.multiple_of(lax.rem(first + nx - 16, nx), 16), 16)
        after = pl.ds(pl.multiple_of(lax.rem(first + rows_here, nx), 16), 16)

        def scaled(values, c, d):
            lr, li = small_cos_sin(omega * d.astype(f32))
            wr, wi = values[0].astype(f32), values[1].astype(f32)
            ur, ui = wr * lr - wi * li, wr * li + wi * lr
            cf = c.astype(f32)
            return ur, ui, cf * ur, cf * ui

        ur, ui, gr, gi = scaled(
            (out[0, mine, :], out[1, mine, :]), coef_rows[0], coef_rows[1]
        )
        tall[0, pl.ds(8, rows_here), :] = gr
        tall[1, pl.ds(8, rows_here), :] = gi
        _, _, gr, gi = scaled(
            (out[0, before, :][15:16], out[1, before, :][15:16]), before_row[0], before_row[1]
        )
        tall[0, pl.ds(7, 1), :] = gr
        tall[1, pl.ds(7, 1), :] = gi
        _, _, gr, gi = scaled(
            (out[0, after, :][0:1], out[1, after, :][0:1]), after_row[0], after_row[1]
        )
        tall[0, pl.ds(rows_here + 8, 1), :] = gr
        tall[1, pl.ds(rows_here + 8, 1), :] = gi
        end_rows[0] = (ur - laplace_rows(tall, 1, 0, rows_here)).astype(bf16)
        end_rows[1] = (ui + laplace_rows(tall, 0, 0, rows_here)).astype(bf16)


def phase_spec(slot, nx, ny):
    return pl.BlockSpec((1, 2, nx, ny), lambda i: (slot, 0, 0, 0))


def run_first(dims, orders, ints, phases, qx, qy, pieces):
    nx, ny, _ = dims
    return pl.pallas_call(
        partial(first_kernel, dims, orders),
        out_shape=jax.ShapeDtypeStruct((2, nx, ny), bf16),
        grid=(1,),
        in_specs=[sm, phase_spec(0, nx, ny), vm, vm] + [vm] * len(pieces),
        out_specs=vm,
        scratch_shapes=[pltpu.VMEM((2, nx, ny), bf16)] * 3,
        compiler_params=pltpu.CompilerParams(vmem_limit_bytes=vmem_bytes),
        cost_estimate=pl.CostEstimate(flops=2**30, bytes_accessed=2**22, transcendentals=0),
        name="first_step",
    )(ints, phases, qx, qy, *pieces)


def run_step(dims, orders, slot, index, ints, omega, w, coefs, phases, qx, qy, ends=None):
    nx, ny, rows_here = dims
    last = ends is not None
    rows_shape = jax.ShapeDtypeStruct((2, rows_here, ny), bf16)
    full = pltpu.VMEM((2, nx, ny), bf16)
    scratch = [pltpu.VMEM((2, nx, ny), f32), pltpu.VMEM((2, nx + 16, ny), f32), full, full, full]
    if last:
        outs = (rows_shape, rows_shape)
        scratch = [full] + scratch + [pltpu.VMEM((2, rows_here + 16, ny), f32)]
    else:
        outs = (jax.ShapeDtypeStruct((2, nx, ny), bf16), rows_shape)
    return pl.pallas_call(
        partial(step_kernel, dims, orders, index, last),
        out_shape=outs,
        grid=(1,),
        in_specs=[sm, sm, vm, phase_spec(slot + 1, nx, ny), vm, vm]
        + [vm] * (len(coefs) + (3 if last else 0)),
        out_specs=(vm, vm),
        scratch_shapes=scratch,
        compiler_params=pltpu.CompilerParams(vmem_limit_bytes=vmem_bytes),
        cost_estimate=pl.CostEstimate(flops=2**32, bytes_accessed=2**24, transcendentals=0),
        name="end_step" if last else "depth_step",
    )(ints, omega, w, phases, qx, qy, *coefs, *(ends or ()))


def image_kernel(freq_count, last_group, ints_ref, omega_ref, *refs):
    fields, (bottom, out) = refs[:-2], refs[-2:]
    forward, freq, group = ints_ref[1], ints_ref[3], ints_ref[4]

    def total(adjoint_at):
        result = None
        for i in range(freq_count):
            freq_i = freq ^ i
            adjoint = adjoint_at(i, freq_i)
            a = [fields[i][j].astype(f32) for j in range(2)]
            b = [adjoint[j].astype(f32) for j in range(2)]
            weight = omega_ref[freq_i] * (2 * forward - 1).astype(f32)
            term = weight * (a[0] * b[1] - a[1] * b[0])
            result = term if result is None else result + term
        out[0] = result

    @pl.when(group == last_group)
    def _():
        total(lambda i, freq_i: bottom.at[freq_i])

    @pl.when(group != last_group)
    def _():
        total(lambda i, freq_i: fields[freq_count + i])


def run_image(ints, omega, sections, fields, bottom):
    _, rows_here, ny = fields[0].shape
    return pl.pallas_call(
        partial(image_kernel, omega.shape[0], sections - 1),
        out_shape=jax.ShapeDtypeStruct((1, rows_here, ny), f32),
        in_specs=[sm, sm] + [vm] * (len(fields) + 1),
        out_specs=vm,
        compiler_params=pltpu.CompilerParams(vmem_limit_bytes=vmem_bytes),
        name="image",
    )(ints, omega, *fields, bottom)


def swap(values, axis, mask):
    size = lax.axis_size(axis)
    return lax.ppermute(values, axis, [(i, i ^ mask) for i in range(size)])


def doubling_masks(size):
    masks = []
    mask = size // 2
    while mask:
        masks.append(mask)
        mask //= 2
    descending = masks
    ascending = masks[:1] + masks[1:][::-1]
    return descending, ascending


def doubling_orders(masks):
    orders = [[0]]
    seen = [0]
    for mask in masks:
        new = [mask ^ o for o in seen]
        orders.append(new)
        seen = seen + new
    return orders


def first_exchange(pair, axis):
    size = lax.axis_size(axis)
    got = swap(pair, axis, size // 2)
    return [[pair[0:1], got[0:1]], [pair[1:2], got[1:2]]]


def after(values, earlier):
    return lax.optimization_barrier((values, earlier))[0]


def next_exchange(pieces, axis, level):
    masks = doubling_masks(lax.axis_size(axis))
    return [
        have + [swap(jnp.concatenate(have, 0), axis, masks[which][level])]
        for which, have in enumerate(pieces)
    ]


def per_device(source_top, adjoint_bottom, slowness, correction, slowness_ref, omega):
    row_parts = lax.axis_size("rows")
    sections = lax.axis_size("depth")
    group = lax.axis_index("depth")
    part_id = lax.axis_index("rows")
    freq_count = omega.shape[0]
    chains = 2 * freq_count
    rep = sections // chains
    rows_here, ny = slowness.shape[1:]
    nx = rows_here * row_parts
    dims = (nx, ny, rows_here)
    hy = ny // 2
    chain = lax.div(group, rep)
    forward = lax.div(chain, freq_count)
    freq = lax.rem(chain, freq_count)
    side = lax.rem(group, 2)
    half_sections = sections // 2
    masks = doubling_masks(row_parts)
    orders = [doubling_orders(m) for m in masks]
    rounds = len(masks[0])
    ints = jnp.stack([part_id, forward, side, freq, group]).astype(jnp.int32)

    def pick(values, index):
        return lax.dynamic_index_in_dim(values, index, 0, keepdims=False)

    plane, packed, same, other = run_pack(
        ints, slowness_ref, source_top, adjoint_bottom, slowness, correction
    )
    planes = first_exchange(plane, "rows")
    blocks = [packed]
    for k in range(1, sections):
        blocks.append(swap(packed if k < half_sections else (same, other)[k % 2], "depth", k))
    early, late, refs, coef_rows, ends = run_sort(ints, blocks, rows_here, hy)
    early = first_exchange(early, "rows")
    late = first_exchange(late, "rows")
    phases = phase_table(nx, ny, ints, omega, refs)
    rows_up = [(i, (i + 1) % row_parts) for i in range(row_parts)]
    rows_down = [(j, i) for i, j in rows_up]
    edges = [lax.ppermute(ends[0], "rows", rows_up), lax.ppermute(ends[1], "rows", rows_down)]

    def both_sides(pieces, earlier):
        mine, theirs = [], []
        for have in pieces:
            mine += have
            theirs += [swap(piece, "depth", 1) for piece in have[:-1]]
            theirs.append(swap(after(have[-1], earlier), "depth", 1))
        return mine + theirs

    qx, qy = basis_tables(nx), basis_tables(ny)
    for level in range(1, rounds):
        planes = next_exchange(planes, "rows", level)
        early = after(early, (planes, (phases, edges)) if level == rounds - 1 else planes)
        early = next_exchange(early, "rows", level)
        if level < rounds - 1:
            late = next_exchange(after(late, early), "rows", level)
    w = run_first(dims, orders, ints, phases, qx, qy, planes[0] + planes[1])
    late = next_exchange(after(late, w), "rows", rounds - 1)
    coefs = both_sides(early, w)

    row_outs = []
    for slot in range(sections - 1):
        ends = (coef_rows, *edges) if slot == sections - 2 else None
        first, second = run_step(dims, orders, slot, max(slot - 1, 0), ints, omega, w, coefs, phases, qx, qy, ends)
        if ends is None:
            w = first
            row_outs.append(second)
            if slot == 0:
                coefs = both_sides(late, w)
        else:
            row_outs += [first, second]

    def index_for(g, target):
        return target if g >= half_sections else sections - 2 - target

    def payload_for(mask):
        used = sorted(
            {index_for(g, g ^ mask) for g in range(sections) if index_for(g, g ^ mask) >= 0}
        )
        low = used[0]
        stack = jnp.stack(row_outs[low : used[-1] + 1])
        target = group ^ mask
        index = jnp.where(forward == 1, target, sections - 2 - target)
        return pick(stack, jnp.clip(index - low, 0, len(stack) - 1))

    far = [swap(payload_for(i * rep), "depth", i * rep) for i in range(freq_count, chains)]
    near = [payload_for(i * rep) for i in range(freq_count)]
    far, near = lax.optimization_barrier((far, near))
    fields = [f if i == 0 else swap(f, "depth", i * rep) for i, f in enumerate(near)] + far
    return run_image(ints, omega, sections, fields, adjoint_bottom)


def solution(mesh):
    in_specs = (
        P(None, None, "rows", None),
        P(None, None, "rows", None),
        P("depth", "rows", None),
        P("depth", "rows", None),
        P("depth"),
        P(),
    )
    out_specs = P("depth", "rows", None)
    return jax.shard_map(
        per_device, mesh=mesh, in_specs=in_specs, out_specs=out_specs, check_vma=False
    )
```

time: 115 us -> 83 us (0.72)
  waiting for transfers between devices: 35.7 us -> 15.3 us
  other arithmetic: 11.4 us -> 0.38 us
  local copies, waits for them, and re-layouts: 2.56 us -> 8.21 us
  Pallas kernels: 29.9 us -> 25.8 us
  between operations: 2.45 us -> 1.01 us
    ppermute x32 -> x37, waiting for transfers between devices: 30 us -> 12.4 us  [swap(): return lax.ppermute(values, axis, [(i, i ^ mask) for i in range(size)])]
    unnamed x19 -> x24, local copies, waits for them, and re-layouts: 0.32 us -> 6.62 us
    ppermute x32 -> x37, starting transfers between devices: 31.8 us -> 27.1 us  [swap(): return lax.ppermute(values, axis, [(i, i ^ mask) for i in range(size)])]
    ppermute x2, starting transfers between devices: 0.74 us -> 4.9 us  [the longest x1 4.34 us: per_device(): lax.ppermute(ends[1], 'rows', rows_down)]
    another operation x7 -> x1, other arithmetic: 4.07 us -> 0.05 us  [payload_for(): stack = jnp.stack(row_outs[low:used[-1] + 1])]
    pallas_call x1, Pallas kernels: 7.88 us -> 4.1 us  [phase_table(): pl.pallas_call(partial(phase_kernel, nx, ny), out_shape=jax.ShapeDtypeStr...]
    mul x1 -> x0, other arithmetic: 3.3 us -> none  [per_device(): phases = phase_table(nx, ny, levels * omega_here, sign)]
    ppermute x2, waiting for transfers between devices: 5.7 us -> 2.84 us  [the longest x1 2.84 us: per_device(): lax.ppermute(ends[1], 'rows', rows_down)]
  transfers between devices with their start and end apart: 34 -> 39, of which waited for: 17 -> 12; matrix products, arithmetic and copies ran while one was open for 11% -> 1% of each run, Pallas kernels for 20% -> 20%
where the time goes in v2:
time: 83 us; the launch traced here: 82.7 us
  starting transfers between devices  32 us (39%)
  Pallas kernels  25.8 us (31%)
  waiting for transfers between devices  15.3 us (18%)
  local copies, waits for them, and re-layouts  8.21 us (10%)
  between operations  1.01 us (1%)
    ppermute x37, starting transfers between devices, swap(): return lax.ppermute(values, axis, [(i, i ^ mask) for i in range(size)])  27.1 us
    pallas_call x3, Pallas kernels, run_step(): pl.pallas_call(partial(step_kernel, dims, orders, index, last), out_shape...  16.5 us
    ppermute x37, waiting for transfers between devices, swap(): return lax.ppermute(values, axis, [(i, i ^ mask) for i in range(size)])  12.4 us
    unnamed x24, local copies, waits for them, and re-layouts  6.62 us
    ppermute x1, starting transfers between devices, per_device(): lax.ppermute(ends[1], 'rows', rows_down)  4.34 us
    pallas_call x1, Pallas kernels, phase_table(): pl.pallas_call(partial(phase_kernel, nx, ny), out_shape=jax.ShapeDtypeStr...  4.1 us
    ppermute x1, waiting for transfers between devices, per_device(): lax.ppermute(ends[1], 'rows', rows_down)  2.84 us
    pallas_call x1, Pallas kernels, run_pack(): pl.pallas_call(partial(pack_kernel, rows_here, hy), out_shape=(jax.ShapeD...  2.48 us
  transfers between devices with their start and end apart: 39, of which 12 were waited for; matrix products, arithmetic and copies ran while one was open for 1% of the time, Pallas kernels for 20%

profile of v2, /device:TPU:0, one launch (start us, length us, event | category | flops | bytes accessed | tf_op | source)
XLA Modules:
  0.0 82.7 jit_solution(11358010757318901156)
XLA Ops:
  1.3 2.5 %pack_rows.1 = (bf16[2,64,512]{2,1,0:T(8,128)(2,1)}, bf16[2,144,256]{2,1,0:T(8,128)(2,1)}, bf16[144,256]{1,0:T(8,128)(2,1)}, bf16[144,256]{1,0:T(8,128)(2,1)}) custom-call(s32[5]{0:T(128)} %stack.46.ints_ref, f32[1]{0:T(128)S(6)} %copy.13.ref_ref, bf16[2,2,64,512]{3,2,1,0:T(8,128)(2,1)} %source.1, bf16[2,2,64,512]{3,2,1,0:T(8,128)(2,1)} %refs_4_.1, ...), custom_call_target="tpu_custom_call" | custom-call | tf_op jit(solution)/shard_map/pack_rows/pallas_call | solution.py:175
  3.8 4.1 %collective-permute-start.3 = (bf16[2,64,512]{2,1,0:T(8,128)(2,1)}, bf16[2,64,512]{2,1,0:T(8,128)(2,1)S(1)}, u32[]{:S(2)}, u32[]{:S(2)}) collective-permute-start(bf16[2,64,512]{2,1,0:T(8,128)(2,1)} %get-tuple-element.52), channel_id=1, source_target_pairs={{0,4},{1,5},{2,6},{3,7},{4,0},{5,1},{6,2},{7,3},{8,12},{9,13},{10,... | collective-permute-start | bytes 393224 | tf_op jit(solution)/shard_map/ppermute | solution.py:571
  7.9 1.5 %collective-permute-start.1 = (bf16[144,256]{1,0:T(8,128)(2,1)}, bf16[144,256]{1,0:T(8,128)(2,1)S(1)}, u32[]{:S(2)}, u32[]{:S(2)}) collective-permute-start(bf16[144,256]{1,0:T(8,128)(2,1)} %get-tuple-element.49), channel_id=1, source_target_pairs={{0,16},{8,24},{16,0},{24,8},{1,17},{9,25},{17,1},{25,9},{2,18},{10... | collective-permute-start | bytes 221192 | tf_op jit(solution)/shard_map/ppermute | solution.py:571
  10.6 3.8 %collective-permute-done.3 = bf16[2,64,512]{2,1,0:T(8,128)(2,1)S(1)} collective-permute-done((bf16[2,64,512]{2,1,0:T(8,128)(2,1)}, bf16[2,64,512]{2,1,0:T(8,128)(2,1)S(1)}, u32[]{:S(2)}, u32[]{:S(2)}) %collective-permute-start.3) | collective-permute-done | bytes 131104 | tf_op jit(solution)/shard_map/ppermute | solution.py:571
  15.3 1.6 %collective-permute-start.6 = (bf16[2,64,512]{2,1,0:T(8,128)(2,1)S(1)}, bf16[2,64,512]{2,1,0:T(8,128)(2,1)S(1)}, u32[]{:S(2)}, u32[]{:S(2)}) collective-permute-start(bf16[2,64,512]{2,1,0:T(8,128)(2,1)S(1)} %pad_maximum_fusion.6), channel_id=1, source_target_pairs={{0,1},{1,0},{2,3},{3,2},{4,5},{5,4},{6,7},{7,6},{8,9},{9,8},{10,11... | collective-permute-start | bytes 393224 | tf_op jit(solution)/shard_map/ppermute | solution.py:571
  19.2 3.3 %collective-permute-start.8 = (bf16[2,1,64,256]{3,2,1,0:T(8,128)(2,1)S(1)}, bf16[2,1,64,256]{3,2,1,0:T(8,128)(2,1)S(1)}, u32[]{:S(2)}, u32[]{:S(2)}) collective-permute-start(bf16[2,1,64,256]{3,2,1,0:T(8,128)(2,1)S(1)} %get-tuple-element.53), channel_id=1, source_target_pairs={{0,4},{1,5},{2,6},{3,7},{4,0},{5,1},{6,2},{7,3},{8,12},{9,13},{10,... | collective-permute-start | bytes 196616 | tf_op jit(solution)/shard_map/ppermute | solution.py:571
  23.9 4.1 %phase_table.1.phase = bf16[4,2,512,512]{3,2,1,0:T(8,128)(2,1)S(1)} custom-call(s32[5]{0:T(128)S(1)} %copy-done.6, f32[2]{0:T(128)S(1)} %copy-done.8, f32[4,8,128]{2,1,0:T(8,128)S(1)} %get-tuple-element.51.refs_ref), custom_call_target="tpu_custom_call" | custom-call | tf_op jit(solution)/shard_map/phase_table/pallas_call | solution.py:118
  28.6 1.3 %collective-permute-start.10 = (bf16[2,1,64,256]{3,2,1,0:T(8,128)(2,1)S(1)}, bf16[2,1,64,256]{3,2,1,0:T(8,128)(2,1)S(1)}, u32[]{:S(2)}, u32[]{:S(2)}) collective-permute-start(bf16[2,1,64,256]{3,2,1,0:T(8,128)(2,1)S(1)} %pad_maximum_fusion.12), channel_id=1, source_target_pairs={{0,1},{1,0},{2,3},{3,2},{4,5},{5,4},{6,7},{7,6},{8,9},{9,8},{10,11... | collective-permute-start | bytes 196616 | tf_op jit(solution)/shard_map/ppermute | solution.py:571
  29.9 2.6 %collective-permute-start.9 = (bf16[2,1,64,256]{3,2,1,0:T(8,128)(2,1)S(1)}, bf16[2,1,64,256]{3,2,1,0:T(8,128)(2,1)S(1)}, u32[]{:S(2)}, u32[]{:S(2)}) collective-permute-start(bf16[2,1,64,256]{3,2,1,0:T(8,128)(2,1)S(1)} %pad_maximum_fusion.11), channel_id=1, source_target_pairs={{0,2},{1,3},{2,0},{3,1},{4,6},{5,7},{6,4},{7,5},{8,10},{9,11},{10,... | collective-permute-start | bytes 196616 | tf_op jit(solution)/shard_map/ppermute | solution.py:571
  33.0 4.3 %collective-permute-start.12 = (bf16[2,1,512]{2,1,0:T(2,128)(2,1)S(1)}, bf16[2,1,512]{2,1,0:T(2,128)(2,1)S(1)}, u32[]{:S(2)}, u32[]{:S(2)}) collective-permute-start(bf16[2,1,512]{2,1,0:T(2,128)(2,1)S(1)} %get-tuple-element.107), channel_id=1, source_target_pairs={{1,0},{2,1},{3,2},{4,3},{5,4},{6,5},{7,6},{0,7},{9,8},{10,9},{11,1... | collective-permute-start | bytes 6152 | tf_op jit(solution)/shard_map/ppermute | solution.py:651
  37.8 2.8 %collective-permute-done.12.rest_18_ = bf16[2,1,512]{2,1,0:T(2,128)(2,1)S(1)} collective-permute-done((bf16[2,1,512]{2,1,0:T(2,128)(2,1)S(1)}, bf16[2,1,512]{2,1,0:T(2,128)(2,1)S(1)}, u32[]{:S(2)}, u32[]{:S(2)}) %collective-permute-start.12) | collective-permute-done | bytes 2080 | tf_op jit(solution)/shard_map/ppermute | solution.py:651
  40.6 1.4 %collective-permute-done.7.rest_7_ = bf16[4,64,512]{2,1,0:T(8,128)(2,1)S(1)} collective-permute-done((bf16[4,64,512]{2,1,0:T(8,128)(2,1)S(1)}, bf16[4,64,512]{2,1,0:T(8,128)(2,1)S(1)}, u32[]{:S(2)}, u32[]{:S(2)}) %collective-permute-start.7) | collective-permute-done | bytes 262176 | tf_op jit(solution)/shard_map/ppermute | solution.py:571
  43.1 1.1 %collective-permute-start.13 = (bf16[4,1,64,256]{3,2,1,0:T(8,128)(2,1)S(1)}, bf16[4,1,64,256]{3,2,1,0:T(8,128)(2,1)S(1)}, u32[]{:S(2)}, u32[]{:S(2)}) collective-permute-start(bf16[4,1,64,256]{3,2,1,0:T(8,128)(2,1)S(1)} %pad_maximum_fusion.7), channel_id=1, source_target_pairs={{0,1},{1,0},{2,3},{3,2},{4,5},{5,4},{6,7},{7,6},{8,9},{9,8},{10,11... | collective-permute-start | bytes 393224 | tf_op jit(solution)/shard_map/ppermute | solution.py:571
  45.6 1.4 %collective-permute-done.14.rest_7_ = bf16[4,1,64,256]{3,2,1,0:T(8,128)(2,1)S(1)} collective-permute-done((bf16[4,1,64,256]{3,2,1,0:T(8,128)(2,1)S(1)}, bf16[4,1,64,256]{3,2,1,0:T(8,128)(2,1)S(1)}, u32[]{:S(2)}, u32[]{:S(2)}) %collective-permute-start.14) | collective-permute-done | bytes 131104 | tf_op jit(solution)/shard_map/ppermute | solution.py:571
  47.1 1.1 %collective-permute-done.13.rest_3_ = bf16[4,1,64,256]{3,2,1,0:T(8,128)(2,1)S(1)} collective-permute-done((bf16[4,1,64,256]{3,2,1,0:T(8,128)(2,1)S(1)}, bf16[4,1,64,256]{3,2,1,0:T(8,128)(2,1)S(1)}, u32[]{:S(2)}, u32[]{:S(2)}) %collective-permute-start.13) | collective-permute-done | bytes 131104 | tf_op jit(solution)/shard_map/ppermute | solution.py:571
  51.2 1.6 %collective-permute-start.26 = (bf16[4,2,64,256]{3,2,1,0:T(8,128)(2,1)S(1)}, bf16[4,2,64,256]{3,2,1,0:T(8,128)(2,1)S(1)}, u32[]{:S(2)}, u32[]{:S(2)}) collective-permute-start(bf16[4,2,64,256]{3,2,1,0:T(8,128)(2,1)S(1)} %pad_maximum_fusion.3), channel_id=1, source_target_pairs={{0,1},{1,0},{2,3},{3,2},{4,5},{5,4},{6,7},{7,6},{8,9},{9,8},{10,11... | collective-permute-start | bytes 786440 | tf_op jit(solution)/shard_map/ppermute | solution.py:571
  52.8 5.5 %depth_step.2 = (bf16[2,512,512]{2,1,0:T(8,128)(2,1)S(1)}, bf16[2,64,512]{2,1,0:T(8,128)(2,1)S(1)}) custom-call(s32[5]{0:T(128)S(1)} %copy-done.6, f32[2]{0:T(128)S(1)} %copy-done.9, bf16[2,512,512]{2,1,0:T(8,128)(2,1)S(1)} %first_step.1.w_ref, bf16[4,2,512,512]{3,2,1,0:T(8,128)(2,1)S(1)} %phase_table.1.phase, bf16[4,256,256]{2,1,0:T(8,128)(2,1)S(1)} %copy-done.3, ...), custom_call_target="tpu_custom_call" | custom-call | flops 4294967296 | bytes 16777216 | tf_op jit(solution)/shard_map/depth_step/pallas_call | solution.py:518
  62.0 1.1 %collective-permute-done.33.rest_13_ = bf16[1,2,64,256]{3,2,1,0:T(8,128)(2,1)S(1)} collective-permute-done((bf16[1,2,64,256]{3,2,1,0:T(8,128)(2,1)S(1)}, bf16[1,2,64,256]{3,2,1,0:T(8,128)(2,1)S(1)}, u32[]{:S(2)}, u32[]{:S(2)}) %collective-permute-start.33) | collective-permute-done | bytes 65568 | tf_op jit(solution)/shard_map/ppermute | solution.py:571
  63.2 2.2 %copy-done.1 = bf16[4,2,512,512]{3,2,1,0:T(8,128)(2,1)S(1)} copy-done((bf16[4,2,512,512]{3,2,1,0:T(8,128)(2,1)S(1)}, bf16[4,2,512,512]{3,2,1,0:T(8,128)(2,1)}, u32[]{:S(2)}) %copy-start.1) | copy-done | bytes 4194328
  65.4 1.2 %copy-done.11 = bf16[2,512,512]{2,1,0:T(8,128)(2,1)S(1)} copy-done((bf16[2,512,512]{2,1,0:T(8,128)(2,1)S(1)}, bf16[2,512,512]{2,1,0:T(8,128)(2,1)}, u32[]{:S(2)}) %copy-start.11) | copy-done | bytes 1048600
  66.6 5.3 %depth_step.3 = (bf16[2,512,512]{2,1,0:T(8,128)(2,1)S(1)}, bf16[2,64,512]{2,1,0:T(8,128)(2,1)S(1)}) custom-call(s32[5]{0:T(128)S(1)} %copy-done.7, f32[2]{0:T(128)S(1)} %copy-done.9, bf16[2,512,512]{2,1,0:T(8,128)(2,1)S(1)} %copy-done.11, bf16[4,2,512,512]{3,2,1,0:T(8,128)(2,1)S(1)} %copy-done.1, bf16[4,256,256]{2,1,0:T(8,128)(2,1)S(1)} %copy-done.3, ...), custom_call_target="tpu_custom_call" | custom-call | flops 4294967296 | bytes 16777216 | tf_op jit(solution)/shard_map/depth_step/pallas_call | solution.py:518
  72.1 1.8 %collective-permute-start.36 = (bf16[2,64,512]{2,1,0:T(8,128)(2,1)S(1)}, bf16[2,64,512]{2,1,0:T(8,128)(2,1)S(1)}, u32[]{:S(2)}, u32[]{:S(2)}) collective-permute-start(bf16[2,64,512]{2,1,0:T(8,128)(2,1)S(1)} %get-tuple-element.94), channel_id=1, source_target_pairs={{0,16},{8,24},{16,0},{24,8},{1,17},{9,25},{17,1},{25,9},{2,18},{10... | collective-permute-start | bytes 393224 | tf_op jit(solution)/shard_map/ppermute | solution.py:571
  73.9 5.6 %end_step.1 = (bf16[2,64,512]{2,1,0:T(8,128)(2,1)S(1)}, bf16[2,64,512]{2,1,0:T(8,128)(2,1)S(1)}) custom-call(s32[5]{0:T(128)S(1)} %copy-done.7, f32[2]{0:T(128)S(1)} %copy-done.9, bf16[2,512,512]{2,1,0:T(8,128)(2,1)S(1)} %get-tuple-element.83.w_ref, bf16[4,2,512,512]{3,2,1,0:T(8,128)(2,1)S(1)} %copy-done.2, bf16[4,256,256]{2,1,0:T(8,128)(2,1)S(1)} %copy-done.3, ...), custom_call_target="tpu_custom_call" | custom-call | flops 4294967296 | bytes 16777216 | tf_op jit(solution)/shard_map/end_step/pallas_call | solution.py:518
  81.4 1.3 %image.1 = f32[1,64,512]{2,1,0:T(8,128)} custom-call(s32[5]{0:T(128)S(1)} %copy-done.7, f32[2]{0:T(128)S(1)} %copy-done.9, bf16[2,64,512]{2,1,0:T(8,128)(2,1)S(1)} %get-tuple-element.87.refs_0_, bf16[2,64,512]{2,1,0:T(8,128)(2,1)S(1)} %collective-permute-done.38.refs_1_, bf16[2,64,512]{2,1,0:T(8,128)(2,1)S(1)} %collective-permute-done.36.refs_2_, ...), custom_call_target="tpu_custom_call" | custom-call | tf_op jit(solution)/shard_map/image/pallas_call | solution.py:559
  (109 shorter events, 18.9 us)
Async XLA Ops:
  3.8 10.6 %collective-permute-start.3 = (bf16[2,64,512]{2,1,0:T(8,128)(2,1)}, bf16[2,64,512]{2,1,0:T(8,128)(2,1)S(1)}, u32[]{:S(2)}, u32[]{:S(2)}) collective-permute-start(bf16[2,64,512]{2,1,0:T(8,128)(2,1)} %get-tuple-element.52), channel_id=1, source_target_pairs={{0,4},{1,5},{2,6},{3,7},{4,0},{5,1},{6,2},{7,3},{8,12},{9,13},{10,... | collective-permute-start | bytes 393224 | tf_op jit(solution)/shard_map/ppermute | solution.py:571
  7.9 9.1 %collective-permute-start = (bf16[2,144,256]{2,1,0:T(8,128)(2,1)}, bf16[2,144,256]{2,1,0:T(8,128)(2,1)S(1)}, u32[]{:S(2)}, u32[]{:S(2)}) collective-permute-start(bf16[2,144,256]{2,1,0:T(8,128)(2,1)} %get-tuple-element.48.refs_0_), channel_id=1, source_target_pairs={{0,8},{8,0},{16,24},{24,16},{1,9},{9,1},{17,25},{25,17},{2,10},{10... | collective-permute-start | bytes 442376 | tf_op jit(solution)/shard_map/ppermute | solution.py:571
  7.9 9.1 %collective-permute-start.1 = (bf16[144,256]{1,0:T(8,128)(2,1)}, bf16[144,256]{1,0:T(8,128)(2,1)S(1)}, u32[]{:S(2)}, u32[]{:S(2)}) collective-permute-start(bf16[144,256]{1,0:T(8,128)(2,1)} %get-tuple-element.49), channel_id=1, source_target_pairs={{0,16},{8,24},{16,0},{24,8},{1,17},{9,25},{17,1},{25,9},{2,18},{10... | collective-permute-start | bytes 221192 | tf_op jit(solution)/shard_map/ppermute | solution.py:571
  9.4 7.6 %collective-permute-start.2 = (bf16[144,256]{1,0:T(8,128)(2,1)}, bf16[144,256]{1,0:T(8,128)(2,1)S(1)}, u32[]{:S(2)}, u32[]{:S(2)}) collective-permute-start(bf16[144,256]{1,0:T(8,128)(2,1)} %get-tuple-element.50), channel_id=1, source_target_pairs={{0,24},{8,16},{16,8},{24,0},{1,25},{9,17},{17,9},{25,1},{2,26},{10... | collective-permute-start | bytes 221192 | tf_op jit(solution)/shard_map/ppermute | solution.py:571
  14.4 14.1 %collective-permute-start.4 = (bf16[2,64,512]{2,1,0:T(8,128)(2,1)S(1)}, bf16[2,64,512]{2,1,0:T(8,128)(2,1)S(1)}, u32[]{:S(2)}, u32[]{:S(2)}) collective-permute-start(bf16[2,64,512]{2,1,0:T(8,128)(2,1)S(1)} %pad_maximum_fusion.5), channel_id=1, source_target_pairs={{0,2},{1,3},{2,0},{3,1},{4,6},{5,7},{6,4},{7,5},{8,10},{9,11},{10,... | collective-permute-start | bytes 393224 | tf_op jit(solution)/shard_map/ppermute | solution.py:571
  15.3 13.2 %collective-permute-start.6 = (bf16[2,64,512]{2,1,0:T(8,128)(2,1)S(1)}, bf16[2,64,512]{2,1,0:T(8,128)(2,1)S(1)}, u32[]{:S(2)}, u32[]{:S(2)}) collective-permute-start(bf16[2,64,512]{2,1,0:T(8,128)(2,1)S(1)} %pad_maximum_fusion.6), channel_id=1, source_target_pairs={{0,1},{1,0},{2,3},{3,2},{4,5},{5,4},{6,7},{7,6},{8,9},{9,8},{10,11... | collective-permute-start | bytes 393224 | tf_op jit(solution)/shard_map/ppermute | solution.py:571
  19.2 9.3 %collective-permute-start.8 = (bf16[2,1,64,256]{3,2,1,0:T(8,128)(2,1)S(1)}, bf16[2,1,64,256]{3,2,1,0:T(8,128)(2,1)S(1)}, u32[]{:S(2)}, u32[]{:S(2)}) collective-permute-start(bf16[2,1,64,256]{3,2,1,0:T(8,128)(2,1)S(1)} %get-tuple-element.53), channel_id=1, source_target_pairs={{0,4},{1,5},{2,6},{3,7},{4,0},{5,1},{6,2},{7,3},{8,12},{9,13},{10,... | collective-permute-start | bytes 196616 | tf_op jit(solution)/shard_map/ppermute | solution.py:571
  22.5 10.2 %collective-permute-start.23 = (bf16[2,2,64,256]{3,2,1,0:T(8,128)(2,1)S(1)}, bf16[2,2,64,256]{3,2,1,0:T(8,128)(2,1)S(1)}, u32[]{:S(2)}, u32[]{:S(2)}) collective-permute-start(bf16[2,2,64,256]{3,2,1,0:T(8,128)(2,1)S(1)} %get-tuple-element.69), channel_id=1, source_target_pairs={{0,4},{1,5},{2,6},{3,7},{4,0},{5,1},{6,2},{7,3},{8,12},{9,13},{10,... | collective-permute-start | bytes 393224 | tf_op jit(solution)/shard_map/ppermute | solution.py:571
  22.7 14.8 %collective-permute-start.11 = (bf16[2,1,512]{2,1,0:T(2,128)(2,1)S(1)}, bf16[2,1,512]{2,1,0:T(2,128)(2,1)S(1)}, u32[]{:S(2)}, u32[]{:S(2)}) collective-permute-start(bf16[2,1,512]{2,1,0:T(2,128)(2,1)S(1)} %get-tuple-element.108), channel_id=1, source_target_pairs={{0,1},{1,2},{2,3},{3,4},{4,5},{5,6},{6,7},{7,0},{8,9},{9,10},{10,1... | collective-permute-start | bytes 6152 | tf_op jit(solution)/shard_map/ppermute | solution.py:651
  28.6 4.4 %collective-permute-start.10 = (bf16[2,1,64,256]{3,2,1,0:T(8,128)(2,1)S(1)}, bf16[2,1,64,256]{3,2,1,0:T(8,128)(2,1)S(1)}, u32[]{:S(2)}, u32[]{:S(2)}) collective-permute-start(bf16[2,1,64,256]{3,2,1,0:T(8,128)(2,1)S(1)} %pad_maximum_fusion.12), channel_id=1, source_target_pairs={{0,1},{1,0},{2,3},{3,2},{4,5},{5,4},{6,7},{7,6},{8,9},{9,8},{10,11... | collective-permute-start | bytes 196616 | tf_op jit(solution)/shard_map/ppermute | solution.py:571
  29.9 7.4 %collective-permute-start.9 = (bf16[2,1,64,256]{3,2,1,0:T(8,128)(2,1)S(1)}, bf16[2,1,64,256]{3,2,1,0:T(8,128)(2,1)S(1)}, u32[]{:S(2)}, u32[]{:S(2)}) collective-permute-start(bf16[2,1,64,256]{3,2,1,0:T(8,128)(2,1)S(1)} %pad_maximum_fusion.11), channel_id=1, source_target_pairs={{0,2},{1,3},{2,0},{3,1},{4,6},{5,7},{6,4},{7,5},{8,10},{9,11},{10,... | collective-permute-start | bytes 196616 | tf_op jit(solution)/shard_map/ppermute | solution.py:571
  32.6 8.0 %collective-permute-start.5 = (bf16[4,64,512]{2,1,0:T(8,128)(2,1)S(1)}, bf16[4,64,512]{2,1,0:T(8,128)(2,1)S(1)}, u32[]{:S(2)}, u32[]{:S(2)}) collective-permute-start(bf16[4,64,512]{2,1,0:T(8,128)(2,1)S(1)} %pad_maximum_fusion.1), channel_id=1, source_target_pairs={{0,1},{1,0},{2,3},{3,2},{4,5},{5,4},{6,7},{7,6},{8,9},{9,8},{10,11... | collective-permute-start | bytes 786440 | tf_op jit(solution)/shard_map/ppermute | solution.py:571
  32.7 9.3 %collective-permute-start.7 = (bf16[4,64,512]{2,1,0:T(8,128)(2,1)S(1)}, bf16[4,64,512]{2,1,0:T(8,128)(2,1)S(1)}, u32[]{:S(2)}, u32[]{:S(2)}) collective-permute-start(bf16[4,64,512]{2,1,0:T(8,128)(2,1)S(1)} %pad_maximum_fusion.2), channel_id=1, source_target_pairs={{0,2},{1,3},{2,0},{3,1},{4,6},{5,7},{6,4},{7,5},{8,10},{9,11},{10,... | collective-permute-start | bytes 786440 | tf_op jit(solution)/shard_map/ppermute | solution.py:571
  33.0 7.6 %collective-permute-start.12 = (bf16[2,1,512]{2,1,0:T(2,128)(2,1)S(1)}, bf16[2,1,512]{2,1,0:T(2,128)(2,1)S(1)}, u32[]{:S(2)}, u32[]{:S(2)}) collective-permute-start(bf16[2,1,512]{2,1,0:T(2,128)(2,1)S(1)} %get-tuple-element.107), channel_id=1, source_target_pairs={{1,0},{2,1},{3,2},{4,3},{5,4},{6,5},{7,6},{0,7},{9,8},{10,9},{11,1... | collective-permute-start | bytes 6152 | tf_op jit(solution)/shard_map/ppermute | solution.py:651
  37.4 7.6 %collective-permute-start.25 = (bf16[2,2,64,256]{3,2,1,0:T(8,128)(2,1)S(1)}, bf16[2,2,64,256]{3,2,1,0:T(8,128)(2,1)S(1)}, u32[]{:S(2)}, u32[]{:S(2)}) collective-permute-start(bf16[2,2,64,256]{3,2,1,0:T(8,128)(2,1)S(1)} %pad_maximum_fusion.10), channel_id=1, source_target_pairs={{0,1},{1,0},{2,3},{3,2},{4,5},{5,4},{6,7},{7,6},{8,9},{9,8},{10,11... | collective-permute-start | bytes 393224 | tf_op jit(solution)/shard_map/ppermute | solution.py:571
  37.5 8.1 %collective-permute-start.24 = (bf16[2,2,64,256]{3,2,1,0:T(8,128)(2,1)S(1)}, bf16[2,2,64,256]{3,2,1,0:T(8,128)(2,1)S(1)}, u32[]{:S(2)}, u32[]{:S(2)}) collective-permute-start(bf16[2,2,64,256]{3,2,1,0:T(8,128)(2,1)S(1)} %pad_maximum_fusion.9), channel_id=1, source_target_pairs={{0,2},{1,3},{2,0},{3,1},{4,6},{5,7},{6,4},{7,5},{8,10},{9,11},{10,... | collective-permute-start | bytes 393224 | tf_op jit(solution)/shard_map/ppermute | solution.py:571
  42.0 5.0 %collective-permute-start.14 = (bf16[4,1,64,256]{3,2,1,0:T(8,128)(2,1)S(1)}, bf16[4,1,64,256]{3,2,1,0:T(8,128)(2,1)S(1)}, u32[]{:S(2)}, u32[]{:S(2)}) collective-permute-start(bf16[4,1,64,256]{3,2,1,0:T(8,128)(2,1)S(1)} %pad_maximum_fusion.8), channel_id=1, source_target_pairs={{0,2},{1,3},{2,0},{3,1},{4,6},{5,7},{6,4},{7,5},{8,10},{9,11},{10,... | collective-permute-start | bytes 393224 | tf_op jit(solution)/shard_map/ppermute | solution.py:571
  43.1 5.0 %collective-permute-start.13 = (bf16[4,1,64,256]{3,2,1,0:T(8,128)(2,1)S(1)}, bf16[4,1,64,256]{3,2,1,0:T(8,128)(2,1)S(1)}, u32[]{:S(2)}, u32[]{:S(2)}) collective-permute-start(bf16[4,1,64,256]{3,2,1,0:T(8,128)(2,1)S(1)} %pad_maximum_fusion.7), channel_id=1, source_target_pairs={{0,1},{1,0},{2,3},{3,2},{4,5},{5,4},{6,7},{7,6},{8,9},{9,8},{10,11... | collective-permute-start | bytes 393224 | tf_op jit(solution)/shard_map/ppermute | solution.py:571
  47.1 5.7 %collective-permute-start.22 = (bf16[4,1,64,256]{3,2,1,0:T(8,128)(2,1)S(1)}, bf16[4,1,64,256]{3,2,1,0:T(8,128)(2,1)S(1)}, u32[]{:S(2)}, u32[]{:S(2)}) collective-permute-start(bf16[4,1,64,256]{3,2,1,0:T(8,128)(2,1)S(1)} %collective-permute-done.14.rest_7_), channel_id=1, source_target_pairs={{0,8},{8,0},{16,24},{24,16},{1,9},{9,1},{17,25},{25,17},{2,10},{10... | collective-permute-start | bytes 393224 | tf_op jit(solution)/shard_map/ppermute | solution.py:571
  48.2 4.6 %collective-permute-start.18 = (bf16[4,1,64,256]{3,2,1,0:T(8,128)(2,1)S(1)}, bf16[4,1,64,256]{3,2,1,0:T(8,128)(2,1)S(1)}, u32[]{:S(2)}, u32[]{:S(2)}) collective-permute-start(bf16[4,1,64,256]{3,2,1,0:T(8,128)(2,1)S(1)} %collective-permute-done.13.rest_3_), channel_id=1, source_target_pairs={{0,8},{8,0},{16,24},{24,16},{1,9},{9,1},{17,25},{25,17},{2,10},{10... | collective-permute-start | bytes 393224 | tf_op jit(solution)/shard_map/ppermute | solution.py:571
  50.2 9.2 %collective-permute-start.27 = (bf16[4,2,64,256]{3,2,1,0:T(8,128)(2,1)S(1)}, bf16[4,2,64,256]{3,2,1,0:T(8,128)(2,1)S(1)}, u32[]{:S(2)}, u32[]{:S(2)}) collective-permute-start(bf16[4,2,64,256]{3,2,1,0:T(8,128)(2,1)S(1)} %pad_maximum_fusion.4), channel_id=1, source_target_pairs={{0,2},{1,3},{2,0},{3,1},{4,6},{5,7},{6,4},{7,5},{8,10},{9,11},{10,... | collective-permute-start | bytes 786440 | tf_op jit(solution)/shard_map/ppermute | solution.py:571
  51.2 8.3 %collective-permute-start.26 = (bf16[4,2,64,256]{3,2,1,0:T(8,128)(2,1)S(1)}, bf16[4,2,64,256]{3,2,1,0:T(8,128)(2,1)S(1)}, u32[]{:S(2)}, u32[]{:S(2)}) collective-permute-start(bf16[4,2,64,256]{3,2,1,0:T(8,128)(2,1)S(1)} %pad_maximum_fusion.3), channel_id=1, source_target_pairs={{0,1},{1,0},{2,3},{3,2},{4,5},{5,4},{6,7},{7,6},{8,9},{9,8},{10,11... | collective-permute-start | bytes 786440 | tf_op jit(solution)/shard_map/ppermute | solution.py:571
  72.1 7.5 %collective-permute-start.36 = (bf16[2,64,512]{2,1,0:T(8,128)(2,1)S(1)}, bf16[2,64,512]{2,1,0:T(8,128)(2,1)S(1)}, u32[]{:S(2)}, u32[]{:S(2)}) collective-permute-start(bf16[2,64,512]{2,1,0:T(8,128)(2,1)S(1)} %get-tuple-element.94), channel_id=1, source_target_pairs={{0,16},{8,24},{16,0},{24,8},{1,17},{9,25},{17,1},{25,9},{2,18},{10... | collective-permute-start | bytes 393224 | tf_op jit(solution)/shard_map/ppermute | solution.py:571
  73.9 5.9 %collective-permute-start.37 = (bf16[2,64,512]{2,1,0:T(8,128)(2,1)S(1)}, bf16[2,64,512]{2,1,0:T(8,128)(2,1)S(1)}, u32[]{:S(2)}, u32[]{:S(2)}) collective-permute-start(bf16[2,64,512]{2,1,0:T(8,128)(2,1)S(1)} %get-tuple-element.93), channel_id=1, source_target_pairs={{0,24},{8,16},{16,8},{24,0},{1,25},{9,17},{17,9},{25,1},{2,26},{10... | collective-permute-start | bytes 393224 | tf_op jit(solution)/shard_map/ppermute | solution.py:571
  (27 other events, 137.0 us)

commit v3 on v2

--- a/solution.py
+++ b/solution.py
@@ -11,7 +11,7 @@
 
 bf16 = jnp.bfloat16
 f32 = jnp.float32
-vmem_bytes = 20 * 1024 * 1024
+vmem_bytes = 48 * 1024 * 1024
 
 
 def basis(length):
@@ -70,10 +70,8 @@
     return horner(lens_cos, s), a * horner(lens_sin, s)
 
 
-def phase_kernel(nx, ny, ints_ref, omega_ref, refs_ref, out_ref):
+def fill_phase(nx, ny, level, sign, out):
     qx, qy = nx // 4, ny // 4
-    sign = (2 * ints_ref[1] - 1).astype(f32)
-    level = omega_ref[ints_ref[3]] * refs_ref[0, 0:1, 0:1]
 
     def waves(rows, cols, axis, parity, length):
         j = lax.broadcasted_iota(jnp.int32, (rows, cols), axis)
@@ -110,90 +108,11 @@
                             v = jnp.where(row_zero & col_zero, corner[part][0:1], v)
                         rows = pl.ds((2 * px + sx) * qx, qx)
                         cols = pl.ds((2 * py + sy) * qy, qy)
-                        out_ref[0, part, rows, cols] = v.astype(bf16)
-
-
-def phase_table(nx, ny, ints, omega, refs):
-    slots = refs.shape[0]
-    return pl.pallas_call(
-        partial(phase_kernel, nx, ny),
-        out_shape=jax.ShapeDtypeStruct((slots, 2, nx, ny), bf16),
-        grid=(slots,),
-        in_specs=[
-            pl.BlockSpec(memory_space=pltpu.SMEM),
-            pl.BlockSpec(memory_space=pltpu.SMEM),
-            pl.BlockSpec((1, 8, 128), lambda i: (i, 0, 0)),
-        ],
-        out_specs=pl.BlockSpec((1, 2, nx, ny), lambda i: (i, 0, 0, 0)),
-        compiler_params=pltpu.CompilerParams(vmem_limit_bytes=vmem_bytes),
-        name="phase_table",
-    )(ints, omega, refs)
-
-
-def pack_kernel(
-    rows_here, hy, ints_ref, ref_ref, source, adjoint, slow_ref, coef_ref, plane, packed, same, other, slow, coef, sems
-):
-    forward, side, freq = ints_ref[1], ints_ref[2], ints_ref[3]
-    slow_copy = pltpu.make_async_copy(slow_ref, slow, sems.at[0])
-    coef_copy = pltpu.make_async_copy(coef_ref, coef, sems.at[1])
-
-    @pl.when(forward == 1)
-    def _():
-        pltpu.make_async_copy(source.at[freq], plane, sems.at[2]).start()
-
-    @pl.when(forward == 0)
-    def _():
-        pltpu.make_async_copy(adjoint.at[freq], plane, sems.at[2]).start()
-
-    slow_copy.start()
-    coef_copy.start()
-    slow_copy.wait()
-    coef_copy.wait()
-    level = jnp.full((16, hy), ref_ref[0], f32)
-    high = level.astype(bf16)
-    rest = level - high.astype(f32)
-    middle = rest.astype(bf16)
-    low = (rest - middle.astype(f32)).astype(bf16)
-    row = lax.broadcasted_iota(jnp.int32, (16, hy), 0)
-    parts = jnp.where(row == 0, high.astype(f32), jnp.where(row == 1, middle.astype(f32), low.astype(f32)))
-    parts = parts.astype(bf16)
-    for i, alone in enumerate((same, other)):
-        cols = pl.ds(pl.multiple_of((side ^ i) * hy, hy), hy)
-        c = coef[0, :, cols].astype(bf16)
-        d = (slow[0, :, cols] - ref_ref[0]).astype(bf16)
-        for out in (packed.at[i], alone):
-            out[pl.ds(0, rows_here), :] = c
-            out[pl.ds(rows_here, rows_here), :] = d
-            out[pl.ds(2 * rows_here, 16), :] = parts
-    pltpu.make_async_copy(source.at[freq], plane, sems.at[2]).wait()
-
-
-def run_pack(ints, slowness_ref, source_top, adjoint_bottom, slowness, correction):
-    rows_here, ny = slowness.shape[1:]
-    hy = ny // 2
-    half = jax.ShapeDtypeStruct((2 * rows_here + 16, hy), bf16)
-    return pl.pallas_call(
-        partial(pack_kernel, rows_here, hy),
-        out_shape=(
-            jax.ShapeDtypeStruct((2, rows_here, ny), bf16),
-            jax.ShapeDtypeStruct((2,) + half.shape, bf16),
-            half,
-            half,
-        ),
-        in_specs=[sm, sm] + [pl.BlockSpec(memory_space=pl.ANY)] * 4,
-        out_specs=(vm, vm, vm, vm),
-        scratch_shapes=[
-            pltpu.VMEM((1, rows_here, ny), f32),
-            pltpu.VMEM((1, rows_here, ny), f32),
-            pltpu.SemaphoreType.DMA((3,)),
-        ],
-        compiler_params=pltpu.CompilerParams(vmem_limit_bytes=60 * 1024 * 1024),
-        name="pack_rows",
-    )(ints, slowness_ref, source_top, adjoint_bottom, slowness, correction)
+                        out[part, rows, cols] = v.astype(bf16)
 
 
 def sort_kernel(rows_here, hy, sections, ints_ref, *refs):
-    blocks, (early, late, refs_out, coef_rows, ends) = refs[:sections], refs[sections:]
+    blocks, (pair, refs_out, coef_rows) = refs[:sections], refs[sections:]
     forward, side, group = ints_ref[1], ints_ref[2], ints_ref[4]
     half_sections = sections // 2
 
@@ -204,14 +123,13 @@
         for k in range(sections):
             pl.when(index == k)(partial(body, k))
 
-    for slot in range(sections - 1):
+    for slot in range(half_sections):
         depth = jnp.where(forward == 1, slot, sections - 1 - slot)
 
         def place(k, slot=slot):
             block = block_of(k)
             for j in range(2):
-                out = early.at[j, 0] if slot == 0 else late.at[j, slot - 1]
-                out[...] = block[pl.ds(j * rows_here, rows_here), :]
+                pair[j, slot] = block[pl.ds(j * rows_here, rows_here), :]
 
         chosen(group ^ depth, place)
     for slot in range(sections):
@@ -233,8 +151,6 @@
                 for j in range(2):
                     part = block[pl.ds(j * rows_here, rows_here), :]
                     coef_rows[j, :, cols] = part
-                    ends[0, j, :, cols] = part[rows_here - 1 :]
-                    ends[1, j, :, cols] = part[:1]
 
 
 def run_sort(ints, blocks, rows_here, hy):
@@ -242,14 +158,12 @@
     return pl.pallas_call(
         partial(sort_kernel, rows_here, hy, sections),
         out_shape=(
-            jax.ShapeDtypeStruct((2, 1, rows_here, hy), bf16),
-            jax.ShapeDtypeStruct((2, sections - 2, rows_here, hy), bf16),
+            jax.ShapeDtypeStruct((2, sections // 2, rows_here, hy), bf16),
             jax.ShapeDtypeStruct((sections, 8, 128), f32),
             jax.ShapeDtypeStruct((2, rows_here, 2 * hy), bf16),
-            jax.ShapeDtypeStruct((2, 2, 1, 2 * hy), bf16),
         ),
         in_specs=[sm] + [vm] * sections,
-        out_specs=(vm, vm, vm, vm, vm),
+        out_specs=(vm, vm, vm),
         compiler_params=pltpu.CompilerParams(vmem_limit_bytes=vmem_bytes),
         name="sort_depths",
     )(ints, *blocks)
@@ -284,8 +198,8 @@
             rows = pl.ds(par * hx, hx)
             zr = dot(qx_ref[2 + par], mid[0, rows, cols])
             zi = dot(qx_ref[2 + par], mid[1, rows, cols])
-            pr = phase[0, 0, rows, cols].astype(f32)
-            pi = phase[0, 1, rows, cols].astype(f32)
+            pr = phase[0, rows, cols].astype(f32)
+            pi = phase[1, rows, cols].astype(f32)
             yr = (zr * pr - zi * pi).astype(bf16)
             yi = (zr * pi + zi * pr).astype(bf16)
             back.append((dot(qx_ref[par], yr), dot(qx_ref[par], yi)))
@@ -302,10 +216,10 @@
             out[part, rows, pl.ds(hy, hy)] = (a - b).astype(bf16)
 
 
-def first_kernel(dims, orders, ints_ref, phase, qx_ref, qy_ref, *rest):
+def first_kernel(dims, orders, ints_ref, omega_ref, refs_ref, qx_ref, qy_ref, *rest):
     nx, ny, rows_here = dims
     counts = [len(o) for o in orders]
-    pieces, (out, folded, mid, spec) = rest[: sum(counts)], rest[sum(counts) :]
+    pieces, (out, folded, mid, spec, phase) = rest[: sum(counts)], rest[sum(counts) :]
     part_id, forward = ints_ref[0], ints_ref[1]
     at = 0
     for part, order in enumerate(orders):
@@ -329,6 +243,8 @@
 
     @pl.when(forward == 1)
     def _():
+        level = omega_ref[ints_ref[3]] * refs_ref[0, 0:1, 0:1]
+        fill_phase(nx, ny, level, 1.0, phase)
         transform(nx, ny, folded, phase, qx_ref, qy_ref, mid, spec, out)
 
 
@@ -350,27 +266,22 @@
         ref[part, pl.ds(nx + 8, 1), :] = ref[part, pl.ds(8, 1), :]
 
 
-def step_kernel(dims, orders, slot, last, ints_ref, omega_ref, w_ref, phase, qx_ref, qy_ref, *rest):
+def step_kernel(dims, orders, index, edges, last, ints_ref, omega_ref, w_ref, refs_ref, qx_ref, qy_ref, *rest):
     nx, ny, rows_here = dims
-    count = sum(len(o) for o in orders)
-    coefs, rest = (rest[:count], rest[count : 2 * count]), rest[2 * count :]
+    coefs, rest = rest[:2], rest[2:]
     if last:
-        coef_rows, before_row, after_row, out_rows, end_rows, out, plane, halo, folded, mid, spec, tall = rest
+        coef_rows, edge_rows, out_rows, end_rows, out, plane, halo, folded, mid, spec, phase, tall = rest
+    elif edges:
+        out, out_rows, edge_out, plane, halo, folded, mid, spec, phase = rest
     else:
-        out, out_rows, plane, halo, folded, mid, spec = rest
+        out, out_rows, plane, halo, folded, mid, spec, phase = rest
     part_id, forward, side = ints_ref[0], ints_ref[1], ints_ref[2]
     omega = omega_ref[ints_ref[3]]
     hy = ny // 2
     blocks = nx // rows_here
     place = []
-    at = 0
-    for order in orders:
-        where = {}
-        for piece_order in order:
-            for i, offset in enumerate(piece_order):
-                where[offset] = (at, i)
-            at += 1
-        place.append(where)
+    for which, order in enumerate(orders):
+        place.append({offset: which * blocks + i for i, offset in enumerate(sum(order, []))})
     step = min(32, rows_here)
 
     def portions():
@@ -381,12 +292,24 @@
 
     def lens_at(q, offset, sub):
         cols = pl.ds(pl.multiple_of((side ^ q) * hy, hy), hy)
-        (ca, ci), (da, di) = place[0][offset], place[1][offset]
         rows = pl.ds(sub, step)
-        c = coefs[q][ca][ci, slot, rows, :].astype(f32)
-        cos, sin = small_cos_sin(omega * coefs[q][da][di, slot, rows, :].astype(f32))
+        c = coefs[q][place[0][offset], rows, :].astype(f32)
+        cos, sin = small_cos_sin(omega * coefs[q][place[1][offset], rows, :].astype(f32))
         return cols, c, cos, sin
 
+    def keep_edges():
+        for i, (beside, first) in enumerate(((blocks - 1, rows_here - 16), (1, 0))):
+            wanted = part_id ^ lax.rem(part_id + beside, blocks)
+            for j in range(2):
+                at = jnp.int32(0)
+                for offset in range(blocks):
+                    at = jnp.where(wanted == offset, place[j][offset], at)
+                for q in range(2):
+                    cols = pl.ds(pl.multiple_of((side ^ q) * hy, hy), hy)
+                    edge_out[i, j, :, cols] = coefs[q][at, pl.ds(first, 16), :]
+
+    if edges:
+        keep_edges()
     chunk = 32
 
     @pl.when(forward == 1)
@@ -438,6 +361,7 @@
                 folded[part, rows, pl.ds(0, hy)] = (a + b).astype(bf16)
                 folded[part, rows, pl.ds(hy, hy)] = (flip * (a - b)).astype(bf16)
 
+    fill_phase(nx, ny, omega * refs_ref[index + 1, 0:1, 0:1], (2 * forward - 1).astype(f32), phase)
     transform(nx, ny, folded, phase, qx_ref, qy_ref, mid, spec, out)
     first = pl.multiple_of(part_id * rows_here, rows_here)
     mine = pl.ds(first, rows_here)
@@ -472,12 +396,12 @@
         tall[0, pl.ds(8, rows_here), :] = gr
         tall[1, pl.ds(8, rows_here), :] = gi
         _, _, gr, gi = scaled(
-            (out[0, before, :][15:16], out[1, before, :][15:16]), before_row[0], before_row[1]
+            (out[0, before, :][15:16], out[1, before, :][15:16]), edge_rows[0, 0, 15:16, :], edge_rows[0, 1, 15:16, :]
         )
         tall[0, pl.ds(7, 1), :] = gr
         tall[1, pl.ds(7, 1), :] = gi
         _, _, gr, gi = scaled(
-            (out[0, after, :][0:1], out[1, after, :][0:1]), after_row[0], after_row[1]
+            (out[0, after, :][0:1], out[1, after, :][0:1]), edge_rows[1, 0, 0:1, :], edge_rows[1, 1, 0:1, :]
         )
         tall[0, pl.ds(rows_here + 8, 1), :] = gr
         tall[1, pl.ds(rows_here + 8, 1), :] = gi
@@ -485,48 +409,67 @@
         end_rows[1] = (ui + laplace_rows(tall, 0, 0, rows_here)).astype(bf16)
 
 
-def phase_spec(slot, nx, ny):
-    return pl.BlockSpec((1, 2, nx, ny), lambda i: (slot, 0, 0, 0))
-
-
-def run_first(dims, orders, ints, phases, qx, qy, pieces):
+def run_first(dims, orders, ints, omega, refs, qx, qy, pieces):
     nx, ny, _ = dims
     return pl.pallas_call(
         partial(first_kernel, dims, orders),
         out_shape=jax.ShapeDtypeStruct((2, nx, ny), bf16),
-        grid=(1,),
-        in_specs=[sm, phase_spec(0, nx, ny), vm, vm] + [vm] * len(pieces),
+        in_specs=[sm, sm, vm, vm, vm] + [vm] * len(pieces),
         out_specs=vm,
-        scratch_shapes=[pltpu.VMEM((2, nx, ny), bf16)] * 3,
+        scratch_shapes=[pltpu.VMEM((2, nx, ny), bf16)] * 4,
         compiler_params=pltpu.CompilerParams(vmem_limit_bytes=vmem_bytes),
         cost_estimate=pl.CostEstimate(flops=2**30, bytes_accessed=2**22, transcendentals=0),
         name="first_step",
-    )(ints, phases, qx, qy, *pieces)
-
-
-def run_step(dims, orders, slot, index, ints, omega, w, coefs, phases, qx, qy, ends=None):
+    )(ints, omega, refs, qx, qy, *pieces)
+
+
+def run_step(dims, orders, index, ints, omega, w, coefs, refs, qx, qy, edges=False, ends=None):
     nx, ny, rows_here = dims
     last = ends is not None
     rows_shape = jax.ShapeDtypeStruct((2, rows_here, ny), bf16)
     full = pltpu.VMEM((2, nx, ny), bf16)
-    scratch = [pltpu.VMEM((2, nx, ny), f32), pltpu.VMEM((2, nx + 16, ny), f32), full, full, full]
+    scratch = [pltpu.VMEM((2, nx, ny), f32), pltpu.VMEM((2, nx + 16, ny), f32)]
+    scratch += [full] * 4
     if last:
         outs = (rows_shape, rows_shape)
         scratch = [full] + scratch + [pltpu.VMEM((2, rows_here + 16, ny), f32)]
     else:
         outs = (jax.ShapeDtypeStruct((2, nx, ny), bf16), rows_shape)
+        if edges:
+            outs += (jax.ShapeDtypeStruct((2, 2, 16, ny), bf16),)
     return pl.pallas_call(
-        partial(step_kernel, dims, orders, index, last),
+        partial(step_kernel, dims, orders, index, edges, last),
         out_shape=outs,
-        grid=(1,),
-        in_specs=[sm, sm, vm, phase_spec(slot + 1, nx, ny), vm, vm]
-        + [vm] * (len(coefs) + (3 if last else 0)),
-        out_specs=(vm, vm),
+        in_specs=[sm, sm] + [vm] * (8 if last else 6),
+        out_specs=(vm,) * len(outs),
         scratch_shapes=scratch,
         compiler_params=pltpu.CompilerParams(vmem_limit_bytes=vmem_bytes),
         cost_estimate=pl.CostEstimate(flops=2**32, bytes_accessed=2**24, transcendentals=0),
         name="end_step" if last else "depth_step",
-    )(ints, omega, w, phases, qx, qy, *coefs, *(ends or ()))
+    )(ints, omega, w, refs, qx, qy, *coefs, *(ends or ()))
+
+
+def join_kernel(counts, *refs):
+    pieces, outs = refs[: len(counts)], refs[len(counts) :]
+    for slot, out in enumerate(outs):
+        at = 0
+        for piece, count in zip(pieces, counts):
+            for i in range(count):
+                out[at + i] = piece[i, slot]
+            at += count
+
+
+def run_join(pieces):
+    _, slots, rows_here, hy = pieces[0].shape
+    counts = [piece.shape[0] for piece in pieces]
+    return pl.pallas_call(
+        partial(join_kernel, counts),
+        out_shape=[jax.ShapeDtypeStruct((sum(counts), rows_here, hy), bf16)] * slots,
+        in_specs=[vm] * len(pieces),
+        out_specs=[vm] * slots,
+        compiler_params=pltpu.CompilerParams(vmem_limit_bytes=vmem_bytes),
+        name="join_pieces",
+    )(*pieces)
 
 
 def image_kernel(freq_count, last_group, ints_ref, omega_ref, *refs):
@@ -635,51 +578,49 @@
     def pick(values, index):
         return lax.dynamic_index_in_dim(values, index, 0, keepdims=False)
 
-    plane, packed, same, other = run_pack(
-        ints, slowness_ref, source_top, adjoint_bottom, slowness, correction
-    )
+    plane = jnp.where(forward == 1, pick(source_top, freq), pick(adjoint_bottom, freq))
     planes = first_exchange(plane, "rows")
+    high = slowness_ref.astype(bf16)
+    middle = (slowness_ref - high.astype(f32)).astype(bf16)
+    low = (slowness_ref - high.astype(f32) - middle.astype(f32)).astype(bf16)
+    terms = jnp.concatenate([high, middle, low, jnp.zeros((13,), bf16)])
+    values = jnp.concatenate([correction[0], slowness[0] - slowness_ref[0]], 0).astype(bf16)
+    values = jnp.concatenate([values, jnp.broadcast_to(terms[:, None], (16, ny))], 0)
+    left, right = values[:, :hy], values[:, hy:]
+    same = jnp.where(side == 0, left, right)
+    other = jnp.where(side == 0, right, left)
+    packed = jnp.stack([same, other])
     blocks = [packed]
     for k in range(1, sections):
         blocks.append(swap(packed if k < half_sections else (same, other)[k % 2], "depth", k))
-    early, late, refs, coef_rows, ends = run_sort(ints, blocks, rows_here, hy)
-    early = first_exchange(early, "rows")
-    late = first_exchange(late, "rows")
-    phases = phase_table(nx, ny, ints, omega, refs)
-    rows_up = [(i, (i + 1) % row_parts) for i in range(row_parts)]
-    rows_down = [(j, i) for i, j in rows_up]
-    edges = [lax.ppermute(ends[0], "rows", rows_up), lax.ppermute(ends[1], "rows", rows_down)]
-
-    def both_sides(pieces, earlier):
-        mine, theirs = [], []
-        for have in pieces:
-            mine += have
-            theirs += [swap(piece, "depth", 1) for piece in have[:-1]]
-            theirs.append(swap(after(have[-1], earlier), "depth", 1))
-        return mine + theirs
-
+    pair, refs, coef_rows = run_sort(ints, blocks, rows_here, hy)
+    pieces = first_exchange(pair, "rows")
     qx, qy = basis_tables(nx), basis_tables(ny)
+    planes = after(planes, pair)
     for level in range(1, rounds):
         planes = next_exchange(planes, "rows", level)
-        early = after(early, (planes, (phases, edges)) if level == rounds - 1 else planes)
-        early = next_exchange(early, "rows", level)
-        if level < rounds - 1:
-            late = next_exchange(after(late, early), "rows", level)
-    w = run_first(dims, orders, ints, phases, qx, qy, planes[0] + planes[1])
-    late = next_exchange(after(late, w), "rows", rounds - 1)
-    coefs = both_sides(early, w)
-
+        before = pieces
+        pieces = next_exchange(after(pieces, planes), "rows", level)
+    w = run_first(dims, orders, ints, omega, refs, qx, qy, after(planes[0] + planes[1], before))
+    mine = list(run_join(after(pieces[0] + pieces[1], w)))
+    theirs = [swap(m, "depth", 1) for m in mine]
+    far = [swap(mine[sections - 1 - slot], "depth", half_sections) for slot in range(half_sections, sections - 1)]
     row_outs = []
+    edge_rows = None
     for slot in range(sections - 1):
-        ends = (coef_rows, *edges) if slot == sections - 2 else None
-        first, second = run_step(dims, orders, slot, max(slot - 1, 0), ints, omega, w, coefs, phases, qx, qy, ends)
-        if ends is None:
-            w = first
-            row_outs.append(second)
-            if slot == 0:
-                coefs = both_sides(late, w)
-        else:
-            row_outs += [first, second]
+        ends = (coef_rows, edge_rows) if slot == sections - 2 else None
+        w, *rest = run_step(
+            dims, orders, slot, ints, omega, w, (mine[slot], theirs[slot]), refs, qx, qy, slot == 0, ends
+        )
+        if slot == 0:
+            edge_rows = swap(rest.pop(), "depth", half_sections)
+        if slot == half_sections - 1:
+            far = after(far, w)
+            mine += far
+            theirs += [swap(m, "depth", 1) for m in far]
+        if ends:
+            rest.insert(0, w)
+        row_outs += rest
 
     def index_for(g, target):
         return target if g >= half_sections else sections - 2 - target

time: 83 us -> 72.7 us (0.88)
  waiting for transfers between devices: 15.3 us -> 25.1 us
  starting transfers between devices: 32 us -> 23.9 us
  local copies, waits for them, and re-layouts: 8.21 us -> 0.47 us
  Pallas kernels: 25.8 us -> 20.6 us
  other arithmetic: 0.38 us -> 1.52 us
    ppermute x37 -> x21, waiting for transfers between devices: 12.4 us -> 25.1 us  [swap(): return lax.ppermute(values, axis, [(i, i ^ mask) for i in range(size)])]
    unnamed x24 -> x8, local copies, waits for them, and re-layouts: 6.62 us -> 0.32 us
    pallas_call x5 -> x4, Pallas kernels: 23 us -> 17.9 us  [the longest x3 17.9 us: run_step(): pl.pallas_call(partial(step_kernel, dims, orders, index, edges, last), ou...]
    ppermute x2 -> x0, starting transfers between devices: 4.9 us -> none  [the longest x1 4.34 us: per_device(): lax.ppermute(ends[1], 'rows', rows_down)]
    ppermute x37 -> x21, starting transfers between devices: 27.1 us -> 23.9 us  [swap(): return lax.ppermute(values, axis, [(i, i ^ mask) for i in range(size)])]
    ppermute x2 -> x0, waiting for transfers between devices: 2.84 us -> none  [the longest x1 2.84 us: per_device(): lax.ppermute(ends[1], 'rows', rows_down)]
    sub x0 -> x1, other arithmetic: none -> 0.99 us  [per_device(): slowness[0] - slowness_ref[0]]
    slice x6 -> x4, local copies, waits for them, and re-layouts: 0.92 us -> 0.04 us  [first_exchange(): return [[pair[0:1], got[0:1]], [pair[1:2], got[1:2]]]]
  transfers between devices with their start and end apart: 39 -> 21, of which waited for: 12 -> 9; matrix products, arithmetic and copies ran while one was open for 1% -> 1% of each run, Pallas kernels for 20% -> 26%
where the time goes in v3:
time: 72.7 us; the launch traced here: 72.5 us
  waiting for transfers between devices  25.1 us (35%)
  starting transfers between devices  23.9 us (33%)
  Pallas kernels  20.6 us (28%)
  other arithmetic  1.52 us (2%)
  between operations  0.95 us (1%)
    ppermute x21, waiting for transfers between devices, swap(): return lax.ppermute(values, axis, [(i, i ^ mask) for i in range(size)])  25.1 us
    ppermute x21, starting transfers between devices, swap(): return lax.ppermute(values, axis, [(i, i ^ mask) for i in range(size)])  23.9 us
    pallas_call x3, Pallas kernels, run_step(): pl.pallas_call(partial(step_kernel, dims, orders, index, edges, last), ou...  17.9 us
  transfers between devices with their start and end apart: 21, of which 9 were waited for; matrix products, arithmetic and copies ran while one was open for 1% of the time, Pallas kernels for 26%

profile of v3, /device:TPU:0, one launch (start us, length us, event | category | flops | bytes accessed | tf_op | source)
XLA Modules:
  0.0 72.5 jit_solution(14517599480891678970)
XLA Ops:
  0.8 1.0 %fusion.4 = (bf16[64,512]{1,0:T(8,128)(2,1)S(1)}, bf16[64,512]{1,0:T(8,128)(2,1)S(1)}) fusion(f32[1,64,512]{2,1,0:T(8,128)} %param.10, f32[]{:T(128)} %bitcast.28, f32[1,64,512]{2,1,0:T(8,128)} %param.11), kind=kLoop, calls=%fused_computation.25 | loop fusion | flops 98304 | bytes 393220 | tf_op jit(solution)/shard_map/sub | solution.py:587
  1.9 3.0 %collective-permute-start.1 = (bf16[144,256]{1,0:T(8,128)(2,1)S(1)}, bf16[144,256]{1,0:T(8,128)(2,1)S(1)}, u32[]{:S(2)}, u32[]{:S(2)}) collective-permute-start(bf16[144,256]{1,0:T(8,128)(2,1)S(1)} %get-tuple-element.103), channel_id=1, source_target_pairs={{0,16},{8,24},{16,0},{24,8},{1,17},{9,25},{17,1},{25,9},{2,18},{10... | collective-permute-start | bytes 221192 | tf_op jit(solution)/shard_map/ppermute | solution.py:514
  5.2 3.1 %collective-permute-start.3 = (bf16[2,64,512]{2,1,0:T(8,128)(2,1)S(1)}, bf16[2,64,512]{2,1,0:T(8,128)(2,1)S(1)}, u32[]{:S(2)}, u32[]{:S(2)}) collective-permute-start(bf16[2,64,512]{2,1,0:T(8,128)(2,1)S(1)} %bitcast.34), channel_id=1, source_target_pairs={{0,4},{1,5},{2,6},{3,7},{4,0},{5,1},{6,2},{7,3},{8,12},{9,13},{10,... | collective-permute-start | bytes 393224 | tf_op jit(solution)/shard_map/ppermute | solution.py:514
  8.4 6.4 %collective-permute-done.3 = bf16[2,64,512]{2,1,0:T(8,128)(2,1)S(1)} collective-permute-done((bf16[2,64,512]{2,1,0:T(8,128)(2,1)S(1)}, bf16[2,64,512]{2,1,0:T(8,128)(2,1)S(1)}, u32[]{:S(2)}, u32[]{:S(2)}) %collective-permute-start.3) | collective-permute-done | bytes 131104 | tf_op jit(solution)/shard_map/ppermute | solution.py:514
  15.7 1.6 %collective-permute-start.6 = (bf16[2,64,512]{2,1,0:T(8,128)(2,1)S(1)}, bf16[2,64,512]{2,1,0:T(8,128)(2,1)S(1)}, u32[]{:S(2)}, u32[]{:S(2)}) collective-permute-start(bf16[2,64,512]{2,1,0:T(8,128)(2,1)S(1)} %pad_maximum_fusion.7), channel_id=1, source_target_pairs={{0,1},{1,0},{2,3},{3,2},{4,5},{5,4},{6,7},{7,6},{8,9},{9,8},{10,11... | collective-permute-start | bytes 393224 | tf_op jit(solution)/shard_map/ppermute | solution.py:514
  17.3 4.1 %collective-permute-start.4 = (bf16[2,64,512]{2,1,0:T(8,128)(2,1)S(1)}, bf16[2,64,512]{2,1,0:T(8,128)(2,1)S(1)}, u32[]{:S(2)}, u32[]{:S(2)}) collective-permute-start(bf16[2,64,512]{2,1,0:T(8,128)(2,1)S(1)} %pad_maximum_fusion.6), channel_id=1, source_target_pairs={{0,2},{1,3},{2,0},{3,1},{4,6},{5,7},{6,4},{7,5},{8,10},{9,11},{10,... | collective-permute-start | bytes 393224 | tf_op jit(solution)/shard_map/ppermute | solution.py:514
  21.5 2.9 %collective-permute-done.8 = bf16[2,2,64,256]{3,2,1,0:T(8,128)(2,1)S(1)} collective-permute-done((bf16[2,2,64,256]{3,2,1,0:T(8,128)(2,1)S(1)}, bf16[2,2,64,256]{3,2,1,0:T(8,128)(2,1)S(1)}, u32[]{:S(2)}, u32[]{:S(2)}) %collective-permute-start.8) | collective-permute-done | bytes 131104 | tf_op jit(solution)/shard_map/ppermute | solution.py:514
  24.4 1.5 %collective-permute-done.4.rest_2_ = bf16[2,64,512]{2,1,0:T(8,128)(2,1)S(1)} collective-permute-done((bf16[2,64,512]{2,1,0:T(8,128)(2,1)S(1)}, bf16[2,64,512]{2,1,0:T(8,128)(2,1)S(1)}, u32[]{:S(2)}, u32[]{:S(2)}) %collective-permute-start.4) | collective-permute-done | bytes 131104 | tf_op jit(solution)/shard_map/ppermute | solution.py:514
  27.1 1.6 %collective-permute-start.10 = (bf16[2,2,64,256]{3,2,1,0:T(8,128)(2,1)S(1)}, bf16[2,2,64,256]{3,2,1,0:T(8,128)(2,1)S(1)}, u32[]{:S(2)}, u32[]{:S(2)}) collective-permute-start(bf16[2,2,64,256]{3,2,1,0:T(8,128)(2,1)S(1)} %pad_maximum_fusion.9), channel_id=1, source_target_pairs={{0,1},{1,0},{2,3},{3,2},{4,5},{5,4},{6,7},{7,6},{8,9},{9,8},{10,11... | collective-permute-start | bytes 393224 | tf_op jit(solution)/shard_map/ppermute | solution.py:514
  28.7 1.6 %collective-permute-start.9 = (bf16[2,2,64,256]{3,2,1,0:T(8,128)(2,1)S(1)}, bf16[2,2,64,256]{3,2,1,0:T(8,128)(2,1)S(1)}, u32[]{:S(2)}, u32[]{:S(2)}) collective-permute-start(bf16[2,2,64,256]{3,2,1,0:T(8,128)(2,1)S(1)} %pad_maximum_fusion.8), channel_id=1, source_target_pairs={{0,2},{1,3},{2,0},{3,1},{4,6},{5,7},{6,4},{7,5},{8,10},{9,11},{10,... | collective-permute-start | bytes 393224 | tf_op jit(solution)/shard_map/ppermute | solution.py:514
  30.3 6.0 %collective-permute-done.10.refs_6_ = bf16[2,2,64,256]{3,2,1,0:T(8,128)(2,1)S(1)} collective-permute-done((bf16[2,2,64,256]{3,2,1,0:T(8,128)(2,1)S(1)}, bf16[2,2,64,256]{3,2,1,0:T(8,128)(2,1)S(1)}, u32[]{:S(2)}, u32[]{:S(2)}) %collective-permute-start.10) | collective-permute-done | bytes 131104 | tf_op jit(solution)/shard_map/ppermute | solution.py:514
  36.3 1.8 %collective-permute-start.12 = (bf16[4,2,64,256]{3,2,1,0:T(8,128)(2,1)S(1)}, bf16[4,2,64,256]{3,2,1,0:T(8,128)(2,1)S(1)}, u32[]{:S(2)}, u32[]{:S(2)}) collective-permute-start(bf16[4,2,64,256]{3,2,1,0:T(8,128)(2,1)S(1)} %pad_maximum_fusion.4), channel_id=1, source_target_pairs={{0,2},{1,3},{2,0},{3,1},{4,6},{5,7},{6,4},{7,5},{8,10},{9,11},{10,... | collective-permute-start | bytes 786440 | tf_op jit(solution)/shard_map/ppermute | solution.py:514
  38.8 0.7 first_step.1.w_ref
  39.5 3.2 %collective-permute-done.12.refs_7_ = bf16[4,2,64,256]{3,2,1,0:T(8,128)(2,1)S(1)} collective-permute-done((bf16[4,2,64,256]{3,2,1,0:T(8,128)(2,1)S(1)}, bf16[4,2,64,256]{3,2,1,0:T(8,128)(2,1)S(1)}, u32[]{:S(2)}, u32[]{:S(2)}) %collective-permute-start.12) | collective-permute-done | bytes 262176 | tf_op jit(solution)/shard_map/ppermute | solution.py:514
  42.7 1.8 %collective-permute-done.11.refs_3_ = bf16[4,2,64,256]{3,2,1,0:T(8,128)(2,1)S(1)} collective-permute-done((bf16[4,2,64,256]{3,2,1,0:T(8,128)(2,1)S(1)}, bf16[4,2,64,256]{3,2,1,0:T(8,128)(2,1)S(1)}, u32[]{:S(2)}, u32[]{:S(2)}) %collective-permute-start.11) | collective-permute-done | bytes 262176 | tf_op jit(solution)/shard_map/ppermute | solution.py:514
  45.2 1.5 %collective-permute-start.17 = (bf16[16,64,256]{2,1,0:T(8,128)(2,1)S(1)}, bf16[16,64,256]{2,1,0:T(8,128)(2,1)S(1)}, u32[]{:S(2)}, u32[]{:S(2)}) collective-permute-start(bf16[16,64,256]{2,1,0:T(8,128)(2,1)S(1)} %get-tuple-element.87.rest_0_), channel_id=1, source_target_pairs={{0,16},{8,24},{16,0},{24,8},{1,17},{9,25},{17,1},{25,9},{2,18},{10... | collective-permute-start | bytes 1572872 | tf_op jit(solution)/shard_map/ppermute | solution.py:514
  46.7 6.0 %depth_step.2 = (bf16[2,512,512]{2,1,0:T(8,128)(2,1)S(1)}, bf16[2,64,512]{2,1,0:T(8,128)(2,1)S(1)}, bf16[2,2,16,512]{3,2,1,0:T(8,128)(2,1)S(1)}) custom-call(s32[5]{0:T(128)S(1)} %stack.55.ints_ref, f32[2]{0:T(128)S(1)} %copy-done.1, bf16[2,512,512]{2,1,0:T(8,128)(2,1)S(1)} %first_step.1.w_ref, f32[4,8,128]{2,1,0:T(8,128)S(1)} %get-tuple-element.52.refs_ref, ...), custom_call_target="tpu_custom_call" | custom-call | flops 4294967296 | bytes 16777216 | tf_op jit(solution)/shard_map/depth_step/pallas_call | solution.py:440
  52.8 5.8 %depth_step.3 = (bf16[2,512,512]{2,1,0:T(8,128)(2,1)S(1)}, bf16[2,64,512]{2,1,0:T(8,128)(2,1)S(1)}) custom-call(s32[5]{0:T(128)S(1)} %stack.55.ints_ref, f32[2]{0:T(128)S(1)} %copy-done.1, bf16[2,512,512]{2,1,0:T(8,128)(2,1)S(1)} %get-tuple-element.86.w_ref, f32[4,8,128]{2,1,0:T(8,128)S(1)} %get-tuple-element.52.refs_ref, ...), custom_call_target="tpu_custom_call" | custom-call | flops 4294967296 | bytes 16777216 | tf_op jit(solution)/shard_map/depth_step/pallas_call | solution.py:440
  59.1 1.5 %collective-permute-start.19 = (bf16[2,2,16,512]{3,2,1,0:T(8,128)(2,1)S(1)}, bf16[2,2,16,512]{3,2,1,0:T(8,128)(2,1)S(1)}, u32[]{:S(2)}, u32[]{:S(2)}) collective-permute-start(bf16[2,2,16,512]{3,2,1,0:T(8,128)(2,1)S(1)} %get-tuple-element.92), channel_id=1, source_target_pairs={{0,16},{8,24},{16,0},{24,8},{1,17},{9,25},{17,1},{25,9},{2,18},{10... | collective-permute-start | bytes 196616 | tf_op jit(solution)/shard_map/ppermute | solution.py:514
  61.3 1.0 %collective-permute-start.16 = (bf16[2,64,512]{2,1,0:T(8,128)(2,1)S(1)}, bf16[2,64,512]{2,1,0:T(8,128)(2,1)S(1)}, u32[]{:S(2)}, u32[]{:S(2)}) collective-permute-start(bf16[2,64,512]{2,1,0:T(8,128)(2,1)S(1)} %get-tuple-element.101), channel_id=1, source_target_pairs={{0,24},{8,16},{16,8},{24,0},{1,25},{9,17},{17,9},{25,1},{2,26},{10... | collective-permute-start | bytes 393224 | tf_op jit(solution)/shard_map/ppermute | solution.py:514
  62.4 1.3 %collective-permute-done.19.rest_3_ = bf16[2,2,16,512]{3,2,1,0:T(8,128)(2,1)S(1)} collective-permute-done((bf16[2,2,16,512]{3,2,1,0:T(8,128)(2,1)S(1)}, bf16[2,2,16,512]{3,2,1,0:T(8,128)(2,1)S(1)}, u32[]{:S(2)}, u32[]{:S(2)}) %collective-permute-start.19) | collective-permute-done | bytes 65568 | tf_op jit(solution)/shard_map/ppermute | solution.py:514
  63.7 6.0 %end_step.1 = (bf16[2,64,512]{2,1,0:T(8,128)(2,1)S(1)}, bf16[2,64,512]{2,1,0:T(8,128)(2,1)S(1)}) custom-call(s32[5]{0:T(128)S(1)} %stack.55.ints_ref, f32[2]{0:T(128)S(1)} %copy-done.1, bf16[2,512,512]{2,1,0:T(8,128)(2,1)S(1)} %get-tuple-element.89.w_ref, f32[4,8,128]{2,1,0:T(8,128)S(1)} %get-tuple-element.52.refs_ref, bf16[4,256,256]{2,1,0:T(8,128)(2,1)S(1)} %copy-done.2, ...), custom_call_target="tpu_custom_call" | custom-call | flops 4294967296 | bytes 16777216 | tf_op jit(solution)/shard_map/end_step/pallas_call | solution.py:440
  69.9 1.3 %collective-permute-done.20.refs_1_ = bf16[2,64,512]{2,1,0:T(8,128)(2,1)S(1)} collective-permute-done((bf16[2,64,512]{2,1,0:T(8,128)(2,1)S(1)}, bf16[2,64,512]{2,1,0:T(8,128)(2,1)S(1)}, u32[]{:S(2)}, u32[]{:S(2)}) %collective-permute-start.20) | collective-permute-done | bytes 131104 | tf_op jit(solution)/shard_map/ppermute | solution.py:514
  71.3 1.3 %image.1 = f32[1,64,512]{2,1,0:T(8,128)} custom-call(s32[5]{0:T(128)S(1)} %stack.55.ints_ref, f32[2]{0:T(128)S(1)} %copy-done.1, bf16[2,64,512]{2,1,0:T(8,128)(2,1)S(1)} %get-tuple-element.95.refs_0_, bf16[2,64,512]{2,1,0:T(8,128)(2,1)S(1)} %collective-permute-done.20.refs_1_, bf16[2,64,512]{2,1,0:T(8,128)(2,1)S(1)} %collective-permute-done.15.refs_2_, ...), custom_call_target="tpu_custom_call" | custom-call | tf_op jit(solution)/shard_map/image/pallas_call | solution.py:502
  (56 shorter events, 5.5 us)
Async XLA Ops:
  1.9 3.3 %copy-start = (bf16[2,2,64,512]{3,2,1,0:T(8,128)(2,1)S(1)}, bf16[2,2,64,512]{3,2,1,0:T(8,128)(2,1)}, u32[]{:S(2)}) copy-start(bf16[2,2,64,512]{3,2,1,0:T(8,128)(2,1)} %refs_4_.1) | copy-start | bytes 786436
  1.9 3.3 %copy-start.3 = (bf16[2,2,64,512]{3,2,1,0:T(8,128)(2,1)S(1)}, bf16[2,2,64,512]{3,2,1,0:T(8,128)(2,1)}, u32[]{:S(2)}) copy-start(bf16[2,2,64,512]{3,2,1,0:T(8,128)(2,1)} %param.8) | copy-start | bytes 786436
  1.9 13.0 %collective-permute-start.1 = (bf16[144,256]{1,0:T(8,128)(2,1)S(1)}, bf16[144,256]{1,0:T(8,128)(2,1)S(1)}, u32[]{:S(2)}, u32[]{:S(2)}) collective-permute-start(bf16[144,256]{1,0:T(8,128)(2,1)S(1)} %get-tuple-element.103), channel_id=1, source_target_pairs={{0,16},{8,24},{16,0},{24,8},{1,17},{9,25},{17,1},{25,9},{2,18},{10... | collective-permute-start | bytes 221192 | tf_op jit(solution)/shard_map/ppermute | solution.py:514
  4.9 10.0 %collective-permute-start.2 = (bf16[144,256]{1,0:T(8,128)(2,1)S(1)}, bf16[144,256]{1,0:T(8,128)(2,1)S(1)}, u32[]{:S(2)}, u32[]{:S(2)}) collective-permute-start(bf16[144,256]{1,0:T(8,128)(2,1)S(1)} %get-tuple-element.104), channel_id=1, source_target_pairs={{0,24},{8,16},{16,8},{24,0},{1,25},{9,17},{17,9},{25,1},{2,26},{10... | collective-permute-start | bytes 221192 | tf_op jit(solution)/shard_map/ppermute | solution.py:514
  4.9 10.0 %collective-permute-start = (bf16[2,144,256]{2,1,0:T(8,128)(2,1)S(1)}, bf16[2,144,256]{2,1,0:T(8,128)(2,1)S(1)}, u32[]{:S(2)}, u32[]{:S(2)}) collective-permute-start(bf16[2,144,256]{2,1,0:T(8,128)(2,1)S(1)} %pad_maximum_fusion.5.refs_0_), channel_id=1, source_target_pairs={{0,8},{8,0},{16,24},{24,16},{1,9},{9,1},{17,25},{25,17},{2,10},{10... | collective-permute-start | bytes 442376 | tf_op jit(solution)/shard_map/ppermute | solution.py:514
  5.2 9.6 %collective-permute-start.3 = (bf16[2,64,512]{2,1,0:T(8,128)(2,1)S(1)}, bf16[2,64,512]{2,1,0:T(8,128)(2,1)S(1)}, u32[]{:S(2)}, u32[]{:S(2)}) collective-permute-start(bf16[2,64,512]{2,1,0:T(8,128)(2,1)S(1)} %bitcast.34), channel_id=1, source_target_pairs={{0,4},{1,5},{2,6},{3,7},{4,0},{5,1},{6,2},{7,3},{8,12},{9,13},{10,... | collective-permute-start | bytes 393224 | tf_op jit(solution)/shard_map/ppermute | solution.py:514
  15.6 8.8 %collective-permute-start.8 = (bf16[2,2,64,256]{3,2,1,0:T(8,128)(2,1)S(1)}, bf16[2,2,64,256]{3,2,1,0:T(8,128)(2,1)S(1)}, u32[]{:S(2)}, u32[]{:S(2)}) collective-permute-start(bf16[2,2,64,256]{3,2,1,0:T(8,128)(2,1)S(1)} %get-tuple-element.53), channel_id=1, source_target_pairs={{0,4},{1,5},{2,6},{3,7},{4,0},{5,1},{6,2},{7,3},{8,12},{9,13},{10,... | collective-permute-start | bytes 393224 | tf_op jit(solution)/shard_map/ppermute | solution.py:514
  15.7 8.7 %collective-permute-start.6 = (bf16[2,64,512]{2,1,0:T(8,128)(2,1)S(1)}, bf16[2,64,512]{2,1,0:T(8,128)(2,1)S(1)}, u32[]{:S(2)}, u32[]{:S(2)}) collective-permute-start(bf16[2,64,512]{2,1,0:T(8,128)(2,1)S(1)} %pad_maximum_fusion.7), channel_id=1, source_target_pairs={{0,1},{1,0},{2,3},{3,2},{4,5},{5,4},{6,7},{7,6},{8,9},{9,8},{10,11... | collective-permute-start | bytes 393224 | tf_op jit(solution)/shard_map/ppermute | solution.py:514
  17.3 8.5 %collective-permute-start.4 = (bf16[2,64,512]{2,1,0:T(8,128)(2,1)S(1)}, bf16[2,64,512]{2,1,0:T(8,128)(2,1)S(1)}, u32[]{:S(2)}, u32[]{:S(2)}) collective-permute-start(bf16[2,64,512]{2,1,0:T(8,128)(2,1)S(1)} %pad_maximum_fusion.6), channel_id=1, source_target_pairs={{0,2},{1,3},{2,0},{3,1},{4,6},{5,7},{6,4},{7,5},{8,10},{9,11},{10,... | collective-permute-start | bytes 393224 | tf_op jit(solution)/shard_map/ppermute | solution.py:514
  25.9 10.4 %collective-permute-start.7 = (bf16[4,64,512]{2,1,0:T(8,128)(2,1)S(1)}, bf16[4,64,512]{2,1,0:T(8,128)(2,1)S(1)}, u32[]{:S(2)}, u32[]{:S(2)}) collective-permute-start(bf16[4,64,512]{2,1,0:T(8,128)(2,1)S(1)} %pad_maximum_fusion.2), channel_id=1, source_target_pairs={{0,2},{1,3},{2,0},{3,1},{4,6},{5,7},{6,4},{7,5},{8,10},{9,11},{10,... | collective-permute-start | bytes 786440 | tf_op jit(solution)/shard_map/ppermute | solution.py:514
  26.5 9.7 %collective-permute-start.5 = (bf16[4,64,512]{2,1,0:T(8,128)(2,1)S(1)}, bf16[4,64,512]{2,1,0:T(8,128)(2,1)S(1)}, u32[]{:S(2)}, u32[]{:S(2)}) collective-permute-start(bf16[4,64,512]{2,1,0:T(8,128)(2,1)S(1)} %pad_maximum_fusion.1), channel_id=1, source_target_pairs={{0,1},{1,0},{2,3},{3,2},{4,5},{5,4},{6,7},{7,6},{8,9},{9,8},{10,11... | collective-permute-start | bytes 786440 | tf_op jit(solution)/shard_map/ppermute | solution.py:514
  27.1 9.1 %collective-permute-start.10 = (bf16[2,2,64,256]{3,2,1,0:T(8,128)(2,1)S(1)}, bf16[2,2,64,256]{3,2,1,0:T(8,128)(2,1)S(1)}, u32[]{:S(2)}, u32[]{:S(2)}) collective-permute-start(bf16[2,2,64,256]{3,2,1,0:T(8,128)(2,1)S(1)} %pad_maximum_fusion.9), channel_id=1, source_target_pairs={{0,1},{1,0},{2,3},{3,2},{4,5},{5,4},{6,7},{7,6},{8,9},{9,8},{10,11... | collective-permute-start | bytes 393224 | tf_op jit(solution)/shard_map/ppermute | solution.py:514
  28.7 9.8 %copy-start.2 = (bf16[4,256,256]{2,1,0:T(8,128)(2,1)S(1)}, bf16[4,256,256]{2,1,0:T(8,128)(2,1)}, u32[]{:S(2)}) copy-start(bf16[4,256,256]{2,1,0:T(8,128)(2,1)} %constant.49.clone.qx_ref.qy_ref) | copy-start | bytes 1572868
  28.7 7.5 %collective-permute-start.9 = (bf16[2,2,64,256]{3,2,1,0:T(8,128)(2,1)S(1)}, bf16[2,2,64,256]{3,2,1,0:T(8,128)(2,1)S(1)}, u32[]{:S(2)}, u32[]{:S(2)}) collective-permute-start(bf16[2,2,64,256]{3,2,1,0:T(8,128)(2,1)S(1)} %pad_maximum_fusion.8), channel_id=1, source_target_pairs={{0,2},{1,3},{2,0},{3,1},{4,6},{5,7},{6,4},{7,5},{8,10},{9,11},{10,... | collective-permute-start | bytes 393224 | tf_op jit(solution)/shard_map/ppermute | solution.py:514
  36.3 6.4 %collective-permute-start.12 = (bf16[4,2,64,256]{3,2,1,0:T(8,128)(2,1)S(1)}, bf16[4,2,64,256]{3,2,1,0:T(8,128)(2,1)S(1)}, u32[]{:S(2)}, u32[]{:S(2)}) collective-permute-start(bf16[4,2,64,256]{3,2,1,0:T(8,128)(2,1)S(1)} %pad_maximum_fusion.4), channel_id=1, source_target_pairs={{0,2},{1,3},{2,0},{3,1},{4,6},{5,7},{6,4},{7,5},{8,10},{9,11},{10,... | collective-permute-start | bytes 786440 | tf_op jit(solution)/shard_map/ppermute | solution.py:514
  38.1 6.4 %collective-permute-start.11 = (bf16[4,2,64,256]{3,2,1,0:T(8,128)(2,1)S(1)}, bf16[4,2,64,256]{3,2,1,0:T(8,128)(2,1)S(1)}, u32[]{:S(2)}, u32[]{:S(2)}) collective-permute-start(bf16[4,2,64,256]{3,2,1,0:T(8,128)(2,1)S(1)} %pad_maximum_fusion.3), channel_id=1, source_target_pairs={{0,1},{1,0},{2,3},{3,2},{4,5},{5,4},{6,7},{7,6},{8,9},{9,8},{10,11... | collective-permute-start | bytes 786440 | tf_op jit(solution)/shard_map/ppermute | solution.py:514
  44.6 2.1 %collective-permute-start.13 = (bf16[16,64,256]{2,1,0:T(8,128)(2,1)S(1)}, bf16[16,64,256]{2,1,0:T(8,128)(2,1)S(1)}, u32[]{:S(2)}, u32[]{:S(2)}) collective-permute-start(bf16[16,64,256]{2,1,0:T(8,128)(2,1)S(1)} %get-tuple-element.84.rest_0_), channel_id=1, source_target_pairs={{0,8},{8,0},{16,24},{24,16},{1,9},{9,1},{17,25},{25,17},{2,10},{10... | collective-permute-start | bytes 1572872 | tf_op jit(solution)/shard_map/ppermute | solution.py:514
  44.7 8.0 %collective-permute-start.14 = (bf16[16,64,256]{2,1,0:T(8,128)(2,1)S(1)}, bf16[16,64,256]{2,1,0:T(8,128)(2,1)S(1)}, u32[]{:S(2)}, u32[]{:S(2)}) collective-permute-start(bf16[16,64,256]{2,1,0:T(8,128)(2,1)S(1)} %get-tuple-element.87.rest_0_), channel_id=1, source_target_pairs={{0,8},{8,0},{16,24},{24,16},{1,9},{9,1},{17,25},{25,17},{2,10},{10... | collective-permute-start | bytes 1572872 | tf_op jit(solution)/shard_map/ppermute | solution.py:514
  45.2 13.9 %collective-permute-start.17 = (bf16[16,64,256]{2,1,0:T(8,128)(2,1)S(1)}, bf16[16,64,256]{2,1,0:T(8,128)(2,1)S(1)}, u32[]{:S(2)}, u32[]{:S(2)}) collective-permute-start(bf16[16,64,256]{2,1,0:T(8,128)(2,1)S(1)} %get-tuple-element.87.rest_0_), channel_id=1, source_target_pairs={{0,16},{8,24},{16,0},{24,8},{1,17},{9,25},{17,1},{25,9},{2,18},{10... | collective-permute-start | bytes 1572872 | tf_op jit(solution)/shard_map/ppermute | solution.py:514
  59.1 4.5 %collective-permute-start.18 = (bf16[16,64,256]{2,1,0:T(8,128)(2,1)S(1)}, bf16[16,64,256]{2,1,0:T(8,128)(2,1)S(1)}, u32[]{:S(2)}, u32[]{:S(2)}) collective-permute-start(bf16[16,64,256]{2,1,0:T(8,128)(2,1)S(1)} %collective-permute-done.17.rest_0_), channel_id=1, source_target_pairs={{0,8},{8,0},{16,24},{24,16},{1,9},{9,1},{17,25},{25,17},{2,10},{10... | collective-permute-start | bytes 1572872 | tf_op jit(solution)/shard_map/ppermute | solution.py:514
  59.1 4.5 %collective-permute-start.19 = (bf16[2,2,16,512]{3,2,1,0:T(8,128)(2,1)S(1)}, bf16[2,2,16,512]{3,2,1,0:T(8,128)(2,1)S(1)}, u32[]{:S(2)}, u32[]{:S(2)}) collective-permute-start(bf16[2,2,16,512]{3,2,1,0:T(8,128)(2,1)S(1)} %get-tuple-element.92), channel_id=1, source_target_pairs={{0,16},{8,24},{16,0},{24,8},{1,17},{9,25},{17,1},{25,9},{2,18},{10... | collective-permute-start | bytes 196616 | tf_op jit(solution)/shard_map/ppermute | solution.py:514
  60.7 9.1 %collective-permute-start.15 = (bf16[2,64,512]{2,1,0:T(8,128)(2,1)S(1)}, bf16[2,64,512]{2,1,0:T(8,128)(2,1)S(1)}, u32[]{:S(2)}, u32[]{:S(2)}) collective-permute-start(bf16[2,64,512]{2,1,0:T(8,128)(2,1)S(1)} %get-tuple-element.102), channel_id=1, source_target_pairs={{0,16},{8,24},{16,0},{24,8},{1,17},{9,25},{17,1},{25,9},{2,18},{10... | collective-permute-start | bytes 393224 | tf_op jit(solution)/shard_map/ppermute | solution.py:514
  61.3 8.5 %collective-permute-start.16 = (bf16[2,64,512]{2,1,0:T(8,128)(2,1)S(1)}, bf16[2,64,512]{2,1,0:T(8,128)(2,1)S(1)}, u32[]{:S(2)}, u32[]{:S(2)}) collective-permute-start(bf16[2,64,512]{2,1,0:T(8,128)(2,1)S(1)} %get-tuple-element.101), channel_id=1, source_target_pairs={{0,24},{8,16},{16,8},{24,0},{1,25},{9,17},{17,9},{25,1},{2,26},{10... | collective-permute-start | bytes 393224 | tf_op jit(solution)/shard_map/ppermute | solution.py:514
  69.8 1.4 %collective-permute-start.20 = (bf16[2,64,512]{2,1,0:T(8,128)(2,1)S(1)}, bf16[2,64,512]{2,1,0:T(8,128)(2,1)S(1)}, u32[]{:S(2)}, u32[]{:S(2)}) collective-permute-start(bf16[2,64,512]{2,1,0:T(8,128)(2,1)S(1)} %get-tuple-element.96), channel_id=1, source_target_pairs={{0,8},{8,0},{16,24},{24,16},{1,9},{9,1},{17,25},{25,17},{2,10},{10... | collective-permute-start | bytes 393224 | tf_op jit(solution)/shard_map/ppermute | solution.py:514
  (1 other events, 0.7 us)

commit v4 on v3

v4 whole, which is shorter than its diff:
```python
from functools import partial
import math

import jax
import jax.numpy as jnp
import numpy as np
from jax import lax
from jax.experimental import pallas as pl
from jax.experimental.pallas import tpu as pltpu
from jax.sharding import PartitionSpec as P

bf16 = jnp.bfloat16
f32 = jnp.float32
vmem_bytes = 32 * 1024 * 1024


def basis(length):
    half, quarter = length // 2, length // 4
    n = np.arange(half)[:, None]
    j = np.arange(quarter)[None, :]
    scale = math.sqrt(2.0 / length)
    even_cos = scale * np.cos(2 * np.pi * ((2 * j * n) % length) / length)
    even_sin = scale * np.sin(2 * np.pi * ((2 * j * n) % length) / length)
    even_cos[:, 0] = 1.0 / math.sqrt(length)
    even_sin[:, 0] = (1.0 - 2.0 * (np.arange(half) % 2)) / math.sqrt(length)
    odd_cos = scale * np.cos(2 * np.pi * (((2 * j + 1) * n) % length) / length)
    odd_sin = scale * np.sin(2 * np.pi * (((2 * j + 1) * n) % length) / length)
    even = np.concatenate([even_cos, even_sin], 1).astype(np.float32)
    odd = np.concatenate([odd_cos, odd_sin], 1).astype(np.float32)
    return even, odd


def basis_tables(length):
    even, odd = basis(length)
    half = length // 2
    near = np.eye(half, k=1) + np.eye(half, k=-1)
    across = np.eye(half, k=half - 1) + np.eye(half, k=1 - half)
    tables = [even, odd, even.T, odd.T, near - 4.0 * np.eye(half), near, across]
    return jnp.asarray(np.stack(tables).astype(np.float32), bf16)


def dot(a, b):
    return jnp.dot(a, b, preferred_element_type=f32)


def fitted(function, top, degree):
    fit = np.polynomial.Chebyshev.interpolate(function, degree, [0.0, top])
    return [float(c) for c in fit.convert(kind=np.polynomial.Polynomial).coef]


def horner(coefs, x):
    total = coefs[-1] * x + coefs[-2]
    for c in coefs[-3::-1]:
        total = total * x + c
    return total


def sinc_root(x):
    return np.sinc(np.sqrt(x) / np.pi)


def cos_root(x):
    return np.cos(np.sqrt(x))


lens_top = 0.45
lens_cos, lens_sin = fitted(cos_root, lens_top, 3), fitted(sinc_root, lens_top, 3)
phase_top = 3.2
phase_cos, phase_sin = fitted(cos_root, phase_top, 7), fitted(sinc_root, phase_top, 7)


def small_cos_sin(a):
    s = a * a
    return horner(lens_cos, s), a * horner(lens_sin, s)


def fill_phase(nx, ny, level, sign, out):
    qx, qy = nx // 4, ny // 4

    def waves(rows, cols, axis, parity, length):
        j = lax.broadcasted_iota(jnp.int32, (rows, cols), axis)
        return (2 * j + parity).astype(f32) * (2.0 * math.pi / length)

    def values(kx, ky):
        squared = level * level - kx * kx - ky * ky
        inside = jnp.maximum(squared, 0.0)
        damping = jnp.exp(-jnp.sqrt(jnp.maximum(-squared, 0.0)))
        sine = jnp.sqrt(inside) * horner(phase_sin, inside)
        return damping * horner(phase_cos, inside), sign * damping * sine

    edge = math.pi
    row_zero = lax.broadcasted_iota(jnp.int32, (qx, qy), 0) == 0
    col_zero = lax.broadcasted_iota(jnp.int32, (qx, qy), 1) == 0
    for px in range(2):
        for py in range(2):
            kx = waves(qx, qy, 0, px, nx)
            ky = waves(qx, qy, 1, py, ny)
            base = values(kx, ky)
            across = values(jnp.full((8, qy), edge), waves(8, qy, 1, py, ny))
            along = values(waves(qx, 1, 0, px, nx), jnp.full((qx, 1), edge))
            corner = values(jnp.full((8, 1), edge), jnp.full((8, 1), edge))
            for sx in range(2):
                for sy in range(2):
                    new_row, new_col = sx and not px, sy and not py
                    for part in range(2):
                        v = base[part]
                        if new_col:
                            v = jnp.where(col_zero, along[part], v)
                        if new_row:
                            v = jnp.where(row_zero, across[part][0:1], v)
                        if new_row and new_col:
                            v = jnp.where(row_zero & col_zero, corner[part][0:1], v)
                        rows = pl.ds((2 * px + sx) * qx, qx)
                        cols = pl.ds((2 * py + sy) * qy, qy)
                        out[part, rows, cols] = v.astype(bf16)


def place_of(plan):
    sections, freq_count = plan
    group = lax.axis_index("depth")
    chain = lax.div(group, jnp.int32(sections // (2 * freq_count)))
    forward = lax.div(chain, jnp.int32(freq_count))
    freq = lax.rem(chain, jnp.int32(freq_count))
    return lax.axis_index("rows"), forward, lax.rem(group, jnp.int32(2)), freq, group


vm = pl.BlockSpec(memory_space=pltpu.VMEM)
sm = pl.BlockSpec(memory_space=pltpu.SMEM)


def sort_kernel(rows_here, hy, plan, omega_ref, *refs):
    sections, freq_count = plan
    half_sections = sections // 2
    blocks, refs = refs[:sections], refs[sections:]
    partner, (pair, refs_out, coef_rows) = refs[:half_sections], refs[half_sections:]
    _, forward, side, freq, group = place_of(plan)
    omega = omega_ref[freq]
    for i in range(freq_count):
        refs_out[sections + i] = jnp.full((8, 128), omega_ref[freq ^ i], f32)

    def block_of(k):
        return blocks[k].at[k % 2] if k < half_sections else blocks[k]

    def chosen(index, first, body):
        for k in range(first, sections):
            pl.when(index == k)(partial(body, k))

    for slot in range(half_sections):
        depth = jnp.where(forward == 1, slot, sections - 1 - slot)

        def place(k, slot=slot):
            for j in range(2):
                part = pl.ds(j * rows_here, rows_here)
                pair[j, 0, slot] = blocks[k][part, :]
                pair[j, 1, slot] = partner[k - half_sections][part, :]

        chosen(group ^ depth, half_sections, place)
    for slot in range(sections):
        depth = jnp.where(forward == 1, slot, (sections - slot) % sections)

        def level(k, slot=slot):
            parts = block_of(k)[pl.ds(2 * rows_here, 16), pl.ds(0, 128)].astype(f32)
            refs_out[slot] = jnp.broadcast_to(omega * (parts[0:1] + parts[1:2] + parts[2:3]), (8, 128))

        chosen(group ^ depth, 0, level)

    for k in range(half_sections):

        @pl.when(jnp.clip(group ^ (sections - 1), 0, half_sections - 1) == k)
        def _(k=k):
            for i in range(2):
                cols = pl.ds(pl.multiple_of((side ^ (k % 2) ^ i) * hy, hy), hy)
                block = blocks[k].at[i]
                for j in range(2):
                    coef_rows[j, :, cols] = block[pl.ds(j * rows_here, rows_here), :]


def run_sort(omega, blocks, partner, rows_here, hy):
    sections = len(blocks)
    return pl.pallas_call(
        partial(sort_kernel, rows_here, hy, (sections, omega.shape[0])),
        out_shape=(
            jax.ShapeDtypeStruct((2, 2, sections // 2, rows_here, hy), bf16),
            jax.ShapeDtypeStruct((sections + omega.shape[0], 8, 128), f32),
            jax.ShapeDtypeStruct((2, rows_here, 2 * hy), bf16),
        ),
        in_specs=[sm] + [vm] * (sections + len(partner)),
        out_specs=(vm, vm, vm),
        compiler_params=pltpu.CompilerParams(vmem_limit_bytes=vmem_bytes),
        name="sort_depths",
    )(omega, *blocks, *partner)


def fold_cols(values):
    half = values.shape[1] // 2
    a, b = values[:, :half], values[:, half:]
    return (a + b).astype(bf16), (a - b).astype(bf16)


def add_subtract(mid, part, par, hx, hy, top, low):
    cols = pl.ds(par * hy, hy)
    mid[part, pl.ds(0, hx), cols] = (top + low).astype(bf16)
    mid[part, pl.ds(hx, hx), cols] = (top - low).astype(bf16)


def forward_rows(nx, ny, folded, qy_ref, mid):
    hx, hy = nx // 2, ny // 2
    for part in range(2):
        for par in range(2):
            cols = pl.ds(par * hy, hy)
            top = dot(folded[part, pl.ds(0, hx), cols], qy_ref[par])
            low = dot(folded[part, pl.ds(hx, hx), cols], qy_ref[par])
            add_subtract(mid, part, par, hx, hy, top, low)


def through_columns(nx, ny, mid, phase, qx_ref, spec):
    hx, hy = nx // 2, ny // 2
    for start in range(0, ny, hy):
        cols = pl.ds(start, hy)
        back = []
        for par in range(2):
            rows = pl.ds(par * hx, hx)
            zr = dot(qx_ref[2 + par], mid[0, rows, cols])
            zi = dot(qx_ref[2 + par], mid[1, rows, cols])
            pr = phase[0, rows, cols].astype(f32)
            pi = phase[1, rows, cols].astype(f32)
            yr = (zr * pr - zi * pi).astype(bf16)
            yi = (zr * pi + zi * pr).astype(bf16)
            back.append((dot(qx_ref[par], yr), dot(qx_ref[par], yi)))
        for part in range(2):
            a, b = back[0][part], back[1][part]
            spec[part, pl.ds(0, hx), cols] = (a + b).astype(bf16)
            spec[part, pl.ds(hx, hx), cols] = (a - b).astype(bf16)


def inverse_rows(ny, pieces, spec, qy_ref, out):
    hy = ny // 2
    for part in range(2):
        for start, count in pieces:
            rows = pl.ds(start, count)
            a = dot(spec[part, rows, pl.ds(0, hy)], qy_ref[2])
            b = dot(spec[part, rows, pl.ds(hy, hy)], qy_ref[3])
            out[part, rows, pl.ds(0, hy)] = (a + b).astype(bf16)
            out[part, rows, pl.ds(hy, hy)] = (a - b).astype(bf16)


def laplace_block(src, part, block, hx, hy, qx_ref, qy_ref):
    rows = pl.ds(block * hx, hx)
    left, right = src[part, rows, pl.ds(0, hy)], src[part, rows, pl.ds(hy, hy)]
    sums = []
    for own, other in ((left, right), (right, left)):
        sums.append(dot(qx_ref[4], own) + dot(own, qy_ref[5]) + dot(other, qy_ref[6]))
    return sums


def half_ends(nx):
    hx = nx // 2
    return [(0, nx - 1), (hx - 1, hx), (hx, hx - 1), (nx - 1, 0)]


def one_row(src, part, row):
    return src[part, pl.ds(row // 16 * 16, 16), :].astype(f32)[row % 16 : row % 16 + 1]


def first_kernel(dims, orders, plan, refs_ref, tables, *rest):
    nx, ny, rows_here = dims
    counts = [len(o) for o in orders]
    pieces, (out, folded, mid, spec, phase) = rest[: sum(counts)], rest[sum(counts) :]
    qx_ref = qy_ref = tables
    part_id, forward, _, _, _ = place_of(plan)
    at = 0
    for part, order in enumerate(orders):
        for piece_order in order:
            piece = pieces[at]
            at += 1
            for i, offset in enumerate(piece_order):
                block = part_id ^ offset
                rows = pl.ds(pl.multiple_of(block * rows_here, rows_here), rows_here)
                values = piece[i]

                @pl.when(forward == 1)
                def _():
                    a, b = fold_cols(values.astype(f32))
                    folded[part, rows, pl.ds(0, ny // 2)] = a
                    folded[part, rows, pl.ds(ny // 2, ny // 2)] = b

                @pl.when(forward == 0)
                def _():
                    out[part, rows, :] = values

    @pl.when(forward == 1)
    def _():
        fill_phase(nx, ny, refs_ref[0, 0:1, 0:1], 1.0, phase)
        forward_rows(nx, ny, folded, qy_ref, mid)
        through_columns(nx, ny, mid, phase, qx_ref, spec)
        inverse_rows(ny, [(start, nx // 2) for start in (0, nx // 2)], spec, qy_ref, out)


def laplace_rows(ref, part, start, count):
    center = ref[part, pl.ds(start + 8, count), :]
    width = center.shape[1]
    return (
        ref[part, pl.ds(start + 7, count), :]
        + ref[part, pl.ds(start + 9, count), :]
        + pltpu.roll(center, 1, 1)
        + pltpu.roll(center, width - 1, 1)
        - 4.0 * center
    )


def step_kernel(dims, orders, plan, index, parts, last, w_ref, refs_ref, tables, *rest):
    nx, ny, rows_here = dims
    qx_ref = qy_ref = tables
    coefs, rest = rest[: 2 * parts], rest[2 * parts :]
    coefs = (coefs[:parts], coefs[parts:])
    if last:
        coef_rows, out_rows, end_rows, out, plane, scaled, mid, spec, phase, tall, edge_rows = rest
    else:
        out, out_rows, plane, scaled, mid, spec, phase = rest
    part_id, forward, side, _, _ = place_of(plan)
    omega = refs_ref[plan[0], 0:1, 0:1]
    hy = ny // 2
    blocks = nx // rows_here
    place = []
    for which, order in enumerate(orders):
        share = blocks // parts
        place.append(
            {o: (i // share, which * share + i % share) for i, o in enumerate(sum(order, []))}
        )
    step = min(32, rows_here)

    def portions():
        for offset in range(blocks):
            for sub in range(0, rows_here, step):
                start = pl.multiple_of((part_id ^ offset) * rows_here + sub, step)
                yield offset, sub, start

    def lens_at(q, offset, sub):
        cols = pl.ds(pl.multiple_of((side ^ q) * hy, hy), hy)
        rows = pl.ds(sub, step)
        (ca, ci), (da, di) = place[0][offset], place[1][offset]
        c = coefs[q][ca][ci, rows, :].astype(f32)
        cos, sin = small_cos_sin(omega * coefs[q][da][di, rows, :].astype(f32))
        return cols, c, cos, sin

    hx = nx // 2
    first = pl.multiple_of(part_id * rows_here, rows_here)
    mine = pl.ds(first, rows_here)

    @pl.when(forward == 1)
    def _():
        for offset, sub, start in portions():
            rows = pl.ds(start, step)
            for q in range(2):
                cols, c, lr, li = lens_at(q, offset, sub)
                wr, wi = w_ref[0, rows, cols].astype(f32), w_ref[1, rows, cols].astype(f32)
                ur, ui = wr * lr - wi * li, wr * li + wi * lr
                plane[0, rows, cols] = ur
                plane[1, rows, cols] = ui
                scaled[0, rows, cols] = (c * ur).astype(bf16)
                scaled[1, rows, cols] = (c * ui).astype(bf16)
        for row, beside in half_ends(nx):
            plane[0, pl.ds(row, 1), :] -= one_row(scaled, 1, beside)
            plane[1, pl.ds(row, 1), :] += one_row(scaled, 0, beside)
        spectra = []
        for block in range(2):
            rows = pl.ds(block * hx, hx)
            sums = [laplace_block(scaled, part, block, hx, hy, qx_ref, qy_ref) for part in range(2)]
            for part in range(2):
                left, right = plane[part, rows, pl.ds(0, hy)], plane[part, rows, pl.ds(hy, hy)]
                l, r = sums[1 - part]
                left, right = (left + l, right + r) if part else (left - l, right - r)
                spec[part, rows, pl.ds(0, hy)] = left.astype(bf16)
                spec[part, rows, pl.ds(hy, hy)] = right.astype(bf16)
                spectra.append(
                    (
                        dot((left + right).astype(bf16), qy_ref[0]),
                        dot((left - right).astype(bf16), qy_ref[1]),
                    )
                )
        for part in range(2):
            for par in range(2):
                add_subtract(mid, part, par, hx, hy, spectra[part][par], spectra[2 + part][par])
        for part in range(2):
            out_rows[part] = spec[part, mine, :]

    @pl.when(forward == 0)
    def _():
        for part in range(2):
            for block in range(2):
                rows = pl.ds(block * hx, hx)
                l, r = laplace_block(w_ref, part, block, hx, hy, qx_ref, qy_ref)
                plane[part, rows, pl.ds(0, hy)] = l
                plane[part, rows, pl.ds(hy, hy)] = r
            for row, beside in half_ends(nx):
                plane[part, pl.ds(row, 1), :] += one_row(w_ref, part, beside)
        flip = (1 - 2 * side).astype(f32)
        for offset, sub, start in portions():
            rows = pl.ds(start, step)
            halves = []
            for q in range(2):
                cols, c, lr, li = lens_at(q, offset, sub)
                tr = w_ref[0, rows, cols].astype(f32) + c * plane[1, rows, cols]
                ti = w_ref[1, rows, cols].astype(f32) - c * plane[0, rows, cols]
                halves.append((tr * lr + ti * li, ti * lr - tr * li))
            for part in range(2):
                a, b = halves[0][part], halves[1][part]
                scaled[part, rows, pl.ds(0, hy)] = (a + b).astype(bf16)
                scaled[part, rows, pl.ds(hy, hy)] = (flip * (a - b)).astype(bf16)
        forward_rows(nx, ny, scaled, qy_ref, mid)

    fill_phase(nx, ny, refs_ref[index + 1, 0:1, 0:1], (2 * forward - 1).astype(f32), phase)
    through_columns(nx, ny, mid, phase, qx_ref, spec)
    before_start = pl.multiple_of(lax.rem(first + nx - 16, nx), 16)
    after_start = pl.multiple_of(lax.rem(first + rows_here, nx), 16)
    if last:
        wanted = [(first, rows_here), (before_start, 16), (after_start, 16)]
    else:
        wanted = [(start, hx) for start in (0, hx)]
    inverse_rows(ny, wanted, spec, qy_ref, out)

    @pl.when(forward == 0)
    def _():
        for part in range(2):
            out_rows[part] = out[part, mine, :]

    if not last:
        return
    for q in range(2):
        cols = pl.ds(pl.multiple_of((side ^ q) * hy, hy), hy)
        for i in range(2):
            for j in range(2):
                row = (2 * i + j) * 16
                rows = pl.ds(row % rows_here, 16)
                edge_rows[i, j, :, cols] = coefs[q][-1][2 * (blocks // parts) + row // rows_here, rows, :]

    @pl.when(forward == 0)
    def _():
        end_rows[...] = jnp.zeros_like(end_rows)

    @pl.when(forward == 1)
    def _():
        before = pl.ds(before_start, 16)
        after = pl.ds(after_start, 16)

        def lensed(values, c, d):
            lr, li = small_cos_sin(omega * d.astype(f32))
            wr, wi = values[0].astype(f32), values[1].astype(f32)
            ur, ui = wr * lr - wi * li, wr * li + wi * lr
            cf = c.astype(f32)
            return ur, ui, cf * ur, cf * ui

        ur, ui, gr, gi = lensed(
            (out[0, mine, :], out[1, mine, :]), coef_rows[0], coef_rows[1]
        )
        tall[0, pl.ds(8, rows_here), :] = gr
        tall[1, pl.ds(8, rows_here), :] = gi
        _, _, gr, gi = lensed(
            (out[0, before, :][15:16], out[1, before, :][15:16]), edge_rows[0, 0, 15:16, :], edge_rows[0, 1, 15:16, :]
        )
        tall[0, pl.ds(7, 1), :] = gr
        tall[1, pl.ds(7, 1), :] = gi
        _, _, gr, gi = lensed(
            (out[0, after, :][0:1], out[1, after, :][0:1]), edge_rows[1, 0, 0:1, :], edge_rows[1, 1, 0:1, :]
        )
        tall[0, pl.ds(rows_here + 8, 1), :] = gr
        tall[1, pl.ds(rows_here + 8, 1), :] = gi
        end_rows[0] = (ur - laplace_rows(tall, 1, 0, rows_here)).astype(bf16)
        end_rows[1] = (ui + laplace_rows(tall, 0, 0, rows_here)).astype(bf16)


def run_first(dims, orders, plan, refs, tables, pieces):
    nx, ny, _ = dims
    return pl.pallas_call(
        partial(first_kernel, dims, orders, plan),
        out_shape=jax.ShapeDtypeStruct((2, nx, ny), bf16),
        in_specs=[vm, vm] + [vm] * len(pieces),
        out_specs=vm,
        scratch_shapes=[pltpu.VMEM((2, nx, ny), bf16)] * 4,
        compiler_params=pltpu.CompilerParams(vmem_limit_bytes=vmem_bytes),
        cost_estimate=pl.CostEstimate(flops=2**30, bytes_accessed=2**22, transcendentals=0),
        name="first_step",
    )(refs, tables, *pieces)


def run_step(dims, orders, plan, index, w, coefs, refs, tables, coef_rows=None):
    nx, ny, rows_here = dims
    last = coef_rows is not None
    rows_shape = jax.ShapeDtypeStruct((2, rows_here, ny), bf16)
    full = pltpu.VMEM((2, nx, ny), bf16)
    scratch = [pltpu.VMEM((2, nx, ny), f32)]
    scratch += [full] * 4
    if last:
        outs = (rows_shape, rows_shape)
        scratch = [full] + scratch + [pltpu.VMEM((2, rows_here + 16, ny), f32)]
        scratch += [pltpu.VMEM((2, 2, 16, ny), bf16)]
    else:
        outs = (jax.ShapeDtypeStruct((2, nx, ny), bf16), rows_shape)
    return pl.pallas_call(
        partial(step_kernel, dims, orders, plan, index, len(coefs) // 2, last),
        out_shape=outs,
        in_specs=[vm] * (3 + len(coefs) + (1 if last else 0)),
        out_specs=(vm,) * len(outs),
        scratch_shapes=scratch,
        compiler_params=pltpu.CompilerParams(vmem_limit_bytes=vmem_bytes),
        cost_estimate=pl.CostEstimate(flops=2**32, bytes_accessed=2**24, transcendentals=0),
        name="end_step" if last else "depth_step",
    )(w, refs, tables, *coefs, *([coef_rows] if last else []))


def join_kernel(counts, wanted, sides, *refs):
    count = len(counts)
    kept = (len(refs) - count - len(wanted)) // 2
    pieces, outs = refs[kept : kept + count], refs[2 * kept + count :]
    for (slot, chosen), out in zip(wanted, outs):
        at = 0
        for which in chosen:
            for i in range(counts[which]):
                out[at + i] = pieces[which][i, slot]
            at += counts[which]
    if not sides:
        return
    rows_here = pieces[0].shape[2]
    size = sum(counts) // 2
    part_id = lax.axis_index("rows")
    for i, (beside, first) in enumerate(((size - 1, rows_here - 16), (1, 0))):
        offset_wanted = part_id ^ lax.rem(part_id + beside, size)
        for j, (order, chosen) in enumerate(sides):
            places = [(which, k) for which in chosen for k in range(counts[which])]
            row = (2 * i + j) * 16
            target = outs[-1].at[at + row // rows_here, pl.ds(row % rows_here, 16)]
            for offset, (which, k) in zip(order, places):

                @pl.when(offset_wanted == offset)
                def _(which=which, k=k, first=first, target=target):
                    target[...] = pieces[which][k, 0, pl.ds(first, 16), :]


def run_join(pieces, wanted, kept=(), sides=()):
    _, _, rows_here, hy = pieces[0].shape
    counts = [piece.shape[0] for piece in pieces]
    shapes = [(sum(counts[i] for i in chosen), rows_here, hy) for _, chosen in wanted]
    if sides:
        shapes[-1] = (shapes[-1][0] + -(-64 // rows_here), rows_here, hy)
    return pl.pallas_call(
        partial(join_kernel, counts, wanted, sides),
        out_shape=[jax.ShapeDtypeStruct(k.shape, k.dtype) for k in kept]
        + [jax.ShapeDtypeStruct(shape, bf16) for shape in shapes],
        in_specs=[vm] * (len(kept) + len(pieces)),
        out_specs=[vm] * (len(kept) + len(shapes)),
        input_output_aliases={i: i for i in range(len(kept))},
        compiler_params=pltpu.CompilerParams(vmem_limit_bytes=vmem_bytes),
        cost_estimate=pl.CostEstimate(flops=0, bytes_accessed=2**18, transcendentals=0),
        name="join_pieces",
    )(*kept, *pieces)


def image_kernel(plan, refs_ref, *refs):
    sections, freq_count = plan
    fields, (bottom, out) = refs[:-2], refs[-2:]
    _, forward, _, freq, group = place_of(plan)

    def total(adjoint_at):
        result = None
        for i in range(freq_count):
            freq_i = freq ^ i
            adjoint = adjoint_at(i, freq_i)
            a = [fields[i][j].astype(f32) for j in range(2)]
            b = [adjoint[j].astype(f32) for j in range(2)]
            weight = refs_ref[sections + i, 0:1, 0:1] * (2 * forward - 1).astype(f32)
            term = weight * (a[0] * b[1] - a[1] * b[0])
            result = term if result is None else result + term
        out[0] = result

    @pl.when(group == sections - 1)
    def _():
        total(lambda i, freq_i: bottom.at[freq_i])

    @pl.when(group != sections - 1)
    def _():
        total(lambda i, freq_i: fields[freq_count + i])


def run_image(plan, refs, fields, bottom):
    _, rows_here, ny = fields[0].shape
    return pl.pallas_call(
        partial(image_kernel, plan),
        out_shape=jax.ShapeDtypeStruct((1, rows_here, ny), f32),
        in_specs=[vm] * (len(fields) + 2),
        out_specs=vm,
        compiler_params=pltpu.CompilerParams(vmem_limit_bytes=vmem_bytes),
        name="image",
    )(refs, *fields, bottom)


def swap(values, axis, mask):
    axes = axis if isinstance(axis, tuple) else (axis,)
    size = math.prod(lax.axis_size(a) for a in axes)
    return lax.ppermute(values, axis, [(i, i ^ mask) for i in range(size)])


def doubling_masks(size):
    masks = []
    mask = size // 2
    while mask:
        masks.append(mask)
        mask //= 2
    descending = masks
    ascending = masks[:1] + masks[1:][::-1]
    return descending, ascending


def doubling_orders(masks):
    orders = [[0]]
    seen = [0]
    for mask in masks:
        new = [mask ^ o for o in seen]
        orders.append(new)
        seen = seen + new
    return orders


def first_exchange(pair, axis):
    size = lax.axis_size(axis)
    got = swap(pair, axis, size // 2)
    return [[pair[0:1], got[0:1]], [pair[1:2], got[1:2]]]


def after(values, earlier):
    return lax.optimization_barrier((values, earlier))[0]


def next_exchange(pieces, axis, level):
    masks = doubling_masks(lax.axis_size(axis))
    return [
        have + [swap(jnp.concatenate(have, 0), axis, masks[which][level])]
        for which, have in enumerate(pieces)
    ]


def per_device(source_top, adjoint_bottom, slowness, correction, slowness_ref, omega):
    row_parts = lax.axis_size("rows")
    sections = lax.axis_size("depth")
    group = lax.axis_index("depth")
    part_id = lax.axis_index("rows")
    freq_count = omega.shape[0]
    chains = 2 * freq_count
    rep = sections // chains
    rows_here, ny = slowness.shape[1:]
    nx = rows_here * row_parts
    dims = (nx, ny, rows_here)
    hy = ny // 2
    chain = lax.div(group, rep)
    forward = lax.div(chain, freq_count)
    freq = lax.rem(chain, freq_count)
    side = lax.rem(group, 2)
    half_sections = sections // 2
    masks = doubling_masks(row_parts)
    orders = [doubling_orders(m) for m in masks]
    rounds = len(masks[0])
    plan = (sections, freq_count)

    def pick(values, index):
        return lax.dynamic_index_in_dim(values, index, 0, keepdims=False)

    plane = jnp.where(forward == 1, pick(source_top, freq), pick(adjoint_bottom, freq))
    high = slowness_ref.astype(bf16)
    middle = (slowness_ref - high.astype(f32)).astype(bf16)
    low = (slowness_ref - high.astype(f32) - middle.astype(f32)).astype(bf16)
    terms = jnp.concatenate([high, middle, low, jnp.zeros((13,), bf16)])
    values = jnp.concatenate([correction[0], slowness[0] - slowness_ref[0]], 0).astype(bf16)
    values = jnp.concatenate([values, jnp.broadcast_to(terms[:, None], (16, ny))], 0)
    left, right = values[:, :hy], values[:, hy:]
    same = jnp.where(side == 0, left, right)
    other = jnp.where(side == 0, right, left)
    packed = jnp.stack([same, other])
    blocks, partner = [packed], []
    for k in range(1, sections):
        blocks.append(swap(packed if k < half_sections else (same, other)[k % 2], "depth", k))
    for k in range(half_sections, sections):
        sent = (same, other)[k % 2][: 2 * rows_here]
        mask = k * row_parts + row_parts // 2
        partner.append(swap(sent, ("depth", "rows"), mask))
    planes = first_exchange(plane, "rows")
    assert nx == ny
    tables = basis_tables(nx)
    for level in range(1, rounds):
        planes = next_exchange(planes, "rows", level)
        if level == 1:
            blocks, partner = after((blocks, partner), planes)
            pair, refs, coef_rows = run_sort(omega, blocks, partner, rows_here, hy)
            pieces = [[pair[0]], [pair[1]]]
        before = pieces = after(pieces, planes)
        pieces = next_exchange(pieces, "rows", level)
    w = run_first(dims, orders, plan, refs, tables, after(planes[0] + planes[1], before))
    far_slots = [sections - 1 - slot for slot in range(half_sections, sections - 1)]
    early = before[0] + before[1]
    head = run_join(early, [(slot, range(len(early))) for slot in far_slots])
    head = [swap(h, "depth", half_sections) for h in head]
    last = after([have[-1] for have in pieces], (w, head))
    each = len(before[0])
    order = [*range(each), 2 * each, *range(each, 2 * each), 2 * each + 1]
    wanted = [(slot, order) for slot in range(half_sections)]
    wanted += [(slot, order[each :: each + 1]) for slot in far_slots]
    sides = [
        (sum(orders[j], []), order[j * (each + 1) : (j + 1) * (each + 1)]) for j in range(2)
    ]
    w, refs, *joined = run_join(early + last, wanted, (w, refs), sides)
    mine, rest = joined[:half_sections], joined[half_sections:]
    coefs = [[m, swap(m, "depth", 1)] for m in mine]
    far = [[h, swap(r, "depth", half_sections)] for h, r in zip(head, rest)]
    row_outs = []
    for slot in range(sections - 1):
        last = slot == sections - 2
        w, *rest = run_step(
            dims, orders, plan, slot, w, coefs[slot], refs, tables, coef_rows if last else None
        )
        if slot == half_sections - 2:
            coefs += [have + [swap(part, "depth", 1) for part in have] for have in after(far, w)]
        row_outs += [w, *rest] if last else rest

    def index_for(g, target):
        return target if g >= half_sections else sections - 2 - target

    def payload_for(mask):
        used = sorted(
            {index_for(g, g ^ mask) for g in range(sections) if index_for(g, g ^ mask) >= 0}
        )
        low = used[0]
        stack = jnp.stack(row_outs[low : used[-1] + 1])
        target = group ^ mask
        index = jnp.where(forward == 1, target, sections - 2 - target)
        return pick(stack, jnp.clip(index - low, 0, len(stack) - 1))

    far = [swap(payload_for(i * rep), "depth", i * rep) for i in range(freq_count, chains)]
    near = [payload_for(i * rep) for i in range(freq_count)]
    far, near = lax.optimization_barrier((far, near))
    fields = [f if i == 0 else swap(f, "depth", i * rep) for i, f in enumerate(near)] + far
    return run_image(plan, refs, fields, adjoint_bottom)


def solution(mesh):
    in_specs = (
        P(None, None, "rows", None),
        P(None, None, "rows", None),
        P("depth", "rows", None),
        P("depth", "rows", None),
        P("depth"),
        P(),
    )
    out_specs = P("depth", "rows", None)
    return jax.shard_map(
        per_device, mesh=mesh, in_specs=in_specs, out_specs=out_specs, check_vma=False
    )
```

time: 72.7 us -> 70 us (0.963)
  Pallas kernels: 20.6 us -> 16.1 us
  starting transfers between devices: 23.9 us -> 25.5 us
  local copies, waits for them, and re-layouts: 0.47 us -> 1.92 us
  waiting for transfers between devices: 25.1 us -> 23.8 us
    pallas_call x7 -> x8, Pallas kernels: 20.6 us -> 16.1 us  [the longest x3 14.2 us: run_step(): pl.pallas_call(partial(step_kernel, dims, orders, plan, index, len(coefs)...]
    ppermute x21 -> x23, starting transfers between devices: 23.9 us -> 25.5 us  [swap(): return lax.ppermute(values, axis, [(i, i ^ mask) for i in range(size)])]
    unnamed x8 -> x22, local copies, waits for them, and re-layouts: 0.32 us -> 1.84 us
    ppermute x21 -> x23, waiting for transfers between devices: 25.1 us -> 23.8 us  [swap(): return lax.ppermute(values, axis, [(i, i ^ mask) for i in range(size)])]
    select_n x1, other arithmetic: 0.02 us -> 1.03 us  [per_device(): jnp.where(forward == 1, pick(source_top, freq), pick(adjoint_bottom, freq))]
    sub x1, other arithmetic: 0.99 us -> 0.02 us  [per_device(): slowness[0] - slowness_ref[0]]
  transfers between devices with their start and end apart: 21 -> 23, of which waited for: 9 -> 12; matrix products, arithmetic and copies ran while one was open for 1% -> 1% of each run, Pallas kernels for 26% -> 22%
where the time goes in v4:
time: 70 us; the launch traced here: 69.9 us
  starting transfers between devices  25.5 us (36%)
  waiting for transfers between devices  23.8 us (34%)
  Pallas kernels  16.1 us (23%)
  local copies, waits for them, and re-layouts  1.92 us (3%)
  other arithmetic  1.55 us (2%)
  between operations  0.97 us (1%)
    ppermute x23, starting transfers between devices, swap(): return lax.ppermute(values, axis, [(i, i ^ mask) for i in range(size)])  25.5 us
    ppermute x23, waiting for transfers between devices, swap(): return lax.ppermute(values, axis, [(i, i ^ mask) for i in range(size)])  23.8 us
    pallas_call x3, Pallas kernels, run_step(): pl.pallas_call(partial(step_kernel, dims, orders, plan, index, len(coefs)...  14.2 us
    unnamed x22, local copies, waits for them, and re-layouts  1.84 us
  transfers between devices with their start and end apart: 23, of which 12 were waited for; matrix products, arithmetic and copies ran while one was open for 1% of the time, Pallas kernels for 22%

profile of v4, /device:TPU:0, one launch (start us, length us, event | category | flops | bytes accessed | tf_op | source)
XLA Modules:
  0.0 69.9 jit_solution(14504129069610978349)
XLA Ops:
  1.0 4.1 %collective-permute-start.5 = (bf16[2,64,512]{2,1,0:T(8,128)(2,1)S(1)}, bf16[2,64,512]{2,1,0:T(8,128)(2,1)S(1)}, u32[]{:S(2)}, u32[]{:S(2)}) collective-permute-start(bf16[2,64,512]{2,1,0:T(8,128)(2,1)S(1)} %bitcast.36), channel_id=1, source_target_pairs={{0,4},{1,5},{2,6},{3,7},{4,0},{5,1},{6,2},{7,3},{8,12},{9,13},{10,... | collective-permute-start | bytes 393224 | tf_op jit(solution)/shard_map/ppermute | solution.py:599
  6.2 1.3 %collective-permute-start.3 = (bf16[128,256]{1,0:T(8,128)(2,1)S(1)}, bf16[128,256]{1,0:T(8,128)(2,1)S(1)}, u32[]{:S(2)}, u32[]{:S(2)}) collective-permute-start(bf16[128,256]{1,0:T(8,128)(2,1)S(1)} %slice.50), channel_id=1, source_target_pairs={{0,20},{1,21},{2,22},{3,23},{4,16},{5,17},{6,18},{7,19},{8,28},{9,... | collective-permute-start | bytes 196616 | tf_op jit(solution)/shard_map/ppermute | solution.py:599
  7.5 2.3 %collective-permute-start.4 = (bf16[128,256]{1,0:T(8,128)(2,1)S(1)}, bf16[128,256]{1,0:T(8,128)(2,1)S(1)}, u32[]{:S(2)}, u32[]{:S(2)}) collective-permute-start(bf16[128,256]{1,0:T(8,128)(2,1)S(1)} %slice.51), channel_id=1, source_target_pairs={{0,28},{1,29},{2,30},{3,31},{4,24},{5,25},{6,26},{7,27},{8,20},{9,... | collective-permute-start | bytes 196616 | tf_op jit(solution)/shard_map/ppermute | solution.py:599
  9.8 1.9 %collective-permute-done.5 = bf16[2,64,512]{2,1,0:T(8,128)(2,1)S(1)} collective-permute-done((bf16[2,64,512]{2,1,0:T(8,128)(2,1)S(1)}, bf16[2,64,512]{2,1,0:T(8,128)(2,1)S(1)}, u32[]{:S(2)}, u32[]{:S(2)}) %collective-permute-start.5) | collective-permute-done | bytes 131104 | tf_op jit(solution)/shard_map/ppermute | solution.py:599
  11.8 3.4 %collective-permute-start.6 = (bf16[2,64,512]{2,1,0:T(8,128)(2,1)S(1)}, bf16[2,64,512]{2,1,0:T(8,128)(2,1)S(1)}, u32[]{:S(2)}, u32[]{:S(2)}) collective-permute-start(bf16[2,64,512]{2,1,0:T(8,128)(2,1)S(1)} %pad_maximum_fusion.6), channel_id=1, source_target_pairs={{0,2},{1,3},{2,0},{3,1},{4,6},{5,7},{6,4},{7,5},{8,10},{9,11},{10,... | collective-permute-start | bytes 393224 | tf_op jit(solution)/shard_map/ppermute | solution.py:599
  15.2 1.6 %collective-permute-start.7 = (bf16[2,64,512]{2,1,0:T(8,128)(2,1)S(1)}, bf16[2,64,512]{2,1,0:T(8,128)(2,1)S(1)}, u32[]{:S(2)}, u32[]{:S(2)}) collective-permute-start(bf16[2,64,512]{2,1,0:T(8,128)(2,1)S(1)} %pad_maximum_fusion.7), channel_id=1, source_target_pairs={{0,1},{1,0},{2,3},{3,2},{4,5},{5,4},{6,7},{7,6},{8,9},{9,8},{10,11... | collective-permute-start | bytes 393224 | tf_op jit(solution)/shard_map/ppermute | solution.py:599
  17.4 1.3 %collective-permute-start.1 = (bf16[144,256]{1,0:T(8,128)(2,1)S(1)}, bf16[144,256]{1,0:T(8,128)(2,1)S(1)}, u32[]{:S(2)}, u32[]{:S(2)}) collective-permute-start(bf16[144,256]{1,0:T(8,128)(2,1)S(1)} %get-tuple-element.95), channel_id=1, source_target_pairs={{0,16},{8,24},{16,0},{24,8},{1,17},{9,25},{17,1},{25,9},{2,18},{10... | collective-permute-start | bytes 221192 | tf_op jit(solution)/shard_map/ppermute | solution.py:599
  18.7 3.2 %collective-permute-done.1.refs_2_ = bf16[144,256]{1,0:T(8,128)(2,1)S(1)} collective-permute-done((bf16[144,256]{1,0:T(8,128)(2,1)S(1)}, bf16[144,256]{1,0:T(8,128)(2,1)S(1)}, u32[]{:S(2)}, u32[]{:S(2)}) %collective-permute-start.1) | collective-permute-done | bytes 73760 | tf_op jit(solution)/shard_map/ppermute | solution.py:599
  21.9 1.3 %collective-permute-done.2.refs_3_ = bf16[144,256]{1,0:T(8,128)(2,1)S(1)} collective-permute-done((bf16[144,256]{1,0:T(8,128)(2,1)S(1)}, bf16[144,256]{1,0:T(8,128)(2,1)S(1)}, u32[]{:S(2)}, u32[]{:S(2)}) %collective-permute-start.2) | collective-permute-done | bytes 73760 | tf_op jit(solution)/shard_map/ppermute | solution.py:599
  23.9 1.4 %collective-permute-start.9 = (bf16[4,64,512]{2,1,0:T(8,128)(2,1)S(1)}, bf16[4,64,512]{2,1,0:T(8,128)(2,1)S(1)}, u32[]{:S(2)}, u32[]{:S(2)}) collective-permute-start(bf16[4,64,512]{2,1,0:T(8,128)(2,1)S(1)} %pad_maximum_fusion.2), channel_id=1, source_target_pairs={{0,2},{1,3},{2,0},{3,1},{4,6},{5,7},{6,4},{7,5},{8,10},{9,11},{10,... | collective-permute-start | bytes 786440 | tf_op jit(solution)/shard_map/ppermute | solution.py:599
  27.3 1.5 %collective-permute-start.11 = (bf16[2,2,64,256]{3,2,1,0:T(8,128)(2,1)S(1)}, bf16[2,2,64,256]{3,2,1,0:T(8,128)(2,1)S(1)}, u32[]{:S(2)}, u32[]{:S(2)}) collective-permute-start(bf16[2,2,64,256]{3,2,1,0:T(8,128)(2,1)S(1)} %get-tuple-element.59.refs_2_.refs_4_), channel_id=1, source_target_pairs={{0,1},{1,0},{2,3},{3,2},{4,5},{5,4},{6,7},{7,6},{8,9},{9,8},{10,11... | collective-permute-start | bytes 393224 | tf_op jit(solution)/shard_map/ppermute | solution.py:599
  28.8 6.5 %collective-permute-done.10.refs_1_.refs_3_ = bf16[2,2,64,256]{3,2,1,0:T(8,128)(2,1)S(1)} collective-permute-done((bf16[2,2,64,256]{3,2,1,0:T(8,128)(2,1)S(1)}, bf16[2,2,64,256]{3,2,1,0:T(8,128)(2,1)S(1)}, u32[]{:S(2)}, u32[]{:S(2)}) %collective-permute-start.10) | collective-permute-done | bytes 131104 | tf_op jit(solution)/shard_map/ppermute | solution.py:599
  35.9 1.7 %collective-permute-start.13 = (bf16[4,2,64,256]{3,2,1,0:T(8,128)(2,1)S(1)}, bf16[4,2,64,256]{3,2,1,0:T(8,128)(2,1)S(1)}, u32[]{:S(2)}, u32[]{:S(2)}) collective-permute-start(bf16[4,2,64,256]{3,2,1,0:T(8,128)(2,1)S(1)} %pad_maximum_fusion.4), channel_id=1, source_target_pairs={{0,2},{1,3},{2,0},{3,1},{4,6},{5,7},{6,4},{7,5},{8,10},{9,11},{10,... | collective-permute-start | bytes 786440 | tf_op jit(solution)/shard_map/ppermute | solution.py:599
  37.5 1.5 %collective-permute-start.12 = (bf16[4,2,64,256]{3,2,1,0:T(8,128)(2,1)S(1)}, bf16[4,2,64,256]{3,2,1,0:T(8,128)(2,1)S(1)}, u32[]{:S(2)}, u32[]{:S(2)}) collective-permute-start(bf16[4,2,64,256]{3,2,1,0:T(8,128)(2,1)S(1)} %pad_maximum_fusion.3), channel_id=1, source_target_pairs={{0,1},{1,0},{2,3},{3,2},{4,5},{5,4},{6,7},{7,6},{8,9},{9,8},{10,11... | collective-permute-start | bytes 786440 | tf_op jit(solution)/shard_map/ppermute | solution.py:599
  39.3 3.9 %collective-permute-done.14.rest_0_ = bf16[8,64,256]{2,1,0:T(8,128)(2,1)S(1)} collective-permute-done((bf16[8,64,256]{2,1,0:T(8,128)(2,1)S(1)}, bf16[8,64,256]{2,1,0:T(8,128)(2,1)S(1)}, u32[]{:S(2)}, u32[]{:S(2)}) %collective-permute-start.14) | collective-permute-done | bytes 262176 | tf_op jit(solution)/shard_map/ppermute | solution.py:599
  43.3 1.4 %collective-permute-done.12.refs_6_ = bf16[4,2,64,256]{3,2,1,0:T(8,128)(2,1)S(1)} collective-permute-done((bf16[4,2,64,256]{3,2,1,0:T(8,128)(2,1)S(1)}, bf16[4,2,64,256]{3,2,1,0:T(8,128)(2,1)S(1)}, u32[]{:S(2)}, u32[]{:S(2)}) %collective-permute-start.12) | collective-permute-done | bytes 262176 | tf_op jit(solution)/shard_map/ppermute | solution.py:599
  45.9 1.0 %collective-permute-done.15.rest_1_ = bf16[16,64,256]{2,1,0:T(8,128)(2,1)S(1)} collective-permute-done((bf16[16,64,256]{2,1,0:T(8,128)(2,1)S(1)}, bf16[16,64,256]{2,1,0:T(8,128)(2,1)S(1)}, u32[]{:S(2)}, u32[]{:S(2)}) %collective-permute-start.15) | collective-permute-done | bytes 524320 | tf_op jit(solution)/shard_map/ppermute | solution.py:599
  46.9 1.2 %copy-done.7 = bf16[7,256,256]{2,1,0:T(8,128)(2,1)S(1)} copy-done((bf16[7,256,256]{2,1,0:T(8,128)(2,1)S(1)}, bf16[7,256,256]{2,1,0:T(8,128)(2,1)}, u32[]{:S(2)}) %copy-start.7) | copy-done | bytes 917528
  48.1 4.6 %depth_step.2 = (bf16[2,512,512]{2,1,0:T(8,128)(2,1)S(1)}, bf16[2,64,512]{2,1,0:T(8,128)(2,1)S(1)}) custom-call(bf16[2,512,512]{2,1,0:T(8,128)(2,1)S(1)} %get-tuple-element.72.w_ref, f32[6,8,128]{2,1,0:T(8,128)S(1)} %get-tuple-element.71.refs_ref, bf16[7,256,256]{2,1,0:T(8,128)(2,1)S(1)} %copy-done.7, bf16[16,64,256]{2,1,0:T(8,128)(2,1)S(1)} %get-tuple-element.73.rest_0_, ...), custom_call_target="tpu_custom_call" | custom-call | flops 4294967296 | bytes 16777216 | tf_op jit(solution)/shard_map/depth_step/pallas_call | solution.py:499
  52.7 1.8 %collective-permute-done.19.rest_1_ = bf16[9,64,256]{2,1,0:T(8,128)(2,1)S(1)} collective-permute-done((bf16[9,64,256]{2,1,0:T(8,128)(2,1)S(1)}, bf16[9,64,256]{2,1,0:T(8,128)(2,1)S(1)}, u32[]{:S(2)}, u32[]{:S(2)}) %collective-permute-start.19) | collective-permute-done | bytes 294944 | tf_op jit(solution)/shard_map/ppermute | solution.py:599
  55.0 4.6 %depth_step.3 = (bf16[2,512,512]{2,1,0:T(8,128)(2,1)S(1)}, bf16[2,64,512]{2,1,0:T(8,128)(2,1)S(1)}) custom-call(bf16[2,512,512]{2,1,0:T(8,128)(2,1)S(1)} %get-tuple-element.75.w_ref, f32[6,8,128]{2,1,0:T(8,128)S(1)} %get-tuple-element.71.refs_ref, bf16[7,256,256]{2,1,0:T(8,128)(2,1)S(1)} %copy-done.7, bf16[16,64,256]{2,1,0:T(8,128)(2,1)S(1)} %get-tuple-element.76.rest_0_, ...), custom_call_target="tpu_custom_call" | custom-call | flops 4294967296 | bytes 16777216 | tf_op jit(solution)/shard_map/depth_step/pallas_call | solution.py:499
  60.1 1.3 %collective-permute-start.18 = (bf16[2,64,512]{2,1,0:T(8,128)(2,1)S(1)}, bf16[2,64,512]{2,1,0:T(8,128)(2,1)S(1)}, u32[]{:S(2)}, u32[]{:S(2)}) collective-permute-start(bf16[2,64,512]{2,1,0:T(8,128)(2,1)S(1)} %get-tuple-element.91), channel_id=1, source_target_pairs={{0,24},{8,16},{16,8},{24,0},{1,25},{9,17},{17,9},{25,1},{2,26},{10... | collective-permute-start | bytes 393224 | tf_op jit(solution)/shard_map/ppermute | solution.py:599
  61.5 4.9 %end_step.1 = (bf16[2,64,512]{2,1,0:T(8,128)(2,1)S(1)}, bf16[2,64,512]{2,1,0:T(8,128)(2,1)S(1)}) custom-call(bf16[2,512,512]{2,1,0:T(8,128)(2,1)S(1)} %get-tuple-element.78.w_ref, f32[6,8,128]{2,1,0:T(8,128)S(1)} %get-tuple-element.71.refs_ref, bf16[7,256,256]{2,1,0:T(8,128)(2,1)S(1)} %copy-done.8, bf16[8,64,256]{2,1,0:T(8,128)(2,1)S(1)} %copy-done.3, ...), custom_call_target="tpu_custom_call" | custom-call | flops 4294967296 | bytes 16777216 | tf_op jit(solution)/shard_map/end_step/pallas_call | solution.py:499
  66.5 1.1 %collective-permute-done.18.refs_3_ = bf16[2,64,512]{2,1,0:T(8,128)(2,1)S(1)} collective-permute-done((bf16[2,64,512]{2,1,0:T(8,128)(2,1)S(1)}, bf16[2,64,512]{2,1,0:T(8,128)(2,1)S(1)}, u32[]{:S(2)}, u32[]{:S(2)}) %collective-permute-start.18) | collective-permute-done | bytes 131104 | tf_op jit(solution)/shard_map/ppermute | solution.py:599
  (73 shorter events, 10.1 us)
Async XLA Ops:
  1.0 10.7 %collective-permute-start.5 = (bf16[2,64,512]{2,1,0:T(8,128)(2,1)S(1)}, bf16[2,64,512]{2,1,0:T(8,128)(2,1)S(1)}, u32[]{:S(2)}, u32[]{:S(2)}) collective-permute-start(bf16[2,64,512]{2,1,0:T(8,128)(2,1)S(1)} %bitcast.36), channel_id=1, source_target_pairs={{0,4},{1,5},{2,6},{3,7},{4,0},{5,1},{6,2},{7,3},{8,12},{9,13},{10,... | collective-permute-start | bytes 393224 | tf_op jit(solution)/shard_map/ppermute | solution.py:599
  6.1 17.1 %collective-permute-start = (bf16[2,144,256]{2,1,0:T(8,128)(2,1)S(1)}, bf16[2,144,256]{2,1,0:T(8,128)(2,1)S(1)}, u32[]{:S(2)}, u32[]{:S(2)}) collective-permute-start(bf16[2,144,256]{2,1,0:T(8,128)(2,1)S(1)} %pad_maximum_fusion.5.refs_0_), channel_id=1, source_target_pairs={{0,8},{8,0},{16,24},{24,16},{1,9},{9,1},{17,25},{25,17},{2,10},{10... | collective-permute-start | bytes 442376 | tf_op jit(solution)/shard_map/ppermute | solution.py:599
  6.2 11.2 %collective-permute-start.3 = (bf16[128,256]{1,0:T(8,128)(2,1)S(1)}, bf16[128,256]{1,0:T(8,128)(2,1)S(1)}, u32[]{:S(2)}, u32[]{:S(2)}) collective-permute-start(bf16[128,256]{1,0:T(8,128)(2,1)S(1)} %slice.50), channel_id=1, source_target_pairs={{0,20},{1,21},{2,22},{3,23},{4,16},{5,17},{6,18},{7,19},{8,28},{9,... | collective-permute-start | bytes 196616 | tf_op jit(solution)/shard_map/ppermute | solution.py:599
  7.5 11.1 %collective-permute-start.4 = (bf16[128,256]{1,0:T(8,128)(2,1)S(1)}, bf16[128,256]{1,0:T(8,128)(2,1)S(1)}, u32[]{:S(2)}, u32[]{:S(2)}) collective-permute-start(bf16[128,256]{1,0:T(8,128)(2,1)S(1)} %slice.51), channel_id=1, source_target_pairs={{0,28},{1,29},{2,30},{3,31},{4,24},{5,25},{6,26},{7,27},{8,20},{9,... | collective-permute-start | bytes 196616 | tf_op jit(solution)/shard_map/ppermute | solution.py:599
  11.8 11.4 %collective-permute-start.6 = (bf16[2,64,512]{2,1,0:T(8,128)(2,1)S(1)}, bf16[2,64,512]{2,1,0:T(8,128)(2,1)S(1)}, u32[]{:S(2)}, u32[]{:S(2)}) collective-permute-start(bf16[2,64,512]{2,1,0:T(8,128)(2,1)S(1)} %pad_maximum_fusion.6), channel_id=1, source_target_pairs={{0,2},{1,3},{2,0},{3,1},{4,6},{5,7},{6,4},{7,5},{8,10},{9,11},{10,... | collective-permute-start | bytes 393224 | tf_op jit(solution)/shard_map/ppermute | solution.py:599
  15.2 8.0 %collective-permute-start.7 = (bf16[2,64,512]{2,1,0:T(8,128)(2,1)S(1)}, bf16[2,64,512]{2,1,0:T(8,128)(2,1)S(1)}, u32[]{:S(2)}, u32[]{:S(2)}) collective-permute-start(bf16[2,64,512]{2,1,0:T(8,128)(2,1)S(1)} %pad_maximum_fusion.7), channel_id=1, source_target_pairs={{0,1},{1,0},{2,3},{3,2},{4,5},{5,4},{6,7},{7,6},{8,9},{9,8},{10,11... | collective-permute-start | bytes 393224 | tf_op jit(solution)/shard_map/ppermute | solution.py:599
  17.4 4.5 %collective-permute-start.1 = (bf16[144,256]{1,0:T(8,128)(2,1)S(1)}, bf16[144,256]{1,0:T(8,128)(2,1)S(1)}, u32[]{:S(2)}, u32[]{:S(2)}) collective-permute-start(bf16[144,256]{1,0:T(8,128)(2,1)S(1)} %get-tuple-element.95), channel_id=1, source_target_pairs={{0,16},{8,24},{16,0},{24,8},{1,17},{9,25},{17,1},{25,9},{2,18},{10... | collective-permute-start | bytes 221192 | tf_op jit(solution)/shard_map/ppermute | solution.py:599
  18.6 4.5 %collective-permute-start.2 = (bf16[144,256]{1,0:T(8,128)(2,1)S(1)}, bf16[144,256]{1,0:T(8,128)(2,1)S(1)}, u32[]{:S(2)}, u32[]{:S(2)}) collective-permute-start(bf16[144,256]{1,0:T(8,128)(2,1)S(1)} %get-tuple-element.96), channel_id=1, source_target_pairs={{0,24},{8,16},{16,8},{24,0},{1,25},{9,17},{17,9},{25,1},{2,26},{10... | collective-permute-start | bytes 221192 | tf_op jit(solution)/shard_map/ppermute | solution.py:599
  23.2 12.1 %collective-permute-start.8 = (bf16[4,64,512]{2,1,0:T(8,128)(2,1)S(1)}, bf16[4,64,512]{2,1,0:T(8,128)(2,1)S(1)}, u32[]{:S(2)}, u32[]{:S(2)}) collective-permute-start(bf16[4,64,512]{2,1,0:T(8,128)(2,1)S(1)} %pad_maximum_fusion.1), channel_id=1, source_target_pairs={{0,1},{1,0},{2,3},{3,2},{4,5},{5,4},{6,7},{7,6},{8,9},{9,8},{10,11... | collective-permute-start | bytes 786440 | tf_op jit(solution)/shard_map/ppermute | solution.py:599
  23.9 11.4 %collective-permute-start.9 = (bf16[4,64,512]{2,1,0:T(8,128)(2,1)S(1)}, bf16[4,64,512]{2,1,0:T(8,128)(2,1)S(1)}, u32[]{:S(2)}, u32[]{:S(2)}) collective-permute-start(bf16[4,64,512]{2,1,0:T(8,128)(2,1)S(1)} %pad_maximum_fusion.2), channel_id=1, source_target_pairs={{0,2},{1,3},{2,0},{3,1},{4,6},{5,7},{6,4},{7,5},{8,10},{9,11},{10,... | collective-permute-start | bytes 786440 | tf_op jit(solution)/shard_map/ppermute | solution.py:599
  26.7 12.4 %copy-start.6 = (bf16[7,256,256]{2,1,0:T(8,128)(2,1)S(1)}, bf16[7,256,256]{2,1,0:T(8,128)(2,1)}, u32[]{:S(2)}) copy-start(bf16[7,256,256]{2,1,0:T(8,128)(2,1)} %constant.46.clone.tables) | copy-start | bytes 2752516
  26.7 8.6 %collective-permute-start.10 = (bf16[2,2,64,256]{3,2,1,0:T(8,128)(2,1)S(1)}, bf16[2,2,64,256]{3,2,1,0:T(8,128)(2,1)S(1)}, u32[]{:S(2)}, u32[]{:S(2)}) collective-permute-start(bf16[2,2,64,256]{3,2,1,0:T(8,128)(2,1)S(1)} %get-tuple-element.57.refs_0_.refs_2_), channel_id=1, source_target_pairs={{0,2},{1,3},{2,0},{3,1},{4,6},{5,7},{6,4},{7,5},{8,10},{9,11},{10,... | collective-permute-start | bytes 393224 | tf_op jit(solution)/shard_map/ppermute | solution.py:599
  27.3 8.0 %collective-permute-start.11 = (bf16[2,2,64,256]{3,2,1,0:T(8,128)(2,1)S(1)}, bf16[2,2,64,256]{3,2,1,0:T(8,128)(2,1)S(1)}, u32[]{:S(2)}, u32[]{:S(2)}) collective-permute-start(bf16[2,2,64,256]{3,2,1,0:T(8,128)(2,1)S(1)} %get-tuple-element.59.refs_2_.refs_4_), channel_id=1, source_target_pairs={{0,1},{1,0},{2,3},{3,2},{4,5},{5,4},{6,7},{7,6},{8,9},{9,8},{10,11... | collective-permute-start | bytes 393224 | tf_op jit(solution)/shard_map/ppermute | solution.py:599
  35.4 7.8 %collective-permute-start.14 = (bf16[8,64,256]{2,1,0:T(8,128)(2,1)S(1)}, bf16[8,64,256]{2,1,0:T(8,128)(2,1)S(1)}, u32[]{:S(2)}, u32[]{:S(2)}) collective-permute-start(bf16[8,64,256]{2,1,0:T(8,128)(2,1)S(1)} %join_pieces.2), channel_id=1, source_target_pairs={{0,16},{8,24},{16,0},{24,8},{1,17},{9,25},{17,1},{25,9},{2,18},{10... | collective-permute-start | bytes 786440 | tf_op jit(solution)/shard_map/ppermute | solution.py:599
  35.9 7.4 %collective-permute-start.13 = (bf16[4,2,64,256]{3,2,1,0:T(8,128)(2,1)S(1)}, bf16[4,2,64,256]{3,2,1,0:T(8,128)(2,1)S(1)}, u32[]{:S(2)}, u32[]{:S(2)}) collective-permute-start(bf16[4,2,64,256]{3,2,1,0:T(8,128)(2,1)S(1)} %pad_maximum_fusion.4), channel_id=1, source_target_pairs={{0,2},{1,3},{2,0},{3,1},{4,6},{5,7},{6,4},{7,5},{8,10},{9,11},{10,... | collective-permute-start | bytes 786440 | tf_op jit(solution)/shard_map/ppermute | solution.py:599
  37.5 7.2 %collective-permute-start.12 = (bf16[4,2,64,256]{3,2,1,0:T(8,128)(2,1)S(1)}, bf16[4,2,64,256]{3,2,1,0:T(8,128)(2,1)S(1)}, u32[]{:S(2)}, u32[]{:S(2)}) collective-permute-start(bf16[4,2,64,256]{3,2,1,0:T(8,128)(2,1)S(1)} %pad_maximum_fusion.3), channel_id=1, source_target_pairs={{0,1},{1,0},{2,3},{3,2},{4,5},{5,4},{6,7},{7,6},{8,9},{9,8},{10,11... | collective-permute-start | bytes 786440 | tf_op jit(solution)/shard_map/ppermute | solution.py:599
  44.9 2.0 %collective-permute-start.15 = (bf16[16,64,256]{2,1,0:T(8,128)(2,1)S(1)}, bf16[16,64,256]{2,1,0:T(8,128)(2,1)S(1)}, u32[]{:S(2)}, u32[]{:S(2)}) collective-permute-start(bf16[16,64,256]{2,1,0:T(8,128)(2,1)S(1)} %get-tuple-element.73.rest_0_), channel_id=1, source_target_pairs={{0,8},{8,0},{16,24},{24,16},{1,9},{9,1},{17,25},{25,17},{2,10},{10... | collective-permute-start | bytes 1572872 | tf_op jit(solution)/shard_map/ppermute | solution.py:599
  45.0 10.0 %collective-permute-start.16 = (bf16[16,64,256]{2,1,0:T(8,128)(2,1)S(1)}, bf16[16,64,256]{2,1,0:T(8,128)(2,1)S(1)}, u32[]{:S(2)}, u32[]{:S(2)}) collective-permute-start(bf16[16,64,256]{2,1,0:T(8,128)(2,1)S(1)} %get-tuple-element.76.rest_0_), channel_id=1, source_target_pairs={{0,8},{8,0},{16,24},{24,16},{1,9},{9,1},{17,25},{25,17},{2,10},{10... | collective-permute-start | bytes 1572872 | tf_op jit(solution)/shard_map/ppermute | solution.py:599
  45.5 9.0 %collective-permute-start.19 = (bf16[9,64,256]{2,1,0:T(8,128)(2,1)S(1)}, bf16[9,64,256]{2,1,0:T(8,128)(2,1)S(1)}, u32[]{:S(2)}, u32[]{:S(2)}) collective-permute-start(bf16[9,64,256]{2,1,0:T(8,128)(2,1)S(1)} %get-tuple-element.79), channel_id=1, source_target_pairs={{0,16},{8,24},{16,0},{24,8},{1,17},{9,25},{17,1},{25,9},{2,18},{10... | collective-permute-start | bytes 884744 | tf_op jit(solution)/shard_map/ppermute | solution.py:599
  54.5 6.9 %collective-permute-start.21 = (bf16[9,64,256]{2,1,0:T(8,128)(2,1)S(1)}, bf16[9,64,256]{2,1,0:T(8,128)(2,1)S(1)}, u32[]{:S(2)}, u32[]{:S(2)}) collective-permute-start(bf16[9,64,256]{2,1,0:T(8,128)(2,1)S(1)} %collective-permute-done.19.rest_1_), channel_id=1, source_target_pairs={{0,8},{8,0},{16,24},{24,16},{1,9},{9,1},{17,25},{25,17},{2,10},{10... | collective-permute-start | bytes 884744 | tf_op jit(solution)/shard_map/ppermute | solution.py:599
  54.5 6.9 %collective-permute-start.20 = (bf16[8,64,256]{2,1,0:T(8,128)(2,1)S(1)}, bf16[8,64,256]{2,1,0:T(8,128)(2,1)S(1)}, u32[]{:S(2)}, u32[]{:S(2)}) collective-permute-start(bf16[8,64,256]{2,1,0:T(8,128)(2,1)S(1)} %copy-done.3), channel_id=1, source_target_pairs={{0,8},{8,0},{16,24},{24,16},{1,9},{9,1},{17,25},{25,17},{2,10},{10... | collective-permute-start | bytes 786440 | tf_op jit(solution)/shard_map/ppermute | solution.py:599
  59.8 6.7 %collective-permute-start.17 = (bf16[2,64,512]{2,1,0:T(8,128)(2,1)S(1)}, bf16[2,64,512]{2,1,0:T(8,128)(2,1)S(1)}, u32[]{:S(2)}, u32[]{:S(2)}) collective-permute-start(bf16[2,64,512]{2,1,0:T(8,128)(2,1)S(1)} %get-tuple-element.92), channel_id=1, source_target_pairs={{0,16},{8,24},{16,0},{24,8},{1,17},{9,25},{17,1},{25,9},{2,18},{10... | collective-permute-start | bytes 393224 | tf_op jit(solution)/shard_map/ppermute | solution.py:599
  60.1 7.4 %collective-permute-start.18 = (bf16[2,64,512]{2,1,0:T(8,128)(2,1)S(1)}, bf16[2,64,512]{2,1,0:T(8,128)(2,1)S(1)}, u32[]{:S(2)}, u32[]{:S(2)}) collective-permute-start(bf16[2,64,512]{2,1,0:T(8,128)(2,1)S(1)} %get-tuple-element.91), channel_id=1, source_target_pairs={{0,24},{8,16},{16,8},{24,0},{1,25},{9,17},{17,9},{25,1},{2,26},{10... | collective-permute-start | bytes 393224 | tf_op jit(solution)/shard_map/ppermute | solution.py:599
  67.6 1.5 %collective-permute-start.22 = (bf16[2,64,512]{2,1,0:T(8,128)(2,1)S(1)}, bf16[2,64,512]{2,1,0:T(8,128)(2,1)S(1)}, u32[]{:S(2)}, u32[]{:S(2)}) collective-permute-start(bf16[2,64,512]{2,1,0:T(8,128)(2,1)S(1)} %get-tuple-element.86), channel_id=1, source_target_pairs={{0,8},{8,0},{16,24},{24,16},{1,9},{9,1},{17,25},{25,17},{2,10},{10... | collective-permute-start | bytes 393224 | tf_op jit(solution)/shard_map/ppermute | solution.py:599
  (10 other events, 35.3 us)

commit v5 on v4

--- a/solution.py
+++ b/solution.py
@@ -690,7 +690,8 @@
             blocks, partner = after((blocks, partner), planes)
             pair, refs, coef_rows = run_sort(omega, blocks, partner, rows_here, hy)
             pieces = [[pair[0]], [pair[1]]]
-        before = pieces = after(pieces, planes)
+            planes = after(planes, pair)
+        before = pieces
         pieces = next_exchange(pieces, "rows", level)
     w = run_first(dims, orders, plan, refs, tables, after(planes[0] + planes[1], before))
     far_slots = [sections - 1 - slot for slot in range(half_sections, sections - 1)]
@@ -715,7 +716,7 @@
         w, *rest = run_step(
             dims, orders, plan, slot, w, coefs[slot], refs, tables, coef_rows if last else None
         )
-        if slot == half_sections - 2:
+        if slot == half_sections - 1:
             coefs += [have + [swap(part, "depth", 1) for part in have] for have in after(far, w)]
         row_outs += [w, *rest] if last else rest
 

time: 70 us -> 64.2 us (0.917)
  waiting for transfers between devices: 23.8 us -> 20.2 us
  local copies, waits for them, and re-layouts: 1.92 us -> 0.1 us
    ppermute x23, waiting for transfers between devices: 23.8 us -> 20.2 us  [swap(): return lax.ppermute(values, axis, [(i, i ^ mask) for i in range(size)])]
    unnamed x22 -> x10, local copies, waits for them, and re-layouts: 1.84 us -> 0.02 us
  transfers between devices with their start and end apart: 23 -> 23, of which waited for: 12 -> 13; matrix products, arithmetic and copies ran while one was open for 1% -> 1% of each run, Pallas kernels for 22% -> 23%
where the time goes in v5:
time: 64.2 us; the launch traced here: 64.1 us
  starting transfers between devices  25 us (39%)
  waiting for transfers between devices  20.2 us (31%)
  Pallas kernels  16.3 us (25%)
  other arithmetic  1.53 us (2%)
  between operations  0.93 us (1%)
    ppermute x23, starting transfers between devices, swap(): return lax.ppermute(values, axis, [(i, i ^ mask) for i in range(size)])  25 us
    ppermute x23, waiting for transfers between devices, swap(): return lax.ppermute(values, axis, [(i, i ^ mask) for i in range(size)])  20.2 us
    pallas_call x3, Pallas kernels, run_step(): pl.pallas_call(partial(step_kernel, dims, orders, plan, index, len(coefs)...  14.4 us
  transfers between devices with their start and end apart: 23, of which 13 were waited for; matrix products, arithmetic and copies ran while one was open for 1% of the time, Pallas kernels for 23%

profile of v5, /device:TPU:0, one launch (start us, length us, event | category | flops | bytes accessed | tf_op | source)
XLA Modules:
  0.0 64.1 jit_solution(4364849973988861168)
XLA Ops:
  0.0 1.0 %dynamic-slice_select_fusion = bf16[1,2,64,512]{3,2,1,0:T(8,128)(2,1)S(1)} fusion(bf16[2,2,64,512]{3,2,1,0:T(8,128)(2,1)} %refs_4_.1, s32[]{:T(128)S(6)} %select_n.50, bf16[2,2,64,512]{3,2,1,0:T(8,128)(2,1)} %param.7, pred[]{:T(512)S(6)} %eq.5), kind=kLoop, calls=%fused_computation.21 | loop fusion | flops 65536 | bytes 393221 | tf_op jit(solution)/shard_map/jit(_where)/select_n | solution.py:666
  1.0 4.1 %collective-permute-start.5 = (bf16[2,64,512]{2,1,0:T(8,128)(2,1)S(1)}, bf16[2,64,512]{2,1,0:T(8,128)(2,1)S(1)}, u32[]{:S(2)}, u32[]{:S(2)}) collective-permute-start(bf16[2,64,512]{2,1,0:T(8,128)(2,1)S(1)} %bitcast.36), channel_id=1, source_target_pairs={{0,4},{1,5},{2,6},{3,7},{4,0},{5,1},{6,2},{7,3},{8,12},{9,13},{10,... | collective-permute-start | bytes 393224 | tf_op jit(solution)/shard_map/ppermute | solution.py:599
  6.2 1.3 %collective-permute-start.3 = (bf16[128,256]{1,0:T(8,128)(2,1)S(1)}, bf16[128,256]{1,0:T(8,128)(2,1)S(1)}, u32[]{:S(2)}, u32[]{:S(2)}) collective-permute-start(bf16[128,256]{1,0:T(8,128)(2,1)S(1)} %slice.50), channel_id=1, source_target_pairs={{0,20},{1,21},{2,22},{3,23},{4,16},{5,17},{6,18},{7,19},{8,28},{9,... | collective-permute-start | bytes 196616 | tf_op jit(solution)/shard_map/ppermute | solution.py:599
  7.5 2.3 %collective-permute-start.4 = (bf16[128,256]{1,0:T(8,128)(2,1)S(1)}, bf16[128,256]{1,0:T(8,128)(2,1)S(1)}, u32[]{:S(2)}, u32[]{:S(2)}) collective-permute-start(bf16[128,256]{1,0:T(8,128)(2,1)S(1)} %slice.51), channel_id=1, source_target_pairs={{0,28},{1,29},{2,30},{3,31},{4,24},{5,25},{6,26},{7,27},{8,20},{9,... | collective-permute-start | bytes 196616 | tf_op jit(solution)/shard_map/ppermute | solution.py:599
  9.8 1.9 %collective-permute-done.5 = bf16[2,64,512]{2,1,0:T(8,128)(2,1)S(1)} collective-permute-done((bf16[2,64,512]{2,1,0:T(8,128)(2,1)S(1)}, bf16[2,64,512]{2,1,0:T(8,128)(2,1)S(1)}, u32[]{:S(2)}, u32[]{:S(2)}) %collective-permute-start.5) | collective-permute-done | bytes 131104 | tf_op jit(solution)/shard_map/ppermute | solution.py:599
  11.8 3.4 %collective-permute-start.6 = (bf16[2,64,512]{2,1,0:T(8,128)(2,1)S(1)}, bf16[2,64,512]{2,1,0:T(8,128)(2,1)S(1)}, u32[]{:S(2)}, u32[]{:S(2)}) collective-permute-start(bf16[2,64,512]{2,1,0:T(8,128)(2,1)S(1)} %pad_maximum_fusion.6), channel_id=1, source_target_pairs={{0,2},{1,3},{2,0},{3,1},{4,6},{5,7},{6,4},{7,5},{8,10},{9,11},{10,... | collective-permute-start | bytes 393224 | tf_op jit(solution)/shard_map/ppermute | solution.py:599
  15.2 1.6 %collective-permute-start.7 = (bf16[2,64,512]{2,1,0:T(8,128)(2,1)S(1)}, bf16[2,64,512]{2,1,0:T(8,128)(2,1)S(1)}, u32[]{:S(2)}, u32[]{:S(2)}) collective-permute-start(bf16[2,64,512]{2,1,0:T(8,128)(2,1)S(1)} %pad_maximum_fusion.7), channel_id=1, source_target_pairs={{0,1},{1,0},{2,3},{3,2},{4,5},{5,4},{6,7},{7,6},{8,9},{9,8},{10,11... | collective-permute-start | bytes 393224 | tf_op jit(solution)/shard_map/ppermute | solution.py:599
  17.4 1.3 %collective-permute-start.1 = (bf16[144,256]{1,0:T(8,128)(2,1)S(1)}, bf16[144,256]{1,0:T(8,128)(2,1)S(1)}, u32[]{:S(2)}, u32[]{:S(2)}) collective-permute-start(bf16[144,256]{1,0:T(8,128)(2,1)S(1)} %get-tuple-element.95), channel_id=1, source_target_pairs={{0,16},{8,24},{16,0},{24,8},{1,17},{9,25},{17,1},{25,9},{2,18},{10... | collective-permute-start | bytes 221192 | tf_op jit(solution)/shard_map/ppermute | solution.py:599
  18.7 3.2 %collective-permute-done.1.refs_2_ = bf16[144,256]{1,0:T(8,128)(2,1)S(1)} collective-permute-done((bf16[144,256]{1,0:T(8,128)(2,1)S(1)}, bf16[144,256]{1,0:T(8,128)(2,1)S(1)}, u32[]{:S(2)}, u32[]{:S(2)}) %collective-permute-start.1) | collective-permute-done | bytes 73760 | tf_op jit(solution)/shard_map/ppermute | solution.py:599
  21.9 1.3 %collective-permute-done.2.refs_3_ = bf16[144,256]{1,0:T(8,128)(2,1)S(1)} collective-permute-done((bf16[144,256]{1,0:T(8,128)(2,1)S(1)}, bf16[144,256]{1,0:T(8,128)(2,1)S(1)}, u32[]{:S(2)}, u32[]{:S(2)}) %collective-permute-start.2) | collective-permute-done | bytes 73760 | tf_op jit(solution)/shard_map/ppermute | solution.py:599
  23.9 1.4 %collective-permute-start.10 = (bf16[2,2,64,256]{3,2,1,0:T(8,128)(2,1)S(1)}, bf16[2,2,64,256]{3,2,1,0:T(8,128)(2,1)S(1)}, u32[]{:S(2)}, u32[]{:S(2)}) collective-permute-start(bf16[2,2,64,256]{3,2,1,0:T(8,128)(2,1)S(1)} %get-tuple-element.94.refs_0_.refs_2_), channel_id=1, source_target_pairs={{0,2},{1,3},{2,0},{3,1},{4,6},{5,7},{6,4},{7,5},{8,10},{9,11},{10,... | collective-permute-start | bytes 393224 | tf_op jit(solution)/shard_map/ppermute | solution.py:599
  26.7 1.5 %collective-permute-start.8 = (bf16[4,64,512]{2,1,0:T(8,128)(2,1)S(1)}, bf16[4,64,512]{2,1,0:T(8,128)(2,1)S(1)}, u32[]{:S(2)}, u32[]{:S(2)}) collective-permute-start(bf16[4,64,512]{2,1,0:T(8,128)(2,1)S(1)} %pad_maximum_fusion.1), channel_id=1, source_target_pairs={{0,1},{1,0},{2,3},{3,2},{4,5},{5,4},{6,7},{7,6},{8,9},{9,8},{10,11... | collective-permute-start | bytes 786440 | tf_op jit(solution)/shard_map/ppermute | solution.py:599
  28.3 2.1 %collective-permute-done.10.refs_1_.refs_3_ = bf16[2,2,64,256]{3,2,1,0:T(8,128)(2,1)S(1)} collective-permute-done((bf16[2,2,64,256]{3,2,1,0:T(8,128)(2,1)S(1)}, bf16[2,2,64,256]{3,2,1,0:T(8,128)(2,1)S(1)}, u32[]{:S(2)}, u32[]{:S(2)}) %collective-permute-start.10) | collective-permute-done | bytes 131104 | tf_op jit(solution)/shard_map/ppermute | solution.py:599
  30.3 1.2 %collective-permute-done.11.refs_3_.refs_5_ = bf16[2,2,64,256]{3,2,1,0:T(8,128)(2,1)S(1)} collective-permute-done((bf16[2,2,64,256]{3,2,1,0:T(8,128)(2,1)S(1)}, bf16[2,2,64,256]{3,2,1,0:T(8,128)(2,1)S(1)}, u32[]{:S(2)}, u32[]{:S(2)}) %collective-permute-start.11) | collective-permute-done | bytes 131104 | tf_op jit(solution)/shard_map/ppermute | solution.py:599
  31.6 1.0 %collective-permute-start.14 = (bf16[8,64,256]{2,1,0:T(8,128)(2,1)S(1)}, bf16[8,64,256]{2,1,0:T(8,128)(2,1)S(1)}, u32[]{:S(2)}, u32[]{:S(2)}) collective-permute-start(bf16[8,64,256]{2,1,0:T(8,128)(2,1)S(1)} %join_pieces.2), channel_id=1, source_target_pairs={{0,16},{8,24},{16,0},{24,8},{1,17},{9,25},{17,1},{25,9},{2,18},{10... | collective-permute-start | bytes 786440 | tf_op jit(solution)/shard_map/ppermute | solution.py:599
  33.5 2.5 %collective-permute-done.9.rest_7_ = bf16[4,64,512]{2,1,0:T(8,128)(2,1)S(1)} collective-permute-done((bf16[4,64,512]{2,1,0:T(8,128)(2,1)S(1)}, bf16[4,64,512]{2,1,0:T(8,128)(2,1)S(1)}, u32[]{:S(2)}, u32[]{:S(2)}) %collective-permute-start.9) | collective-permute-done | bytes 262176 | tf_op jit(solution)/shard_map/ppermute | solution.py:599
  36.0 1.2 %collective-permute-done.8.rest_3_ = bf16[4,64,512]{2,1,0:T(8,128)(2,1)S(1)} collective-permute-done((bf16[4,64,512]{2,1,0:T(8,128)(2,1)S(1)}, bf16[4,64,512]{2,1,0:T(8,128)(2,1)S(1)}, u32[]{:S(2)}, u32[]{:S(2)}) %collective-permute-start.8) | collective-permute-done | bytes 262176 | tf_op jit(solution)/shard_map/ppermute | solution.py:599
  38.0 2.7 %collective-permute-done.13.refs_7_ = bf16[4,2,64,256]{3,2,1,0:T(8,128)(2,1)S(1)} collective-permute-done((bf16[4,2,64,256]{3,2,1,0:T(8,128)(2,1)S(1)}, bf16[4,2,64,256]{3,2,1,0:T(8,128)(2,1)S(1)}, u32[]{:S(2)}, u32[]{:S(2)}) %collective-permute-start.13) | collective-permute-done | bytes 262176 | tf_op jit(solution)/shard_map/ppermute | solution.py:599
  42.4 1.5 %collective-permute-start.19 = (bf16[9,64,256]{2,1,0:T(8,128)(2,1)S(1)}, bf16[9,64,256]{2,1,0:T(8,128)(2,1)S(1)}, u32[]{:S(2)}, u32[]{:S(2)}) collective-permute-start(bf16[9,64,256]{2,1,0:T(8,128)(2,1)S(1)} %get-tuple-element.79), channel_id=1, source_target_pairs={{0,16},{8,24},{16,0},{24,8},{1,17},{9,25},{17,1},{25,9},{2,18},{10... | collective-permute-start | bytes 884744 | tf_op jit(solution)/shard_map/ppermute | solution.py:599
  43.9 4.7 %depth_step.2 = (bf16[2,512,512]{2,1,0:T(8,128)(2,1)S(1)}, bf16[2,64,512]{2,1,0:T(8,128)(2,1)S(1)}) custom-call(bf16[2,512,512]{2,1,0:T(8,128)(2,1)S(1)} %get-tuple-element.72.w_ref, f32[6,8,128]{2,1,0:T(8,128)S(1)} %get-tuple-element.71.refs_ref, bf16[7,256,256]{2,1,0:T(8,128)(2,1)S(1)} %copy-done.2, bf16[16,64,256]{2,1,0:T(8,128)(2,1)S(1)} %get-tuple-element.73.rest_0_, ...), custom_call_target="tpu_custom_call" | custom-call | flops 4294967296 | bytes 16777216 | tf_op jit(solution)/shard_map/depth_step/pallas_call | solution.py:499
  48.6 4.9 %depth_step.3 = (bf16[2,512,512]{2,1,0:T(8,128)(2,1)S(1)}, bf16[2,64,512]{2,1,0:T(8,128)(2,1)S(1)}) custom-call(bf16[2,512,512]{2,1,0:T(8,128)(2,1)S(1)} %get-tuple-element.75.w_ref, f32[6,8,128]{2,1,0:T(8,128)S(1)} %get-tuple-element.71.refs_ref, bf16[7,256,256]{2,1,0:T(8,128)(2,1)S(1)} %copy-done.2, bf16[16,64,256]{2,1,0:T(8,128)(2,1)S(1)} %get-tuple-element.76.rest_0_, ...), custom_call_target="tpu_custom_call" | custom-call | flops 4294967296 | bytes 16777216 | tf_op jit(solution)/shard_map/depth_step/pallas_call | solution.py:499
  54.1 1.3 %collective-permute-start.17 = (bf16[2,64,512]{2,1,0:T(8,128)(2,1)S(1)}, bf16[2,64,512]{2,1,0:T(8,128)(2,1)S(1)}, u32[]{:S(2)}, u32[]{:S(2)}) collective-permute-start(bf16[2,64,512]{2,1,0:T(8,128)(2,1)S(1)} %get-tuple-element.92), channel_id=1, source_target_pairs={{0,16},{8,24},{16,0},{24,8},{1,17},{9,25},{17,1},{25,9},{2,18},{10... | collective-permute-start | bytes 393224 | tf_op jit(solution)/shard_map/ppermute | solution.py:599
  55.6 4.9 %end_step.1 = (bf16[2,64,512]{2,1,0:T(8,128)(2,1)S(1)}, bf16[2,64,512]{2,1,0:T(8,128)(2,1)S(1)}) custom-call(bf16[2,512,512]{2,1,0:T(8,128)(2,1)S(1)} %get-tuple-element.78.w_ref, f32[6,8,128]{2,1,0:T(8,128)S(1)} %get-tuple-element.71.refs_ref, bf16[7,256,256]{2,1,0:T(8,128)(2,1)S(1)} %copy-done.2, bf16[8,64,256]{2,1,0:T(8,128)(2,1)S(1)} %collective-permute-done.14.rest_0_, ...), custom_call_target="tpu_custom_call" | custom-call | flops 4294967296 | bytes 16777216 | tf_op jit(solution)/shard_map/end_step/pallas_call | solution.py:499
  62.3 1.0 %collective-permute-done.22.refs_1_ = bf16[2,64,512]{2,1,0:T(8,128)(2,1)S(1)} collective-permute-done((bf16[2,64,512]{2,1,0:T(8,128)(2,1)S(1)}, bf16[2,64,512]{2,1,0:T(8,128)(2,1)S(1)}, u32[]{:S(2)}, u32[]{:S(2)}) %collective-permute-start.22) | collective-permute-done | bytes 131104 | tf_op jit(solution)/shard_map/ppermute | solution.py:599
  (61 shorter events, 9.8 us)
Async XLA Ops:
  1.0 10.7 %collective-permute-start.5 = (bf16[2,64,512]{2,1,0:T(8,128)(2,1)S(1)}, bf16[2,64,512]{2,1,0:T(8,128)(2,1)S(1)}, u32[]{:S(2)}, u32[]{:S(2)}) collective-permute-start(bf16[2,64,512]{2,1,0:T(8,128)(2,1)S(1)} %bitcast.36), channel_id=1, source_target_pairs={{0,4},{1,5},{2,6},{3,7},{4,0},{5,1},{6,2},{7,3},{8,12},{9,13},{10,... | collective-permute-start | bytes 393224 | tf_op jit(solution)/shard_map/ppermute | solution.py:599
  6.1 17.1 %collective-permute-start = (bf16[2,144,256]{2,1,0:T(8,128)(2,1)S(1)}, bf16[2,144,256]{2,1,0:T(8,128)(2,1)S(1)}, u32[]{:S(2)}, u32[]{:S(2)}) collective-permute-start(bf16[2,144,256]{2,1,0:T(8,128)(2,1)S(1)} %pad_maximum_fusion.5.refs_0_), channel_id=1, source_target_pairs={{0,8},{8,0},{16,24},{24,16},{1,9},{9,1},{17,25},{25,17},{2,10},{10... | collective-permute-start | bytes 442376 | tf_op jit(solution)/shard_map/ppermute | solution.py:599
  6.2 11.2 %collective-permute-start.3 = (bf16[128,256]{1,0:T(8,128)(2,1)S(1)}, bf16[128,256]{1,0:T(8,128)(2,1)S(1)}, u32[]{:S(2)}, u32[]{:S(2)}) collective-permute-start(bf16[128,256]{1,0:T(8,128)(2,1)S(1)} %slice.50), channel_id=1, source_target_pairs={{0,20},{1,21},{2,22},{3,23},{4,16},{5,17},{6,18},{7,19},{8,28},{9,... | collective-permute-start | bytes 196616 | tf_op jit(solution)/shard_map/ppermute | solution.py:599
  7.5 11.2 %collective-permute-start.4 = (bf16[128,256]{1,0:T(8,128)(2,1)S(1)}, bf16[128,256]{1,0:T(8,128)(2,1)S(1)}, u32[]{:S(2)}, u32[]{:S(2)}) collective-permute-start(bf16[128,256]{1,0:T(8,128)(2,1)S(1)} %slice.51), channel_id=1, source_target_pairs={{0,28},{1,29},{2,30},{3,31},{4,24},{5,25},{6,26},{7,27},{8,20},{9,... | collective-permute-start | bytes 196616 | tf_op jit(solution)/shard_map/ppermute | solution.py:599
  11.8 11.4 %collective-permute-start.6 = (bf16[2,64,512]{2,1,0:T(8,128)(2,1)S(1)}, bf16[2,64,512]{2,1,0:T(8,128)(2,1)S(1)}, u32[]{:S(2)}, u32[]{:S(2)}) collective-permute-start(bf16[2,64,512]{2,1,0:T(8,128)(2,1)S(1)} %pad_maximum_fusion.6), channel_id=1, source_target_pairs={{0,2},{1,3},{2,0},{3,1},{4,6},{5,7},{6,4},{7,5},{8,10},{9,11},{10,... | collective-permute-start | bytes 393224 | tf_op jit(solution)/shard_map/ppermute | solution.py:599
  15.2 8.0 %collective-permute-start.7 = (bf16[2,64,512]{2,1,0:T(8,128)(2,1)S(1)}, bf16[2,64,512]{2,1,0:T(8,128)(2,1)S(1)}, u32[]{:S(2)}, u32[]{:S(2)}) collective-permute-start(bf16[2,64,512]{2,1,0:T(8,128)(2,1)S(1)} %pad_maximum_fusion.7), channel_id=1, source_target_pairs={{0,1},{1,0},{2,3},{3,2},{4,5},{5,4},{6,7},{7,6},{8,9},{9,8},{10,11... | collective-permute-start | bytes 393224 | tf_op jit(solution)/shard_map/ppermute | solution.py:599
  17.4 4.5 %collective-permute-start.1 = (bf16[144,256]{1,0:T(8,128)(2,1)S(1)}, bf16[144,256]{1,0:T(8,128)(2,1)S(1)}, u32[]{:S(2)}, u32[]{:S(2)}) collective-permute-start(bf16[144,256]{1,0:T(8,128)(2,1)S(1)} %get-tuple-element.95), channel_id=1, source_target_pairs={{0,16},{8,24},{16,0},{24,8},{1,17},{9,25},{17,1},{25,9},{2,18},{10... | collective-permute-start | bytes 221192 | tf_op jit(solution)/shard_map/ppermute | solution.py:599
  18.7 4.5 %collective-permute-start.2 = (bf16[144,256]{1,0:T(8,128)(2,1)S(1)}, bf16[144,256]{1,0:T(8,128)(2,1)S(1)}, u32[]{:S(2)}, u32[]{:S(2)}) collective-permute-start(bf16[144,256]{1,0:T(8,128)(2,1)S(1)} %get-tuple-element.96), channel_id=1, source_target_pairs={{0,24},{8,16},{16,8},{24,0},{1,25},{9,17},{17,9},{25,1},{2,26},{10... | collective-permute-start | bytes 221192 | tf_op jit(solution)/shard_map/ppermute | solution.py:599
  23.9 6.4 %collective-permute-start.10 = (bf16[2,2,64,256]{3,2,1,0:T(8,128)(2,1)S(1)}, bf16[2,2,64,256]{3,2,1,0:T(8,128)(2,1)S(1)}, u32[]{:S(2)}, u32[]{:S(2)}) collective-permute-start(bf16[2,2,64,256]{3,2,1,0:T(8,128)(2,1)S(1)} %get-tuple-element.94.refs_0_.refs_2_), channel_id=1, source_target_pairs={{0,2},{1,3},{2,0},{3,1},{4,6},{5,7},{6,4},{7,5},{8,10},{9,11},{10,... | collective-permute-start | bytes 393224 | tf_op jit(solution)/shard_map/ppermute | solution.py:599
  25.4 6.2 %collective-permute-start.11 = (bf16[2,2,64,256]{3,2,1,0:T(8,128)(2,1)S(1)}, bf16[2,2,64,256]{3,2,1,0:T(8,128)(2,1)S(1)}, u32[]{:S(2)}, u32[]{:S(2)}) collective-permute-start(bf16[2,2,64,256]{3,2,1,0:T(8,128)(2,1)S(1)} %get-tuple-element.93.refs_2_.refs_4_), channel_id=1, source_target_pairs={{0,1},{1,0},{2,3},{3,2},{4,5},{5,4},{6,7},{7,6},{8,9},{9,8},{10,11... | collective-permute-start | bytes 393224 | tf_op jit(solution)/shard_map/ppermute | solution.py:599
  25.9 10.0 %collective-permute-start.9 = (bf16[4,64,512]{2,1,0:T(8,128)(2,1)S(1)}, bf16[4,64,512]{2,1,0:T(8,128)(2,1)S(1)}, u32[]{:S(2)}, u32[]{:S(2)}) collective-permute-start(bf16[4,64,512]{2,1,0:T(8,128)(2,1)S(1)} %pad_maximum_fusion.2), channel_id=1, source_target_pairs={{0,2},{1,3},{2,0},{3,1},{4,6},{5,7},{6,4},{7,5},{8,10},{9,11},{10,... | collective-permute-start | bytes 786440 | tf_op jit(solution)/shard_map/ppermute | solution.py:599
  26.7 10.4 %copy-start.2 = (bf16[7,256,256]{2,1,0:T(8,128)(2,1)S(1)}, bf16[7,256,256]{2,1,0:T(8,128)(2,1)}, u32[]{:S(2)}) copy-start(bf16[7,256,256]{2,1,0:T(8,128)(2,1)} %constant.46.clone.tables) | copy-start | bytes 2752516
  26.7 10.4 %collective-permute-start.8 = (bf16[4,64,512]{2,1,0:T(8,128)(2,1)S(1)}, bf16[4,64,512]{2,1,0:T(8,128)(2,1)S(1)}, u32[]{:S(2)}, u32[]{:S(2)}) collective-permute-start(bf16[4,64,512]{2,1,0:T(8,128)(2,1)S(1)} %pad_maximum_fusion.1), channel_id=1, source_target_pairs={{0,1},{1,0},{2,3},{3,2},{4,5},{5,4},{6,7},{7,6},{8,9},{9,8},{10,11... | collective-permute-start | bytes 786440 | tf_op jit(solution)/shard_map/ppermute | solution.py:599
  31.6 6.4 %collective-permute-start.14 = (bf16[8,64,256]{2,1,0:T(8,128)(2,1)S(1)}, bf16[8,64,256]{2,1,0:T(8,128)(2,1)S(1)}, u32[]{:S(2)}, u32[]{:S(2)}) collective-permute-start(bf16[8,64,256]{2,1,0:T(8,128)(2,1)S(1)} %join_pieces.2), channel_id=1, source_target_pairs={{0,16},{8,24},{16,0},{24,8},{1,17},{9,25},{17,1},{25,9},{2,18},{10... | collective-permute-start | bytes 786440 | tf_op jit(solution)/shard_map/ppermute | solution.py:599
  32.6 8.2 %collective-permute-start.13 = (bf16[4,2,64,256]{3,2,1,0:T(8,128)(2,1)S(1)}, bf16[4,2,64,256]{3,2,1,0:T(8,128)(2,1)S(1)}, u32[]{:S(2)}, u32[]{:S(2)}) collective-permute-start(bf16[4,2,64,256]{3,2,1,0:T(8,128)(2,1)S(1)} %pad_maximum_fusion.4), channel_id=1, source_target_pairs={{0,2},{1,3},{2,0},{3,1},{4,6},{5,7},{6,4},{7,5},{8,10},{9,11},{10,... | collective-permute-start | bytes 786440 | tf_op jit(solution)/shard_map/ppermute | solution.py:599
  33.4 8.2 %collective-permute-start.12 = (bf16[4,2,64,256]{3,2,1,0:T(8,128)(2,1)S(1)}, bf16[4,2,64,256]{3,2,1,0:T(8,128)(2,1)S(1)}, u32[]{:S(2)}, u32[]{:S(2)}) collective-permute-start(bf16[4,2,64,256]{3,2,1,0:T(8,128)(2,1)S(1)} %pad_maximum_fusion.3), channel_id=1, source_target_pairs={{0,1},{1,0},{2,3},{3,2},{4,5},{5,4},{6,7},{7,6},{8,9},{9,8},{10,11... | collective-permute-start | bytes 786440 | tf_op jit(solution)/shard_map/ppermute | solution.py:599
  41.8 2.1 %collective-permute-start.15 = (bf16[16,64,256]{2,1,0:T(8,128)(2,1)S(1)}, bf16[16,64,256]{2,1,0:T(8,128)(2,1)S(1)}, u32[]{:S(2)}, u32[]{:S(2)}) collective-permute-start(bf16[16,64,256]{2,1,0:T(8,128)(2,1)S(1)} %get-tuple-element.73.rest_0_), channel_id=1, source_target_pairs={{0,8},{8,0},{16,24},{24,16},{1,9},{9,1},{17,25},{25,17},{2,10},{10... | collective-permute-start | bytes 1572872 | tf_op jit(solution)/shard_map/ppermute | solution.py:599
  41.9 6.7 %collective-permute-start.16 = (bf16[16,64,256]{2,1,0:T(8,128)(2,1)S(1)}, bf16[16,64,256]{2,1,0:T(8,128)(2,1)S(1)}, u32[]{:S(2)}, u32[]{:S(2)}) collective-permute-start(bf16[16,64,256]{2,1,0:T(8,128)(2,1)S(1)} %get-tuple-element.76.rest_0_), channel_id=1, source_target_pairs={{0,8},{8,0},{16,24},{24,16},{1,9},{9,1},{17,25},{25,17},{2,10},{10... | collective-permute-start | bytes 1572872 | tf_op jit(solution)/shard_map/ppermute | solution.py:599
  42.4 11.1 %collective-permute-start.19 = (bf16[9,64,256]{2,1,0:T(8,128)(2,1)S(1)}, bf16[9,64,256]{2,1,0:T(8,128)(2,1)S(1)}, u32[]{:S(2)}, u32[]{:S(2)}) collective-permute-start(bf16[9,64,256]{2,1,0:T(8,128)(2,1)S(1)} %get-tuple-element.79), channel_id=1, source_target_pairs={{0,16},{8,24},{16,0},{24,8},{1,17},{9,25},{17,1},{25,9},{2,18},{10... | collective-permute-start | bytes 884744 | tf_op jit(solution)/shard_map/ppermute | solution.py:599
  53.5 2.2 %collective-permute-start.21 = (bf16[9,64,256]{2,1,0:T(8,128)(2,1)S(1)}, bf16[9,64,256]{2,1,0:T(8,128)(2,1)S(1)}, u32[]{:S(2)}, u32[]{:S(2)}) collective-permute-start(bf16[9,64,256]{2,1,0:T(8,128)(2,1)S(1)} %collective-permute-done.19.rest_1_), channel_id=1, source_target_pairs={{0,8},{8,0},{16,24},{24,16},{1,9},{9,1},{17,25},{25,17},{2,10},{10... | collective-permute-start | bytes 884744 | tf_op jit(solution)/shard_map/ppermute | solution.py:599
  53.6 2.1 %collective-permute-start.20 = (bf16[8,64,256]{2,1,0:T(8,128)(2,1)S(1)}, bf16[8,64,256]{2,1,0:T(8,128)(2,1)S(1)}, u32[]{:S(2)}, u32[]{:S(2)}) collective-permute-start(bf16[8,64,256]{2,1,0:T(8,128)(2,1)S(1)} %collective-permute-done.14.rest_0_), channel_id=1, source_target_pairs={{0,8},{8,0},{16,24},{24,16},{1,9},{9,1},{17,25},{25,17},{2,10},{10... | collective-permute-start | bytes 786440 | tf_op jit(solution)/shard_map/ppermute | solution.py:599
  54.1 6.5 %collective-permute-start.17 = (bf16[2,64,512]{2,1,0:T(8,128)(2,1)S(1)}, bf16[2,64,512]{2,1,0:T(8,128)(2,1)S(1)}, u32[]{:S(2)}, u32[]{:S(2)}) collective-permute-start(bf16[2,64,512]{2,1,0:T(8,128)(2,1)S(1)} %get-tuple-element.92), channel_id=1, source_target_pairs={{0,16},{8,24},{16,0},{24,8},{1,17},{9,25},{17,1},{25,9},{2,18},{10... | collective-permute-start | bytes 393224 | tf_op jit(solution)/shard_map/ppermute | solution.py:599
  55.5 6.2 %collective-permute-start.18 = (bf16[2,64,512]{2,1,0:T(8,128)(2,1)S(1)}, bf16[2,64,512]{2,1,0:T(8,128)(2,1)S(1)}, u32[]{:S(2)}, u32[]{:S(2)}) collective-permute-start(bf16[2,64,512]{2,1,0:T(8,128)(2,1)S(1)} %get-tuple-element.91), channel_id=1, source_target_pairs={{0,24},{8,16},{16,8},{24,0},{1,25},{9,17},{17,9},{25,1},{2,26},{10... | collective-permute-start | bytes 393224 | tf_op jit(solution)/shard_map/ppermute | solution.py:599
  61.6 1.7 %collective-permute-start.22 = (bf16[2,64,512]{2,1,0:T(8,128)(2,1)S(1)}, bf16[2,64,512]{2,1,0:T(8,128)(2,1)S(1)}, u32[]{:S(2)}, u32[]{:S(2)}) collective-permute-start(bf16[2,64,512]{2,1,0:T(8,128)(2,1)S(1)} %get-tuple-element.86), channel_id=1, source_target_pairs={{0,8},{8,0},{16,24},{24,16},{1,9},{9,1},{17,25},{25,17},{2,10},{10... | collective-permute-start | bytes 393224 | tf_op jit(solution)/shard_map/ppermute | solution.py:599
  (4 other events, 22.6 us)

commit v6 on v5

--- a/solution.py
+++ b/solution.py
@@ -735,7 +735,6 @@
 
     far = [swap(payload_for(i * rep), "depth", i * rep) for i in range(freq_count, chains)]
     near = [payload_for(i * rep) for i in range(freq_count)]
-    far, near = lax.optimization_barrier((far, near))
     fields = [f if i == 0 else swap(f, "depth", i * rep) for i, f in enumerate(near)] + far
     return run_image(plan, refs, fields, adjoint_bottom)
 

time: 64.2 us -> 63.3 us (0.986)
  waiting for transfers between devices: 20.2 us -> 19.2 us
    ppermute x23, waiting for transfers between devices: 20.2 us -> 19.2 us  [swap(): return lax.ppermute(values, axis, [(i, i ^ mask) for i in range(size)])]
where the time goes in v6:
time: 63.3 us; the launch traced here: 63.2 us
  starting transfers between devices  25.1 us (40%)
  waiting for transfers between devices  19.2 us (30%)
  Pallas kernels  16.3 us (26%)
  other arithmetic  1.53 us (2%)
  between operations  0.92 us (1%)
    ppermute x23, starting transfers between devices, swap(): return lax.ppermute(values, axis, [(i, i ^ mask) for i in range(size)])  25.1 us
    ppermute x23, waiting for transfers between devices, swap(): return lax.ppermute(values, axis, [(i, i ^ mask) for i in range(size)])  19.2 us
    pallas_call x3, Pallas kernels, run_step(): pl.pallas_call(partial(step_kernel, dims, orders, plan, index, len(coefs)...  14.4 us
  transfers between devices with their start and end apart: 23, of which 13 were waited for; matrix products, arithmetic and copies ran while one was open for 1% of the time, Pallas kernels for 23%

profile of v6, /device:TPU:0, one launch (start us, length us, event | category | flops | bytes accessed | tf_op | source)
XLA Modules:
  0.0 63.2 jit_solution(4135871723200519140)
XLA Ops:
  0.0 1.0 %dynamic-slice_select_fusion = bf16[1,2,64,512]{3,2,1,0:T(8,128)(2,1)S(1)} fusion(bf16[2,2,64,512]{3,2,1,0:T(8,128)(2,1)} %refs_4_.1, s32[]{:T(128)S(6)} %select_n.50, bf16[2,2,64,512]{3,2,1,0:T(8,128)(2,1)} %param.7, pred[]{:T(512)S(6)} %eq.5), kind=kLoop, calls=%fused_computation.21 | loop fusion | flops 65536 | bytes 393221 | tf_op jit(solution)/shard_map/jit(_where)/select_n | solution.py:666
  1.0 4.1 %collective-permute-start.5 = (bf16[2,64,512]{2,1,0:T(8,128)(2,1)S(1)}, bf16[2,64,512]{2,1,0:T(8,128)(2,1)S(1)}, u32[]{:S(2)}, u32[]{:S(2)}) collective-permute-start(bf16[2,64,512]{2,1,0:T(8,128)(2,1)S(1)} %bitcast.36), channel_id=1, source_target_pairs={{0,4},{1,5},{2,6},{3,7},{4,0},{5,1},{6,2},{7,3},{8,12},{9,13},{10,... | collective-permute-start | bytes 393224 | tf_op jit(solution)/shard_map/ppermute | solution.py:599
  6.2 1.3 %collective-permute-start.3 = (bf16[128,256]{1,0:T(8,128)(2,1)S(1)}, bf16[128,256]{1,0:T(8,128)(2,1)S(1)}, u32[]{:S(2)}, u32[]{:S(2)}) collective-permute-start(bf16[128,256]{1,0:T(8,128)(2,1)S(1)} %slice.50), channel_id=1, source_target_pairs={{0,20},{1,21},{2,22},{3,23},{4,16},{5,17},{6,18},{7,19},{8,28},{9,... | collective-permute-start | bytes 196616 | tf_op jit(solution)/shard_map/ppermute | solution.py:599
  7.5 2.3 %collective-permute-start.4 = (bf16[128,256]{1,0:T(8,128)(2,1)S(1)}, bf16[128,256]{1,0:T(8,128)(2,1)S(1)}, u32[]{:S(2)}, u32[]{:S(2)}) collective-permute-start(bf16[128,256]{1,0:T(8,128)(2,1)S(1)} %slice.51), channel_id=1, source_target_pairs={{0,28},{1,29},{2,30},{3,31},{4,24},{5,25},{6,26},{7,27},{8,20},{9,... | collective-permute-start | bytes 196616 | tf_op jit(solution)/shard_map/ppermute | solution.py:599
  9.8 1.9 %collective-permute-done.5 = bf16[2,64,512]{2,1,0:T(8,128)(2,1)S(1)} collective-permute-done((bf16[2,64,512]{2,1,0:T(8,128)(2,1)S(1)}, bf16[2,64,512]{2,1,0:T(8,128)(2,1)S(1)}, u32[]{:S(2)}, u32[]{:S(2)}) %collective-permute-start.5) | collective-permute-done | bytes 131104 | tf_op jit(solution)/shard_map/ppermute | solution.py:599
  11.8 3.4 %collective-permute-start.6 = (bf16[2,64,512]{2,1,0:T(8,128)(2,1)S(1)}, bf16[2,64,512]{2,1,0:T(8,128)(2,1)S(1)}, u32[]{:S(2)}, u32[]{:S(2)}) collective-permute-start(bf16[2,64,512]{2,1,0:T(8,128)(2,1)S(1)} %pad_maximum_fusion.6), channel_id=1, source_target_pairs={{0,2},{1,3},{2,0},{3,1},{4,6},{5,7},{6,4},{7,5},{8,10},{9,11},{10,... | collective-permute-start | bytes 393224 | tf_op jit(solution)/shard_map/ppermute | solution.py:599
  15.2 1.6 %collective-permute-start.7 = (bf16[2,64,512]{2,1,0:T(8,128)(2,1)S(1)}, bf16[2,64,512]{2,1,0:T(8,128)(2,1)S(1)}, u32[]{:S(2)}, u32[]{:S(2)}) collective-permute-start(bf16[2,64,512]{2,1,0:T(8,128)(2,1)S(1)} %pad_maximum_fusion.7), channel_id=1, source_target_pairs={{0,1},{1,0},{2,3},{3,2},{4,5},{5,4},{6,7},{7,6},{8,9},{9,8},{10,11... | collective-permute-start | bytes 393224 | tf_op jit(solution)/shard_map/ppermute | solution.py:599
  17.4 1.3 %collective-permute-start.1 = (bf16[144,256]{1,0:T(8,128)(2,1)S(1)}, bf16[144,256]{1,0:T(8,128)(2,1)S(1)}, u32[]{:S(2)}, u32[]{:S(2)}) collective-permute-start(bf16[144,256]{1,0:T(8,128)(2,1)S(1)} %get-tuple-element.87), channel_id=1, source_target_pairs={{0,16},{8,24},{16,0},{24,8},{1,17},{9,25},{17,1},{25,9},{2,18},{10... | collective-permute-start | bytes 221192 | tf_op jit(solution)/shard_map/ppermute | solution.py:599
  18.7 3.2 %collective-permute-done.1.refs_2_ = bf16[144,256]{1,0:T(8,128)(2,1)S(1)} collective-permute-done((bf16[144,256]{1,0:T(8,128)(2,1)S(1)}, bf16[144,256]{1,0:T(8,128)(2,1)S(1)}, u32[]{:S(2)}, u32[]{:S(2)}) %collective-permute-start.1) | collective-permute-done | bytes 73760 | tf_op jit(solution)/shard_map/ppermute | solution.py:599
  21.9 1.3 %collective-permute-done.2.refs_3_ = bf16[144,256]{1,0:T(8,128)(2,1)S(1)} collective-permute-done((bf16[144,256]{1,0:T(8,128)(2,1)S(1)}, bf16[144,256]{1,0:T(8,128)(2,1)S(1)}, u32[]{:S(2)}, u32[]{:S(2)}) %collective-permute-start.2) | collective-permute-done | bytes 73760 | tf_op jit(solution)/shard_map/ppermute | solution.py:599
  23.9 1.4 %collective-permute-start.10 = (bf16[2,2,64,256]{3,2,1,0:T(8,128)(2,1)S(1)}, bf16[2,2,64,256]{3,2,1,0:T(8,128)(2,1)S(1)}, u32[]{:S(2)}, u32[]{:S(2)}) collective-permute-start(bf16[2,2,64,256]{3,2,1,0:T(8,128)(2,1)S(1)} %get-tuple-element.86.refs_0_.refs_2_), channel_id=1, source_target_pairs={{0,2},{1,3},{2,0},{3,1},{4,6},{5,7},{6,4},{7,5},{8,10},{9,11},{10,... | collective-permute-start | bytes 393224 | tf_op jit(solution)/shard_map/ppermute | solution.py:599
  26.7 1.5 %collective-permute-start.8 = (bf16[4,64,512]{2,1,0:T(8,128)(2,1)S(1)}, bf16[4,64,512]{2,1,0:T(8,128)(2,1)S(1)}, u32[]{:S(2)}, u32[]{:S(2)}) collective-permute-start(bf16[4,64,512]{2,1,0:T(8,128)(2,1)S(1)} %pad_maximum_fusion.1), channel_id=1, source_target_pairs={{0,1},{1,0},{2,3},{3,2},{4,5},{5,4},{6,7},{7,6},{8,9},{9,8},{10,11... | collective-permute-start | bytes 786440 | tf_op jit(solution)/shard_map/ppermute | solution.py:599
  28.3 2.1 %collective-permute-done.10.refs_1_.refs_3_ = bf16[2,2,64,256]{3,2,1,0:T(8,128)(2,1)S(1)} collective-permute-done((bf16[2,2,64,256]{3,2,1,0:T(8,128)(2,1)S(1)}, bf16[2,2,64,256]{3,2,1,0:T(8,128)(2,1)S(1)}, u32[]{:S(2)}, u32[]{:S(2)}) %collective-permute-start.10) | collective-permute-done | bytes 131104 | tf_op jit(solution)/shard_map/ppermute | solution.py:599
  30.3 1.2 %collective-permute-done.11.refs_3_.refs_5_ = bf16[2,2,64,256]{3,2,1,0:T(8,128)(2,1)S(1)} collective-permute-done((bf16[2,2,64,256]{3,2,1,0:T(8,128)(2,1)S(1)}, bf16[2,2,64,256]{3,2,1,0:T(8,128)(2,1)S(1)}, u32[]{:S(2)}, u32[]{:S(2)}) %collective-permute-start.11) | collective-permute-done | bytes 131104 | tf_op jit(solution)/shard_map/ppermute | solution.py:599
  31.6 1.0 %collective-permute-start.14 = (bf16[8,64,256]{2,1,0:T(8,128)(2,1)S(1)}, bf16[8,64,256]{2,1,0:T(8,128)(2,1)S(1)}, u32[]{:S(2)}, u32[]{:S(2)}) collective-permute-start(bf16[8,64,256]{2,1,0:T(8,128)(2,1)S(1)} %join_pieces.2), channel_id=1, source_target_pairs={{0,16},{8,24},{16,0},{24,8},{1,17},{9,25},{17,1},{25,9},{2,18},{10... | collective-permute-start | bytes 786440 | tf_op jit(solution)/shard_map/ppermute | solution.py:599
  33.5 2.5 %collective-permute-done.9.rest_7_ = bf16[4,64,512]{2,1,0:T(8,128)(2,1)S(1)} collective-permute-done((bf16[4,64,512]{2,1,0:T(8,128)(2,1)S(1)}, bf16[4,64,512]{2,1,0:T(8,128)(2,1)S(1)}, u32[]{:S(2)}, u32[]{:S(2)}) %collective-permute-start.9) | collective-permute-done | bytes 262176 | tf_op jit(solution)/shard_map/ppermute | solution.py:599
  36.0 1.2 %collective-permute-done.8.rest_3_ = bf16[4,64,512]{2,1,0:T(8,128)(2,1)S(1)} collective-permute-done((bf16[4,64,512]{2,1,0:T(8,128)(2,1)S(1)}, bf16[4,64,512]{2,1,0:T(8,128)(2,1)S(1)}, u32[]{:S(2)}, u32[]{:S(2)}) %collective-permute-start.8) | collective-permute-done | bytes 262176 | tf_op jit(solution)/shard_map/ppermute | solution.py:599
  38.0 2.7 %collective-permute-done.13.refs_7_ = bf16[4,2,64,256]{3,2,1,0:T(8,128)(2,1)S(1)} collective-permute-done((bf16[4,2,64,256]{3,2,1,0:T(8,128)(2,1)S(1)}, bf16[4,2,64,256]{3,2,1,0:T(8,128)(2,1)S(1)}, u32[]{:S(2)}, u32[]{:S(2)}) %collective-permute-start.13) | collective-permute-done | bytes 262176 | tf_op jit(solution)/shard_map/ppermute | solution.py:599
  40.8 0.8 %collective-permute-done.12.refs_6_ = bf16[4,2,64,256]{3,2,1,0:T(8,128)(2,1)S(1)} collective-permute-done((bf16[4,2,64,256]{3,2,1,0:T(8,128)(2,1)S(1)}, bf16[4,2,64,256]{3,2,1,0:T(8,128)(2,1)S(1)}, u32[]{:S(2)}, u32[]{:S(2)}) %collective-permute-start.12) | collective-permute-done | bytes 262176 | tf_op jit(solution)/shard_map/ppermute | solution.py:599
  42.4 1.5 %collective-permute-start.17 = (bf16[9,64,256]{2,1,0:T(8,128)(2,1)S(1)}, bf16[9,64,256]{2,1,0:T(8,128)(2,1)S(1)}, u32[]{:S(2)}, u32[]{:S(2)}) collective-permute-start(bf16[9,64,256]{2,1,0:T(8,128)(2,1)S(1)} %get-tuple-element.74), channel_id=1, source_target_pairs={{0,16},{8,24},{16,0},{24,8},{1,17},{9,25},{17,1},{25,9},{2,18},{10... | collective-permute-start | bytes 884744 | tf_op jit(solution)/shard_map/ppermute | solution.py:599
  43.9 4.7 %depth_step.2 = (bf16[2,512,512]{2,1,0:T(8,128)(2,1)S(1)}, bf16[2,64,512]{2,1,0:T(8,128)(2,1)S(1)}) custom-call(bf16[2,512,512]{2,1,0:T(8,128)(2,1)S(1)} %get-tuple-element.68.w_ref, f32[6,8,128]{2,1,0:T(8,128)S(1)} %get-tuple-element.67.refs_ref, bf16[7,256,256]{2,1,0:T(8,128)(2,1)S(1)} %copy-done.2, bf16[16,64,256]{2,1,0:T(8,128)(2,1)S(1)} %get-tuple-element.69.rest_0_, ...), custom_call_target="tpu_custom_call" | custom-call | flops 4294967296 | bytes 16777216 | tf_op jit(solution)/shard_map/depth_step/pallas_call | solution.py:499
  48.6 4.9 %depth_step.3 = (bf16[2,512,512]{2,1,0:T(8,128)(2,1)S(1)}, bf16[2,64,512]{2,1,0:T(8,128)(2,1)S(1)}) custom-call(bf16[2,512,512]{2,1,0:T(8,128)(2,1)S(1)} %get-tuple-element.70.w_ref, f32[6,8,128]{2,1,0:T(8,128)S(1)} %get-tuple-element.67.refs_ref, bf16[7,256,256]{2,1,0:T(8,128)(2,1)S(1)} %copy-done.2, bf16[16,64,256]{2,1,0:T(8,128)(2,1)S(1)} %get-tuple-element.71.rest_0_, ...), custom_call_target="tpu_custom_call" | custom-call | flops 4294967296 | bytes 16777216 | tf_op jit(solution)/shard_map/depth_step/pallas_call | solution.py:499
  54.1 1.3 %collective-permute-start.21 = (bf16[2,64,512]{2,1,0:T(8,128)(2,1)S(1)}, bf16[2,64,512]{2,1,0:T(8,128)(2,1)S(1)}, u32[]{:S(2)}, u32[]{:S(2)}) collective-permute-start(bf16[2,64,512]{2,1,0:T(8,128)(2,1)S(1)} %get-tuple-element.84), channel_id=1, source_target_pairs={{0,16},{8,24},{16,0},{24,8},{1,17},{9,25},{17,1},{25,9},{2,18},{10... | collective-permute-start | bytes 393224 | tf_op jit(solution)/shard_map/ppermute | solution.py:599
  55.6 4.9 %end_step.1 = (bf16[2,64,512]{2,1,0:T(8,128)(2,1)S(1)}, bf16[2,64,512]{2,1,0:T(8,128)(2,1)S(1)}) custom-call(bf16[2,512,512]{2,1,0:T(8,128)(2,1)S(1)} %get-tuple-element.73.w_ref, f32[6,8,128]{2,1,0:T(8,128)S(1)} %get-tuple-element.67.refs_ref, bf16[7,256,256]{2,1,0:T(8,128)(2,1)S(1)} %copy-done.2, bf16[8,64,256]{2,1,0:T(8,128)(2,1)S(1)} %collective-permute-done.14.rest_0_, ...), custom_call_target="tpu_custom_call" | custom-call | flops 4294967296 | bytes 16777216 | tf_op jit(solution)/shard_map/end_step/pallas_call | solution.py:499
  (61 shorter events, 9.0 us)
Async XLA Ops:
  1.0 10.7 %collective-permute-start.5 = (bf16[2,64,512]{2,1,0:T(8,128)(2,1)S(1)}, bf16[2,64,512]{2,1,0:T(8,128)(2,1)S(1)}, u32[]{:S(2)}, u32[]{:S(2)}) collective-permute-start(bf16[2,64,512]{2,1,0:T(8,128)(2,1)S(1)} %bitcast.36), channel_id=1, source_target_pairs={{0,4},{1,5},{2,6},{3,7},{4,0},{5,1},{6,2},{7,3},{8,12},{9,13},{10,... | collective-permute-start | bytes 393224 | tf_op jit(solution)/shard_map/ppermute | solution.py:599
  6.1 17.1 %collective-permute-start = (bf16[2,144,256]{2,1,0:T(8,128)(2,1)S(1)}, bf16[2,144,256]{2,1,0:T(8,128)(2,1)S(1)}, u32[]{:S(2)}, u32[]{:S(2)}) collective-permute-start(bf16[2,144,256]{2,1,0:T(8,128)(2,1)S(1)} %pad_maximum_fusion.5.refs_0_), channel_id=1, source_target_pairs={{0,8},{8,0},{16,24},{24,16},{1,9},{9,1},{17,25},{25,17},{2,10},{10... | collective-permute-start | bytes 442376 | tf_op jit(solution)/shard_map/ppermute | solution.py:599
  6.2 11.2 %collective-permute-start.3 = (bf16[128,256]{1,0:T(8,128)(2,1)S(1)}, bf16[128,256]{1,0:T(8,128)(2,1)S(1)}, u32[]{:S(2)}, u32[]{:S(2)}) collective-permute-start(bf16[128,256]{1,0:T(8,128)(2,1)S(1)} %slice.50), channel_id=1, source_target_pairs={{0,20},{1,21},{2,22},{3,23},{4,16},{5,17},{6,18},{7,19},{8,28},{9,... | collective-permute-start | bytes 196616 | tf_op jit(solution)/shard_map/ppermute | solution.py:599
  7.5 11.2 %collective-permute-start.4 = (bf16[128,256]{1,0:T(8,128)(2,1)S(1)}, bf16[128,256]{1,0:T(8,128)(2,1)S(1)}, u32[]{:S(2)}, u32[]{:S(2)}) collective-permute-start(bf16[128,256]{1,0:T(8,128)(2,1)S(1)} %slice.51), channel_id=1, source_target_pairs={{0,28},{1,29},{2,30},{3,31},{4,24},{5,25},{6,26},{7,27},{8,20},{9,... | collective-permute-start | bytes 196616 | tf_op jit(solution)/shard_map/ppermute | solution.py:599
  11.8 11.4 %collective-permute-start.6 = (bf16[2,64,512]{2,1,0:T(8,128)(2,1)S(1)}, bf16[2,64,512]{2,1,0:T(8,128)(2,1)S(1)}, u32[]{:S(2)}, u32[]{:S(2)}) collective-permute-start(bf16[2,64,512]{2,1,0:T(8,128)(2,1)S(1)} %pad_maximum_fusion.6), channel_id=1, source_target_pairs={{0,2},{1,3},{2,0},{3,1},{4,6},{5,7},{6,4},{7,5},{8,10},{9,11},{10,... | collective-permute-start | bytes 393224 | tf_op jit(solution)/shard_map/ppermute | solution.py:599
  15.2 8.0 %collective-permute-start.7 = (bf16[2,64,512]{2,1,0:T(8,128)(2,1)S(1)}, bf16[2,64,512]{2,1,0:T(8,128)(2,1)S(1)}, u32[]{:S(2)}, u32[]{:S(2)}) collective-permute-start(bf16[2,64,512]{2,1,0:T(8,128)(2,1)S(1)} %pad_maximum_fusion.7), channel_id=1, source_target_pairs={{0,1},{1,0},{2,3},{3,2},{4,5},{5,4},{6,7},{7,6},{8,9},{9,8},{10,11... | collective-permute-start | bytes 393224 | tf_op jit(solution)/shard_map/ppermute | solution.py:599
  17.4 4.5 %collective-permute-start.1 = (bf16[144,256]{1,0:T(8,128)(2,1)S(1)}, bf16[144,256]{1,0:T(8,128)(2,1)S(1)}, u32[]{:S(2)}, u32[]{:S(2)}) collective-permute-start(bf16[144,256]{1,0:T(8,128)(2,1)S(1)} %get-tuple-element.87), channel_id=1, source_target_pairs={{0,16},{8,24},{16,0},{24,8},{1,17},{9,25},{17,1},{25,9},{2,18},{10... | collective-permute-start | bytes 221192 | tf_op jit(solution)/shard_map/ppermute | solution.py:599
  18.7 4.5 %collective-permute-start.2 = (bf16[144,256]{1,0:T(8,128)(2,1)S(1)}, bf16[144,256]{1,0:T(8,128)(2,1)S(1)}, u32[]{:S(2)}, u32[]{:S(2)}) collective-permute-start(bf16[144,256]{1,0:T(8,128)(2,1)S(1)} %get-tuple-element.88), channel_id=1, source_target_pairs={{0,24},{8,16},{16,8},{24,0},{1,25},{9,17},{17,9},{25,1},{2,26},{10... | collective-permute-start | bytes 221192 | tf_op jit(solution)/shard_map/ppermute | solution.py:599
  23.9 6.4 %collective-permute-start.10 = (bf16[2,2,64,256]{3,2,1,0:T(8,128)(2,1)S(1)}, bf16[2,2,64,256]{3,2,1,0:T(8,128)(2,1)S(1)}, u32[]{:S(2)}, u32[]{:S(2)}) collective-permute-start(bf16[2,2,64,256]{3,2,1,0:T(8,128)(2,1)S(1)} %get-tuple-element.86.refs_0_.refs_2_), channel_id=1, source_target_pairs={{0,2},{1,3},{2,0},{3,1},{4,6},{5,7},{6,4},{7,5},{8,10},{9,11},{10,... | collective-permute-start | bytes 393224 | tf_op jit(solution)/shard_map/ppermute | solution.py:599
  25.4 6.2 %collective-permute-start.11 = (bf16[2,2,64,256]{3,2,1,0:T(8,128)(2,1)S(1)}, bf16[2,2,64,256]{3,2,1,0:T(8,128)(2,1)S(1)}, u32[]{:S(2)}, u32[]{:S(2)}) collective-permute-start(bf16[2,2,64,256]{3,2,1,0:T(8,128)(2,1)S(1)} %get-tuple-element.85.refs_2_.refs_4_), channel_id=1, source_target_pairs={{0,1},{1,0},{2,3},{3,2},{4,5},{5,4},{6,7},{7,6},{8,9},{9,8},{10,11... | collective-permute-start | bytes 393224 | tf_op jit(solution)/shard_map/ppermute | solution.py:599
  25.9 10.0 %collective-permute-start.9 = (bf16[4,64,512]{2,1,0:T(8,128)(2,1)S(1)}, bf16[4,64,512]{2,1,0:T(8,128)(2,1)S(1)}, u32[]{:S(2)}, u32[]{:S(2)}) collective-permute-start(bf16[4,64,512]{2,1,0:T(8,128)(2,1)S(1)} %pad_maximum_fusion.2), channel_id=1, source_target_pairs={{0,2},{1,3},{2,0},{3,1},{4,6},{5,7},{6,4},{7,5},{8,10},{9,11},{10,... | collective-permute-start | bytes 786440 | tf_op jit(solution)/shard_map/ppermute | solution.py:599
  26.7 10.4 %copy-start.2 = (bf16[7,256,256]{2,1,0:T(8,128)(2,1)S(1)}, bf16[7,256,256]{2,1,0:T(8,128)(2,1)}, u32[]{:S(2)}) copy-start(bf16[7,256,256]{2,1,0:T(8,128)(2,1)} %constant.46.clone.tables) | copy-start | bytes 2752516
  26.7 10.4 %collective-permute-start.8 = (bf16[4,64,512]{2,1,0:T(8,128)(2,1)S(1)}, bf16[4,64,512]{2,1,0:T(8,128)(2,1)S(1)}, u32[]{:S(2)}, u32[]{:S(2)}) collective-permute-start(bf16[4,64,512]{2,1,0:T(8,128)(2,1)S(1)} %pad_maximum_fusion.1), channel_id=1, source_target_pairs={{0,1},{1,0},{2,3},{3,2},{4,5},{5,4},{6,7},{7,6},{8,9},{9,8},{10,11... | collective-permute-start | bytes 786440 | tf_op jit(solution)/shard_map/ppermute | solution.py:599
  31.6 6.4 %collective-permute-start.14 = (bf16[8,64,256]{2,1,0:T(8,128)(2,1)S(1)}, bf16[8,64,256]{2,1,0:T(8,128)(2,1)S(1)}, u32[]{:S(2)}, u32[]{:S(2)}) collective-permute-start(bf16[8,64,256]{2,1,0:T(8,128)(2,1)S(1)} %join_pieces.2), channel_id=1, source_target_pairs={{0,16},{8,24},{16,0},{24,8},{1,17},{9,25},{17,1},{25,9},{2,18},{10... | collective-permute-start | bytes 786440 | tf_op jit(solution)/shard_map/ppermute | solution.py:599
  32.6 8.2 %collective-permute-start.13 = (bf16[4,2,64,256]{3,2,1,0:T(8,128)(2,1)S(1)}, bf16[4,2,64,256]{3,2,1,0:T(8,128)(2,1)S(1)}, u32[]{:S(2)}, u32[]{:S(2)}) collective-permute-start(bf16[4,2,64,256]{3,2,1,0:T(8,128)(2,1)S(1)} %pad_maximum_fusion.4), channel_id=1, source_target_pairs={{0,2},{1,3},{2,0},{3,1},{4,6},{5,7},{6,4},{7,5},{8,10},{9,11},{10,... | collective-permute-start | bytes 786440 | tf_op jit(solution)/shard_map/ppermute | solution.py:599
  33.4 8.2 %collective-permute-start.12 = (bf16[4,2,64,256]{3,2,1,0:T(8,128)(2,1)S(1)}, bf16[4,2,64,256]{3,2,1,0:T(8,128)(2,1)S(1)}, u32[]{:S(2)}, u32[]{:S(2)}) collective-permute-start(bf16[4,2,64,256]{3,2,1,0:T(8,128)(2,1)S(1)} %pad_maximum_fusion.3), channel_id=1, source_target_pairs={{0,1},{1,0},{2,3},{3,2},{4,5},{5,4},{6,7},{7,6},{8,9},{9,8},{10,11... | collective-permute-start | bytes 786440 | tf_op jit(solution)/shard_map/ppermute | solution.py:599
  41.8 2.1 %collective-permute-start.15 = (bf16[16,64,256]{2,1,0:T(8,128)(2,1)S(1)}, bf16[16,64,256]{2,1,0:T(8,128)(2,1)S(1)}, u32[]{:S(2)}, u32[]{:S(2)}) collective-permute-start(bf16[16,64,256]{2,1,0:T(8,128)(2,1)S(1)} %get-tuple-element.69.rest_0_), channel_id=1, source_target_pairs={{0,8},{8,0},{16,24},{24,16},{1,9},{9,1},{17,25},{25,17},{2,10},{10... | collective-permute-start | bytes 1572872 | tf_op jit(solution)/shard_map/ppermute | solution.py:599
  41.9 6.7 %collective-permute-start.16 = (bf16[16,64,256]{2,1,0:T(8,128)(2,1)S(1)}, bf16[16,64,256]{2,1,0:T(8,128)(2,1)S(1)}, u32[]{:S(2)}, u32[]{:S(2)}) collective-permute-start(bf16[16,64,256]{2,1,0:T(8,128)(2,1)S(1)} %get-tuple-element.71.rest_0_), channel_id=1, source_target_pairs={{0,8},{8,0},{16,24},{24,16},{1,9},{9,1},{17,25},{25,17},{2,10},{10... | collective-permute-start | bytes 1572872 | tf_op jit(solution)/shard_map/ppermute | solution.py:599
  42.4 11.1 %collective-permute-start.17 = (bf16[9,64,256]{2,1,0:T(8,128)(2,1)S(1)}, bf16[9,64,256]{2,1,0:T(8,128)(2,1)S(1)}, u32[]{:S(2)}, u32[]{:S(2)}) collective-permute-start(bf16[9,64,256]{2,1,0:T(8,128)(2,1)S(1)} %get-tuple-element.74), channel_id=1, source_target_pairs={{0,16},{8,24},{16,0},{24,8},{1,17},{9,25},{17,1},{25,9},{2,18},{10... | collective-permute-start | bytes 884744 | tf_op jit(solution)/shard_map/ppermute | solution.py:599
  53.5 2.2 %collective-permute-start.19 = (bf16[9,64,256]{2,1,0:T(8,128)(2,1)S(1)}, bf16[9,64,256]{2,1,0:T(8,128)(2,1)S(1)}, u32[]{:S(2)}, u32[]{:S(2)}) collective-permute-start(bf16[9,64,256]{2,1,0:T(8,128)(2,1)S(1)} %collective-permute-done.17.rest_1_), channel_id=1, source_target_pairs={{0,8},{8,0},{16,24},{24,16},{1,9},{9,1},{17,25},{25,17},{2,10},{10... | collective-permute-start | bytes 884744 | tf_op jit(solution)/shard_map/ppermute | solution.py:599
  53.6 2.1 %collective-permute-start.18 = (bf16[8,64,256]{2,1,0:T(8,128)(2,1)S(1)}, bf16[8,64,256]{2,1,0:T(8,128)(2,1)S(1)}, u32[]{:S(2)}, u32[]{:S(2)}) collective-permute-start(bf16[8,64,256]{2,1,0:T(8,128)(2,1)S(1)} %collective-permute-done.14.rest_0_), channel_id=1, source_target_pairs={{0,8},{8,0},{16,24},{24,16},{1,9},{9,1},{17,25},{25,17},{2,10},{10... | collective-permute-start | bytes 786440 | tf_op jit(solution)/shard_map/ppermute | solution.py:599
  54.1 7.3 %collective-permute-start.21 = (bf16[2,64,512]{2,1,0:T(8,128)(2,1)S(1)}, bf16[2,64,512]{2,1,0:T(8,128)(2,1)S(1)}, u32[]{:S(2)}, u32[]{:S(2)}) collective-permute-start(bf16[2,64,512]{2,1,0:T(8,128)(2,1)S(1)} %get-tuple-element.84), channel_id=1, source_target_pairs={{0,16},{8,24},{16,0},{24,8},{1,17},{9,25},{17,1},{25,9},{2,18},{10... | collective-permute-start | bytes 393224 | tf_op jit(solution)/shard_map/ppermute | solution.py:599
  55.5 6.2 %collective-permute-start.22 = (bf16[2,64,512]{2,1,0:T(8,128)(2,1)S(1)}, bf16[2,64,512]{2,1,0:T(8,128)(2,1)S(1)}, u32[]{:S(2)}, u32[]{:S(2)}) collective-permute-start(bf16[2,64,512]{2,1,0:T(8,128)(2,1)S(1)} %get-tuple-element.83), channel_id=1, source_target_pairs={{0,24},{8,16},{16,8},{24,0},{1,25},{9,17},{17,9},{25,1},{2,26},{10... | collective-permute-start | bytes 393224 | tf_op jit(solution)/shard_map/ppermute | solution.py:599
  60.6 1.8 %collective-permute-start.20 = (bf16[2,64,512]{2,1,0:T(8,128)(2,1)S(1)}, bf16[2,64,512]{2,1,0:T(8,128)(2,1)S(1)}, u32[]{:S(2)}, u32[]{:S(2)}) collective-permute-start(bf16[2,64,512]{2,1,0:T(8,128)(2,1)S(1)} %get-tuple-element.81), channel_id=1, source_target_pairs={{0,8},{8,0},{16,24},{24,16},{1,9},{9,1},{17,25},{25,17},{2,10},{10... | collective-permute-start | bytes 393224 | tf_op jit(solution)/shard_map/ppermute | solution.py:599
  (4 other events, 21.7 us)

commit v7 on v6

--- a/solution.py
+++ b/solution.py
@@ -327,7 +327,7 @@
         place.append(
             {o: (i // share, which * share + i % share) for i, o in enumerate(sum(order, []))}
         )
-    step = min(32, rows_here)
+    step = min(16, rows_here)
 
     def portions():
         for offset in range(blocks):

time: 63.3 us -> 63.1 us (level)
  no operation moved by 1% of the time
where the time goes in v7:
time: 63.1 us; the launch traced here: 63 us
  starting transfers between devices  25.1 us (40%)
  waiting for transfers between devices  19.2 us (30%)
  Pallas kernels  16.1 us (26%)
  other arithmetic  1.53 us (2%)
  between operations  0.92 us (1%)
    ppermute x23, starting transfers between devices, swap(): return lax.ppermute(values, axis, [(i, i ^ mask) for i in range(size)])  25.1 us
    ppermute x23, waiting for transfers between devices, swap(): return lax.ppermute(values, axis, [(i, i ^ mask) for i in range(size)])  19.2 us
    pallas_call x3, Pallas kernels, run_step(): pl.pallas_call(partial(step_kernel, dims, orders, plan, index, len(coefs)...  14.2 us
  transfers between devices with their start and end apart: 23, of which 13 were waited for; matrix products, arithmetic and copies ran while one was open for 1% of the time, Pallas kernels for 23%

profile of v7, /device:TPU:0, one launch (start us, length us, event | category | flops | bytes accessed | tf_op | source)
XLA Modules:
  0.0 63.0 jit_solution(16847090984193102369)
XLA Ops:
  0.0 1.0 %dynamic-slice_select_fusion = bf16[1,2,64,512]{3,2,1,0:T(8,128)(2,1)S(1)} fusion(bf16[2,2,64,512]{3,2,1,0:T(8,128)(2,1)} %refs_4_.1, s32[]{:T(128)S(6)} %select_n.50, bf16[2,2,64,512]{3,2,1,0:T(8,128)(2,1)} %param.7, pred[]{:T(512)S(6)} %eq.5), kind=kLoop, calls=%fused_computation.21 | loop fusion | flops 65536 | bytes 393221 | tf_op jit(solution)/shard_map/jit(_where)/select_n | solution.py:666
  1.0 4.1 %collective-permute-start.5 = (bf16[2,64,512]{2,1,0:T(8,128)(2,1)S(1)}, bf16[2,64,512]{2,1,0:T(8,128)(2,1)S(1)}, u32[]{:S(2)}, u32[]{:S(2)}) collective-permute-start(bf16[2,64,512]{2,1,0:T(8,128)(2,1)S(1)} %bitcast.36), channel_id=1, source_target_pairs={{0,4},{1,5},{2,6},{3,7},{4,0},{5,1},{6,2},{7,3},{8,12},{9,13},{10,... | collective-permute-start | bytes 393224 | tf_op jit(solution)/shard_map/ppermute | solution.py:599
  6.2 1.3 %collective-permute-start.3 = (bf16[128,256]{1,0:T(8,128)(2,1)S(1)}, bf16[128,256]{1,0:T(8,128)(2,1)S(1)}, u32[]{:S(2)}, u32[]{:S(2)}) collective-permute-start(bf16[128,256]{1,0:T(8,128)(2,1)S(1)} %slice.50), channel_id=1, source_target_pairs={{0,20},{1,21},{2,22},{3,23},{4,16},{5,17},{6,18},{7,19},{8,28},{9,... | collective-permute-start | bytes 196616 | tf_op jit(solution)/shard_map/ppermute | solution.py:599
  7.5 2.3 %collective-permute-start.4 = (bf16[128,256]{1,0:T(8,128)(2,1)S(1)}, bf16[128,256]{1,0:T(8,128)(2,1)S(1)}, u32[]{:S(2)}, u32[]{:S(2)}) collective-permute-start(bf16[128,256]{1,0:T(8,128)(2,1)S(1)} %slice.51), channel_id=1, source_target_pairs={{0,28},{1,29},{2,30},{3,31},{4,24},{5,25},{6,26},{7,27},{8,20},{9,... | collective-permute-start | bytes 196616 | tf_op jit(solution)/shard_map/ppermute | solution.py:599
  9.8 1.9 %collective-permute-done.5 = bf16[2,64,512]{2,1,0:T(8,128)(2,1)S(1)} collective-permute-done((bf16[2,64,512]{2,1,0:T(8,128)(2,1)S(1)}, bf16[2,64,512]{2,1,0:T(8,128)(2,1)S(1)}, u32[]{:S(2)}, u32[]{:S(2)}) %collective-permute-start.5) | collective-permute-done | bytes 131104 | tf_op jit(solution)/shard_map/ppermute | solution.py:599
  11.8 3.4 %collective-permute-start.6 = (bf16[2,64,512]{2,1,0:T(8,128)(2,1)S(1)}, bf16[2,64,512]{2,1,0:T(8,128)(2,1)S(1)}, u32[]{:S(2)}, u32[]{:S(2)}) collective-permute-start(bf16[2,64,512]{2,1,0:T(8,128)(2,1)S(1)} %pad_maximum_fusion.6), channel_id=1, source_target_pairs={{0,2},{1,3},{2,0},{3,1},{4,6},{5,7},{6,4},{7,5},{8,10},{9,11},{10,... | collective-permute-start | bytes 393224 | tf_op jit(solution)/shard_map/ppermute | solution.py:599
  15.2 1.6 %collective-permute-start.7 = (bf16[2,64,512]{2,1,0:T(8,128)(2,1)S(1)}, bf16[2,64,512]{2,1,0:T(8,128)(2,1)S(1)}, u32[]{:S(2)}, u32[]{:S(2)}) collective-permute-start(bf16[2,64,512]{2,1,0:T(8,128)(2,1)S(1)} %pad_maximum_fusion.7), channel_id=1, source_target_pairs={{0,1},{1,0},{2,3},{3,2},{4,5},{5,4},{6,7},{7,6},{8,9},{9,8},{10,11... | collective-permute-start | bytes 393224 | tf_op jit(solution)/shard_map/ppermute | solution.py:599
  17.4 1.3 %collective-permute-start.1 = (bf16[144,256]{1,0:T(8,128)(2,1)S(1)}, bf16[144,256]{1,0:T(8,128)(2,1)S(1)}, u32[]{:S(2)}, u32[]{:S(2)}) collective-permute-start(bf16[144,256]{1,0:T(8,128)(2,1)S(1)} %get-tuple-element.87), channel_id=1, source_target_pairs={{0,16},{8,24},{16,0},{24,8},{1,17},{9,25},{17,1},{25,9},{2,18},{10... | collective-permute-start | bytes 221192 | tf_op jit(solution)/shard_map/ppermute | solution.py:599
  18.7 3.2 %collective-permute-done.1.refs_2_ = bf16[144,256]{1,0:T(8,128)(2,1)S(1)} collective-permute-done((bf16[144,256]{1,0:T(8,128)(2,1)S(1)}, bf16[144,256]{1,0:T(8,128)(2,1)S(1)}, u32[]{:S(2)}, u32[]{:S(2)}) %collective-permute-start.1) | collective-permute-done | bytes 73760 | tf_op jit(solution)/shard_map/ppermute | solution.py:599
  21.9 1.3 %collective-permute-done.2.refs_3_ = bf16[144,256]{1,0:T(8,128)(2,1)S(1)} collective-permute-done((bf16[144,256]{1,0:T(8,128)(2,1)S(1)}, bf16[144,256]{1,0:T(8,128)(2,1)S(1)}, u32[]{:S(2)}, u32[]{:S(2)}) %collective-permute-start.2) | collective-permute-done | bytes 73760 | tf_op jit(solution)/shard_map/ppermute | solution.py:599
  23.9 1.4 %collective-permute-start.10 = (bf16[2,2,64,256]{3,2,1,0:T(8,128)(2,1)S(1)}, bf16[2,2,64,256]{3,2,1,0:T(8,128)(2,1)S(1)}, u32[]{:S(2)}, u32[]{:S(2)}) collective-permute-start(bf16[2,2,64,256]{3,2,1,0:T(8,128)(2,1)S(1)} %get-tuple-element.86.refs_0_.refs_2_), channel_id=1, source_target_pairs={{0,2},{1,3},{2,0},{3,1},{4,6},{5,7},{6,4},{7,5},{8,10},{9,11},{10,... | collective-permute-start | bytes 393224 | tf_op jit(solution)/shard_map/ppermute | solution.py:599
  26.7 1.5 %collective-permute-start.8 = (bf16[4,64,512]{2,1,0:T(8,128)(2,1)S(1)}, bf16[4,64,512]{2,1,0:T(8,128)(2,1)S(1)}, u32[]{:S(2)}, u32[]{:S(2)}) collective-permute-start(bf16[4,64,512]{2,1,0:T(8,128)(2,1)S(1)} %pad_maximum_fusion.1), channel_id=1, source_target_pairs={{0,1},{1,0},{2,3},{3,2},{4,5},{5,4},{6,7},{7,6},{8,9},{9,8},{10,11... | collective-permute-start | bytes 786440 | tf_op jit(solution)/shard_map/ppermute | solution.py:599
  28.3 2.1 %collective-permute-done.10.refs_1_.refs_3_ = bf16[2,2,64,256]{3,2,1,0:T(8,128)(2,1)S(1)} collective-permute-done((bf16[2,2,64,256]{3,2,1,0:T(8,128)(2,1)S(1)}, bf16[2,2,64,256]{3,2,1,0:T(8,128)(2,1)S(1)}, u32[]{:S(2)}, u32[]{:S(2)}) %collective-permute-start.10) | collective-permute-done | bytes 131104 | tf_op jit(solution)/shard_map/ppermute | solution.py:599
  30.3 1.2 %collective-permute-done.11.refs_3_.refs_5_ = bf16[2,2,64,256]{3,2,1,0:T(8,128)(2,1)S(1)} collective-permute-done((bf16[2,2,64,256]{3,2,1,0:T(8,128)(2,1)S(1)}, bf16[2,2,64,256]{3,2,1,0:T(8,128)(2,1)S(1)}, u32[]{:S(2)}, u32[]{:S(2)}) %collective-permute-start.11) | collective-permute-done | bytes 131104 | tf_op jit(solution)/shard_map/ppermute | solution.py:599
  31.6 1.0 %collective-permute-start.14 = (bf16[8,64,256]{2,1,0:T(8,128)(2,1)S(1)}, bf16[8,64,256]{2,1,0:T(8,128)(2,1)S(1)}, u32[]{:S(2)}, u32[]{:S(2)}) collective-permute-start(bf16[8,64,256]{2,1,0:T(8,128)(2,1)S(1)} %join_pieces.2), channel_id=1, source_target_pairs={{0,16},{8,24},{16,0},{24,8},{1,17},{9,25},{17,1},{25,9},{2,18},{10... | collective-permute-start | bytes 786440 | tf_op jit(solution)/shard_map/ppermute | solution.py:599
  33.5 2.5 %collective-permute-done.9.rest_7_ = bf16[4,64,512]{2,1,0:T(8,128)(2,1)S(1)} collective-permute-done((bf16[4,64,512]{2,1,0:T(8,128)(2,1)S(1)}, bf16[4,64,512]{2,1,0:T(8,128)(2,1)S(1)}, u32[]{:S(2)}, u32[]{:S(2)}) %collective-permute-start.9) | collective-permute-done | bytes 262176 | tf_op jit(solution)/shard_map/ppermute | solution.py:599
  36.0 1.2 %collective-permute-done.8.rest_3_ = bf16[4,64,512]{2,1,0:T(8,128)(2,1)S(1)} collective-permute-done((bf16[4,64,512]{2,1,0:T(8,128)(2,1)S(1)}, bf16[4,64,512]{2,1,0:T(8,128)(2,1)S(1)}, u32[]{:S(2)}, u32[]{:S(2)}) %collective-permute-start.8) | collective-permute-done | bytes 262176 | tf_op jit(solution)/shard_map/ppermute | solution.py:599
  38.0 2.7 %collective-permute-done.13.refs_7_ = bf16[4,2,64,256]{3,2,1,0:T(8,128)(2,1)S(1)} collective-permute-done((bf16[4,2,64,256]{3,2,1,0:T(8,128)(2,1)S(1)}, bf16[4,2,64,256]{3,2,1,0:T(8,128)(2,1)S(1)}, u32[]{:S(2)}, u32[]{:S(2)}) %collective-permute-start.13) | collective-permute-done | bytes 262176 | tf_op jit(solution)/shard_map/ppermute | solution.py:599
  40.8 0.8 %collective-permute-done.12.refs_6_ = bf16[4,2,64,256]{3,2,1,0:T(8,128)(2,1)S(1)} collective-permute-done((bf16[4,2,64,256]{3,2,1,0:T(8,128)(2,1)S(1)}, bf16[4,2,64,256]{3,2,1,0:T(8,128)(2,1)S(1)}, u32[]{:S(2)}, u32[]{:S(2)}) %collective-permute-start.12) | collective-permute-done | bytes 262176 | tf_op jit(solution)/shard_map/ppermute | solution.py:599
  42.4 1.5 %collective-permute-start.17 = (bf16[9,64,256]{2,1,0:T(8,128)(2,1)S(1)}, bf16[9,64,256]{2,1,0:T(8,128)(2,1)S(1)}, u32[]{:S(2)}, u32[]{:S(2)}) collective-permute-start(bf16[9,64,256]{2,1,0:T(8,128)(2,1)S(1)} %get-tuple-element.74), channel_id=1, source_target_pairs={{0,16},{8,24},{16,0},{24,8},{1,17},{9,25},{17,1},{25,9},{2,18},{10... | collective-permute-start | bytes 884744 | tf_op jit(solution)/shard_map/ppermute | solution.py:599
  43.9 4.6 %depth_step.2 = (bf16[2,512,512]{2,1,0:T(8,128)(2,1)S(1)}, bf16[2,64,512]{2,1,0:T(8,128)(2,1)S(1)}) custom-call(bf16[2,512,512]{2,1,0:T(8,128)(2,1)S(1)} %get-tuple-element.68.w_ref, f32[6,8,128]{2,1,0:T(8,128)S(1)} %get-tuple-element.67.refs_ref, bf16[7,256,256]{2,1,0:T(8,128)(2,1)S(1)} %copy-done.2, bf16[16,64,256]{2,1,0:T(8,128)(2,1)S(1)} %get-tuple-element.69.rest_0_, ...), custom_call_target="tpu_custom_call" | custom-call | flops 4294967296 | bytes 16777216 | tf_op jit(solution)/shard_map/depth_step/pallas_call | solution.py:499
  48.5 4.8 %depth_step.3 = (bf16[2,512,512]{2,1,0:T(8,128)(2,1)S(1)}, bf16[2,64,512]{2,1,0:T(8,128)(2,1)S(1)}) custom-call(bf16[2,512,512]{2,1,0:T(8,128)(2,1)S(1)} %get-tuple-element.70.w_ref, f32[6,8,128]{2,1,0:T(8,128)S(1)} %get-tuple-element.67.refs_ref, bf16[7,256,256]{2,1,0:T(8,128)(2,1)S(1)} %copy-done.2, bf16[16,64,256]{2,1,0:T(8,128)(2,1)S(1)} %get-tuple-element.71.rest_0_, ...), custom_call_target="tpu_custom_call" | custom-call | flops 4294967296 | bytes 16777216 | tf_op jit(solution)/shard_map/depth_step/pallas_call | solution.py:499
  54.0 1.3 %collective-permute-start.21 = (bf16[2,64,512]{2,1,0:T(8,128)(2,1)S(1)}, bf16[2,64,512]{2,1,0:T(8,128)(2,1)S(1)}, u32[]{:S(2)}, u32[]{:S(2)}) collective-permute-start(bf16[2,64,512]{2,1,0:T(8,128)(2,1)S(1)} %get-tuple-element.84), channel_id=1, source_target_pairs={{0,16},{8,24},{16,0},{24,8},{1,17},{9,25},{17,1},{25,9},{2,18},{10... | collective-permute-start | bytes 393224 | tf_op jit(solution)/shard_map/ppermute | solution.py:599
  55.5 4.8 %end_step.1 = (bf16[2,64,512]{2,1,0:T(8,128)(2,1)S(1)}, bf16[2,64,512]{2,1,0:T(8,128)(2,1)S(1)}) custom-call(bf16[2,512,512]{2,1,0:T(8,128)(2,1)S(1)} %get-tuple-element.73.w_ref, f32[6,8,128]{2,1,0:T(8,128)S(1)} %get-tuple-element.67.refs_ref, bf16[7,256,256]{2,1,0:T(8,128)(2,1)S(1)} %copy-done.2, bf16[8,64,256]{2,1,0:T(8,128)(2,1)S(1)} %collective-permute-done.14.rest_0_, ...), custom_call_target="tpu_custom_call" | custom-call | flops 4294967296 | bytes 16777216 | tf_op jit(solution)/shard_map/end_step/pallas_call | solution.py:499
  (61 shorter events, 9.1 us)
Async XLA Ops:
  1.0 10.7 %collective-permute-start.5 = (bf16[2,64,512]{2,1,0:T(8,128)(2,1)S(1)}, bf16[2,64,512]{2,1,0:T(8,128)(2,1)S(1)}, u32[]{:S(2)}, u32[]{:S(2)}) collective-permute-start(bf16[2,64,512]{2,1,0:T(8,128)(2,1)S(1)} %bitcast.36), channel_id=1, source_target_pairs={{0,4},{1,5},{2,6},{3,7},{4,0},{5,1},{6,2},{7,3},{8,12},{9,13},{10,... | collective-permute-start | bytes 393224 | tf_op jit(solution)/shard_map/ppermute | solution.py:599
  6.1 17.1 %collective-permute-start = (bf16[2,144,256]{2,1,0:T(8,128)(2,1)S(1)}, bf16[2,144,256]{2,1,0:T(8,128)(2,1)S(1)}, u32[]{:S(2)}, u32[]{:S(2)}) collective-permute-start(bf16[2,144,256]{2,1,0:T(8,128)(2,1)S(1)} %pad_maximum_fusion.5.refs_0_), channel_id=1, source_target_pairs={{0,8},{8,0},{16,24},{24,16},{1,9},{9,1},{17,25},{25,17},{2,10},{10... | collective-permute-start | bytes 442376 | tf_op jit(solution)/shard_map/ppermute | solution.py:599
  6.2 11.2 %collective-permute-start.3 = (bf16[128,256]{1,0:T(8,128)(2,1)S(1)}, bf16[128,256]{1,0:T(8,128)(2,1)S(1)}, u32[]{:S(2)}, u32[]{:S(2)}) collective-permute-start(bf16[128,256]{1,0:T(8,128)(2,1)S(1)} %slice.50), channel_id=1, source_target_pairs={{0,20},{1,21},{2,22},{3,23},{4,16},{5,17},{6,18},{7,19},{8,28},{9,... | collective-permute-start | bytes 196616 | tf_op jit(solution)/shard_map/ppermute | solution.py:599
  7.5 11.2 %collective-permute-start.4 = (bf16[128,256]{1,0:T(8,128)(2,1)S(1)}, bf16[128,256]{1,0:T(8,128)(2,1)S(1)}, u32[]{:S(2)}, u32[]{:S(2)}) collective-permute-start(bf16[128,256]{1,0:T(8,128)(2,1)S(1)} %slice.51), channel_id=1, source_target_pairs={{0,28},{1,29},{2,30},{3,31},{4,24},{5,25},{6,26},{7,27},{8,20},{9,... | collective-permute-start | bytes 196616 | tf_op jit(solution)/shard_map/ppermute | solution.py:599
  11.8 11.4 %collective-permute-start.6 = (bf16[2,64,512]{2,1,0:T(8,128)(2,1)S(1)}, bf16[2,64,512]{2,1,0:T(8,128)(2,1)S(1)}, u32[]{:S(2)}, u32[]{:S(2)}) collective-permute-start(bf16[2,64,512]{2,1,0:T(8,128)(2,1)S(1)} %pad_maximum_fusion.6), channel_id=1, source_target_pairs={{0,2},{1,3},{2,0},{3,1},{4,6},{5,7},{6,4},{7,5},{8,10},{9,11},{10,... | collective-permute-start | bytes 393224 | tf_op jit(solution)/shard_map/ppermute | solution.py:599
  15.2 8.0 %collective-permute-start.7 = (bf16[2,64,512]{2,1,0:T(8,128)(2,1)S(1)}, bf16[2,64,512]{2,1,0:T(8,128)(2,1)S(1)}, u32[]{:S(2)}, u32[]{:S(2)}) collective-permute-start(bf16[2,64,512]{2,1,0:T(8,128)(2,1)S(1)} %pad_maximum_fusion.7), channel_id=1, source_target_pairs={{0,1},{1,0},{2,3},{3,2},{4,5},{5,4},{6,7},{7,6},{8,9},{9,8},{10,11... | collective-permute-start | bytes 393224 | tf_op jit(solution)/shard_map/ppermute | solution.py:599
  17.4 4.5 %collective-permute-start.1 = (bf16[144,256]{1,0:T(8,128)(2,1)S(1)}, bf16[144,256]{1,0:T(8,128)(2,1)S(1)}, u32[]{:S(2)}, u32[]{:S(2)}) collective-permute-start(bf16[144,256]{1,0:T(8,128)(2,1)S(1)} %get-tuple-element.87), channel_id=1, source_target_pairs={{0,16},{8,24},{16,0},{24,8},{1,17},{9,25},{17,1},{25,9},{2,18},{10... | collective-permute-start | bytes 221192 | tf_op jit(solution)/shard_map/ppermute | solution.py:599
  18.7 4.5 %collective-permute-start.2 = (bf16[144,256]{1,0:T(8,128)(2,1)S(1)}, bf16[144,256]{1,0:T(8,128)(2,1)S(1)}, u32[]{:S(2)}, u32[]{:S(2)}) collective-permute-start(bf16[144,256]{1,0:T(8,128)(2,1)S(1)} %get-tuple-element.88), channel_id=1, source_target_pairs={{0,24},{8,16},{16,8},{24,0},{1,25},{9,17},{17,9},{25,1},{2,26},{10... | collective-permute-start | bytes 221192 | tf_op jit(solution)/shard_map/ppermute | solution.py:599
  23.9 6.4 %collective-permute-start.10 = (bf16[2,2,64,256]{3,2,1,0:T(8,128)(2,1)S(1)}, bf16[2,2,64,256]{3,2,1,0:T(8,128)(2,1)S(1)}, u32[]{:S(2)}, u32[]{:S(2)}) collective-permute-start(bf16[2,2,64,256]{3,2,1,0:T(8,128)(2,1)S(1)} %get-tuple-element.86.refs_0_.refs_2_), channel_id=1, source_target_pairs={{0,2},{1,3},{2,0},{3,1},{4,6},{5,7},{6,4},{7,5},{8,10},{9,11},{10,... | collective-permute-start | bytes 393224 | tf_op jit(solution)/shard_map/ppermute | solution.py:599
  25.4 6.2 %collective-permute-start.11 = (bf16[2,2,64,256]{3,2,1,0:T(8,128)(2,1)S(1)}, bf16[2,2,64,256]{3,2,1,0:T(8,128)(2,1)S(1)}, u32[]{:S(2)}, u32[]{:S(2)}) collective-permute-start(bf16[2,2,64,256]{3,2,1,0:T(8,128)(2,1)S(1)} %get-tuple-element.85.refs_2_.refs_4_), channel_id=1, source_target_pairs={{0,1},{1,0},{2,3},{3,2},{4,5},{5,4},{6,7},{7,6},{8,9},{9,8},{10,11... | collective-permute-start | bytes 393224 | tf_op jit(solution)/shard_map/ppermute | solution.py:599
  25.9 10.0 %collective-permute-start.9 = (bf16[4,64,512]{2,1,0:T(8,128)(2,1)S(1)}, bf16[4,64,512]{2,1,0:T(8,128)(2,1)S(1)}, u32[]{:S(2)}, u32[]{:S(2)}) collective-permute-start(bf16[4,64,512]{2,1,0:T(8,128)(2,1)S(1)} %pad_maximum_fusion.2), channel_id=1, source_target_pairs={{0,2},{1,3},{2,0},{3,1},{4,6},{5,7},{6,4},{7,5},{8,10},{9,11},{10,... | collective-permute-start | bytes 786440 | tf_op jit(solution)/shard_map/ppermute | solution.py:599
  26.7 10.4 %copy-start.2 = (bf16[7,256,256]{2,1,0:T(8,128)(2,1)S(1)}, bf16[7,256,256]{2,1,0:T(8,128)(2,1)}, u32[]{:S(2)}) copy-start(bf16[7,256,256]{2,1,0:T(8,128)(2,1)} %constant.46.clone.tables) | copy-start | bytes 2752516
  26.7 10.4 %collective-permute-start.8 = (bf16[4,64,512]{2,1,0:T(8,128)(2,1)S(1)}, bf16[4,64,512]{2,1,0:T(8,128)(2,1)S(1)}, u32[]{:S(2)}, u32[]{:S(2)}) collective-permute-start(bf16[4,64,512]{2,1,0:T(8,128)(2,1)S(1)} %pad_maximum_fusion.1), channel_id=1, source_target_pairs={{0,1},{1,0},{2,3},{3,2},{4,5},{5,4},{6,7},{7,6},{8,9},{9,8},{10,11... | collective-permute-start | bytes 786440 | tf_op jit(solution)/shard_map/ppermute | solution.py:599
  31.6 6.4 %collective-permute-start.14 = (bf16[8,64,256]{2,1,0:T(8,128)(2,1)S(1)}, bf16[8,64,256]{2,1,0:T(8,128)(2,1)S(1)}, u32[]{:S(2)}, u32[]{:S(2)}) collective-permute-start(bf16[8,64,256]{2,1,0:T(8,128)(2,1)S(1)} %join_pieces.2), channel_id=1, source_target_pairs={{0,16},{8,24},{16,0},{24,8},{1,17},{9,25},{17,1},{25,9},{2,18},{10... | collective-permute-start | bytes 786440 | tf_op jit(solution)/shard_map/ppermute | solution.py:599
  32.6 8.2 %collective-permute-start.13 = (bf16[4,2,64,256]{3,2,1,0:T(8,128)(2,1)S(1)}, bf16[4,2,64,256]{3,2,1,0:T(8,128)(2,1)S(1)}, u32[]{:S(2)}, u32[]{:S(2)}) collective-permute-start(bf16[4,2,64,256]{3,2,1,0:T(8,128)(2,1)S(1)} %pad_maximum_fusion.4), channel_id=1, source_target_pairs={{0,2},{1,3},{2,0},{3,1},{4,6},{5,7},{6,4},{7,5},{8,10},{9,11},{10,... | collective-permute-start | bytes 786440 | tf_op jit(solution)/shard_map/ppermute | solution.py:599
  33.4 8.2 %collective-permute-start.12 = (bf16[4,2,64,256]{3,2,1,0:T(8,128)(2,1)S(1)}, bf16[4,2,64,256]{3,2,1,0:T(8,128)(2,1)S(1)}, u32[]{:S(2)}, u32[]{:S(2)}) collective-permute-start(bf16[4,2,64,256]{3,2,1,0:T(8,128)(2,1)S(1)} %pad_maximum_fusion.3), channel_id=1, source_target_pairs={{0,1},{1,0},{2,3},{3,2},{4,5},{5,4},{6,7},{7,6},{8,9},{9,8},{10,11... | collective-permute-start | bytes 786440 | tf_op jit(solution)/shard_map/ppermute | solution.py:599
  41.8 2.1 %collective-permute-start.15 = (bf16[16,64,256]{2,1,0:T(8,128)(2,1)S(1)}, bf16[16,64,256]{2,1,0:T(8,128)(2,1)S(1)}, u32[]{:S(2)}, u32[]{:S(2)}) collective-permute-start(bf16[16,64,256]{2,1,0:T(8,128)(2,1)S(1)} %get-tuple-element.69.rest_0_), channel_id=1, source_target_pairs={{0,8},{8,0},{16,24},{24,16},{1,9},{9,1},{17,25},{25,17},{2,10},{10... | collective-permute-start | bytes 1572872 | tf_op jit(solution)/shard_map/ppermute | solution.py:599
  41.9 6.6 %collective-permute-start.16 = (bf16[16,64,256]{2,1,0:T(8,128)(2,1)S(1)}, bf16[16,64,256]{2,1,0:T(8,128)(2,1)S(1)}, u32[]{:S(2)}, u32[]{:S(2)}) collective-permute-start(bf16[16,64,256]{2,1,0:T(8,128)(2,1)S(1)} %get-tuple-element.71.rest_0_), channel_id=1, source_target_pairs={{0,8},{8,0},{16,24},{24,16},{1,9},{9,1},{17,25},{25,17},{2,10},{10... | collective-permute-start | bytes 1572872 | tf_op jit(solution)/shard_map/ppermute | solution.py:599
  42.4 10.9 %collective-permute-start.17 = (bf16[9,64,256]{2,1,0:T(8,128)(2,1)S(1)}, bf16[9,64,256]{2,1,0:T(8,128)(2,1)S(1)}, u32[]{:S(2)}, u32[]{:S(2)}) collective-permute-start(bf16[9,64,256]{2,1,0:T(8,128)(2,1)S(1)} %get-tuple-element.74), channel_id=1, source_target_pairs={{0,16},{8,24},{16,0},{24,8},{1,17},{9,25},{17,1},{25,9},{2,18},{10... | collective-permute-start | bytes 884744 | tf_op jit(solution)/shard_map/ppermute | solution.py:599
  53.3 2.2 %collective-permute-start.19 = (bf16[9,64,256]{2,1,0:T(8,128)(2,1)S(1)}, bf16[9,64,256]{2,1,0:T(8,128)(2,1)S(1)}, u32[]{:S(2)}, u32[]{:S(2)}) collective-permute-start(bf16[9,64,256]{2,1,0:T(8,128)(2,1)S(1)} %collective-permute-done.17.rest_1_), channel_id=1, source_target_pairs={{0,8},{8,0},{16,24},{24,16},{1,9},{9,1},{17,25},{25,17},{2,10},{10... | collective-permute-start | bytes 884744 | tf_op jit(solution)/shard_map/ppermute | solution.py:599
  53.4 2.1 %collective-permute-start.18 = (bf16[8,64,256]{2,1,0:T(8,128)(2,1)S(1)}, bf16[8,64,256]{2,1,0:T(8,128)(2,1)S(1)}, u32[]{:S(2)}, u32[]{:S(2)}) collective-permute-start(bf16[8,64,256]{2,1,0:T(8,128)(2,1)S(1)} %collective-permute-done.14.rest_0_), channel_id=1, source_target_pairs={{0,8},{8,0},{16,24},{24,16},{1,9},{9,1},{17,25},{25,17},{2,10},{10... | collective-permute-start | bytes 786440 | tf_op jit(solution)/shard_map/ppermute | solution.py:599
  54.0 7.2 %collective-permute-start.21 = (bf16[2,64,512]{2,1,0:T(8,128)(2,1)S(1)}, bf16[2,64,512]{2,1,0:T(8,128)(2,1)S(1)}, u32[]{:S(2)}, u32[]{:S(2)}) collective-permute-start(bf16[2,64,512]{2,1,0:T(8,128)(2,1)S(1)} %get-tuple-element.84), channel_id=1, source_target_pairs={{0,16},{8,24},{16,0},{24,8},{1,17},{9,25},{17,1},{25,9},{2,18},{10... | collective-permute-start | bytes 393224 | tf_op jit(solution)/shard_map/ppermute | solution.py:599
  55.2 6.2 %collective-permute-start.22 = (bf16[2,64,512]{2,1,0:T(8,128)(2,1)S(1)}, bf16[2,64,512]{2,1,0:T(8,128)(2,1)S(1)}, u32[]{:S(2)}, u32[]{:S(2)}) collective-permute-start(bf16[2,64,512]{2,1,0:T(8,128)(2,1)S(1)} %get-tuple-element.83), channel_id=1, source_target_pairs={{0,24},{8,16},{16,8},{24,0},{1,25},{9,17},{17,9},{25,1},{2,26},{10... | collective-permute-start | bytes 393224 | tf_op jit(solution)/shard_map/ppermute | solution.py:599
  60.4 1.8 %collective-permute-start.20 = (bf16[2,64,512]{2,1,0:T(8,128)(2,1)S(1)}, bf16[2,64,512]{2,1,0:T(8,128)(2,1)S(1)}, u32[]{:S(2)}, u32[]{:S(2)}) collective-permute-start(bf16[2,64,512]{2,1,0:T(8,128)(2,1)S(1)} %get-tuple-element.81), channel_id=1, source_target_pairs={{0,8},{8,0},{16,24},{24,16},{1,9},{9,1},{17,25},{25,17},{2,10},{10... | collective-permute-start | bytes 393224 | tf_op jit(solution)/shard_map/ppermute | solution.py:599
  (4 other events, 21.7 us)
